TPU v7x, 512 devices: a whole 4x8x8 slice. The times are simulated.
512 devices in a mesh: wide: 64 (over z_hi, y, core), narrow: 8 (over x, z_lo).
Axes of the slice: x: 4, y: 8, z: 8 (z_hi: 4, z_lo: 2; z = z_hi * 2 + z_lo), core: 2. Of those that a mesh axis runs over, the one named last changes fastest.
Arguments:
- teacher_in: bfloat16 [512, 6144], P('wide', 'narrow')
- teacher_gain: bfloat16 [6144], P('narrow'), may hold values from 0.5 to 1.5
- mlp_in: bfloat16 [6144, 24576], P('narrow', 'wide'), may hold values from -0.078125 to 0.078125
- mlp_out: bfloat16 [24576, 6144], P('wide', 'narrow'), may hold values from -0.0390625 to 0.0390625
- projector: bfloat16 [6144, 1024], P('narrow', 'wide'), may hold values from -0.078125 to 0.078125
- student_in: bfloat16 [256, 256, 1024], P('wide')
- sample_pos: int32 [256, 2], P('wide'), may hold values from 0 to 255, as said below
- w_qkv: bfloat16 [3, 1024, 1024], P(None, None, 'narrow')
- w_attn_out: bfloat16 [1024, 1024], P('narrow'), may hold values from -0.1875 to 0.1875
Outputs:
- grad_qkv: float32 [3, 1024, 1024], P(None, 'wide', 'narrow')
- grad_attn_out: float32 [1024, 1024], P('narrow', 'wide')
- grad_projector: float32 [6144, 1024], P('narrow', 'wide')
Inputs may be any that keep to these rules, and one draw needn't show every extreme that they name: `sample_pos`: position j of an image lies in [j * 128, (j + 1) * 128).
All inputs are finite; a program needn't handle non-finite values.
Results may differ from a plain program's by a relative error of at most 0.012.
Values may be sent and summed in bfloat16 or wider, within the bound.
No kernel may reach another device: no remote copies, remote signals or barrier semaphores. Data moves between devices by JAX's collectives and lax.ppermute only.
A program may use at most 64 MiB of HBM per device.

v0:
```python
import jax
import jax.numpy as jnp
from jax import lax
from jax.sharding import PartitionSpec as P

D_T = 6144
HEAD_DIM = 64


EPSILON = 1e-06


def contract_rows(left, right):
    return lax.dot_general(
        left, right, (((0,), (0,)), ((), ())), preferred_element_type=jnp.float32
    )


def local(
    teacher_in, teacher_gain, mlp_in, mlp_out, projector, student_in, sample_pos, w_qkv, w_attn_out
):
    f32 = jnp.float32
    bf16 = jnp.bfloat16
    gathered = lax.all_gather(teacher_in, "wide", axis=0, tiled=True)
    wide_in = gathered.astype(f32)
    row_total, row_square = lax.psum(
        (jnp.sum(wide_in, axis=1), jnp.sum(wide_in * wide_in, axis=1)), "narrow"
    )
    center = (row_total / D_T)[:, None]
    spread = (row_square / D_T)[:, None] - center * center
    normed = ((wide_in - center) * lax.rsqrt(spread + EPSILON) * teacher_gain.astype(f32)).astype(
        bf16
    )
    pre_part = jnp.dot(normed, mlp_in, preferred_element_type=f32)
    pre_full = lax.psum(pre_part, "narrow")
    hidden = jax.nn.gelu(pre_full, approximate=False).astype(bf16)
    branch = lax.psum_scatter(
        jnp.dot(hidden, mlp_out, preferred_element_type=f32),
        "wide",
        scatter_dimension=0,
        tiled=True,
    )
    teacher_local = (teacher_in.astype(f32) + branch).astype(bf16)
    teacher_out = lax.all_gather(teacher_local, "wide", axis=0, tiled=True)
    target_part = jnp.dot(teacher_out, projector, preferred_element_type=f32)
    target_cols = lax.psum(target_part, "narrow")
    target = lax.all_to_all(target_cols, "wide", split_axis=0, concat_axis=1, tiled=True)
    images, patches, width = student_in.shape
    select = sample_pos.shape[1]
    local_width = w_qkv.shape[2]
    heads_here = local_width // HEAD_DIM
    scale = HEAD_DIM ** (-0.5)
    source = student_in.astype(f32)
    center_s = jnp.mean(source, axis=-1, keepdims=True)
    spread_s = jnp.mean(source * source, axis=-1, keepdims=True) - center_s * center_s
    student_norm = ((source - center_s) * lax.rsqrt(spread_s + EPSILON)).astype(bf16)
    flat_norm = student_norm.reshape(images * patches, width)
    keys = (
        jnp.dot(flat_norm, w_qkv[1], preferred_element_type=f32)
        .astype(bf16)
        .reshape(images, patches, heads_here, HEAD_DIM)
    )
    values = (
        jnp.dot(flat_norm, w_qkv[2], preferred_element_type=f32)
        .astype(bf16)
        .reshape(images, patches, heads_here, HEAD_DIM)
    )
    index = sample_pos[:, :, None]
    picked_norm = jnp.take_along_axis(student_norm, index, axis=1).reshape(images * select, width)
    picked_in = (
        jnp.take_along_axis(student_in, index, axis=1).reshape(images * select, width).astype(f32)
    )
    queries = (
        jnp.dot(picked_norm, w_qkv[0], preferred_element_type=f32)
        .astype(bf16)
        .reshape(images, select, heads_here, HEAD_DIM)
    )
    scores = jnp.einsum("ishd,iphd->ihsp", queries, keys, preferred_element_type=f32) * scale
    probs = jax.nn.softmax(scores, axis=-1)
    probs_low = probs.astype(bf16)
    context = (
        jnp.einsum("ihsp,iphd->ishd", probs_low, values, preferred_element_type=f32)
        .astype(bf16)
        .reshape(images * select, local_width)
    )
    mixed = lax.psum(jnp.dot(context, w_attn_out, preferred_element_type=f32), "narrow")
    student_out = picked_in + mixed
    delta = ((student_out - target) / (select * images)).astype(bf16)
    delta_cols = lax.all_to_all(delta, "wide", split_axis=1, concat_axis=0, tiled=True)
    grad_projector = -contract_rows(teacher_out, delta_cols)
    grad_attn = contract_rows(context, delta)
    d_context = lax.dot_general(
        delta, w_attn_out, (((1,), (1,)), ((), ())), preferred_element_type=f32
    )
    d_context = d_context.astype(bf16).reshape(images, select, heads_here, HEAD_DIM)
    d_probs = jnp.einsum("ishd,iphd->ihsp", d_context, values, preferred_element_type=f32)
    d_scores = (
        probs * (d_probs - jnp.sum(probs * d_probs, axis=-1, keepdims=True)) * scale
    ).astype(bf16)
    d_query = (
        jnp.einsum("ihsp,iphd->ishd", d_scores, keys, preferred_element_type=f32)
        .astype(bf16)
        .reshape(images * select, local_width)
    )
    d_key = (
        jnp.einsum("ihsp,ishd->iphd", d_scores, queries, preferred_element_type=f32)
        .astype(bf16)
        .reshape(images * patches, local_width)
    )
    d_value = (
        jnp.einsum("ihsp,ishd->iphd", probs_low, d_context, preferred_element_type=f32)
        .astype(bf16)
        .reshape(images * patches, local_width)
    )
    stacked = jnp.stack(
        [
            contract_rows(picked_norm, d_query),
            contract_rows(flat_norm, d_key),
            contract_rows(flat_norm, d_value),
        ]
    )
    grad_qkv, grad_attn_out = (
        lax.psum_scatter(stacked, "wide", scatter_dimension=1, tiled=True),
        lax.psum_scatter(grad_attn, "wide", scatter_dimension=1, tiled=True),
    )
    return (grad_qkv, grad_attn_out, grad_projector)


def solution(mesh):
    placed = (
        P("wide", "narrow"),
        P("narrow"),
        P("narrow", "wide"),
        P("wide", "narrow"),
        P("narrow", "wide"),
        P("wide", None, None),
        P("wide", None),
        P(None, None, "narrow"),
        P("narrow", None),
    )
    return jax.shard_map(
        local,
        mesh=mesh,
        in_specs=placed,
        out_specs=(P(None, "wide", "narrow"), P("narrow", "wide"), P("narrow", "wide")),
        check_vma=False,
    )
```

profile of v0, /device:TPU:1, one launch (start us, length us, event | category | flops | bytes accessed | tf_op | source)
XLA Modules:
  0.0 850.8 jit_solution(6942796167830973405)
XLA Ops:
  7.2 0.7 convert_element_type.87
  8.0 92.7 %all_gather.6 = bf16[512,768]{1,0:T(8,128)(2,1)S(1)} all-gather(bf16[8,768]{1,0:T(8,128)(2,1)} %param.11), channel_id=1, replica_groups=mesh['wide'=64,'narrow'=8] {'wide'}, dimensions={0}, use_global_device_ids=true | all-gather | bytes 798720 | tf_op jit(solution)/shard_map/all_gather | solution.py:24
  101.0 16.0 %all-reduce.1 = (f32[512]{0:T(512)S(1)}, f32[512]{0:T(512)S(1)}) all-reduce(f32[512]{0:T(512)S(1)} %get-tuple-element.7, f32[512]{0:T(512)S(1)} %get-tuple-element.6), channel_id=1, replica_groups=mesh['wide'=64,'narrow'=8] {'narrow'}, use_global_device_ids=true, to_apply=%region_8.10 | all-reduce | flops 1024 | bytes 8192 | tf_op jit(solution)/shard_map/psum | solution.py:26
  117.1 2.6 fusion.22
  119.8 0.7 convert_reduce_fusion
  120.5 74.6 %all-reduce.5.cloned.1.call-done = f32[512,384]{1,0:T(8,128)} async-done(((f32[512,384]{1,0:T(8,128)}), f32[512,384]{1,0:T(8,128)}) %all-reduce.5.cloned.1.call-update) | async-done | bytes 786448 | tf_op jit(solution)/shard_map/psum | solution.py:35
  195.0 4.4 fusion.34
  199.8 0.6 gather_fusion.1
  200.5 2.1 fusion.3
  202.6 0.6 gather_fusion
  203.4 1.1 convolution_convert_fusion.7
  204.5 1.7 convolution_convert_fusion.2
  206.8 2.5 convolution_convert_fusion.3
  209.3 1.2 reshape.105
  210.5 1.0 copy.60
  211.5 1.1 convolution_multiply_fusion
  212.6 0.7 fusion.121
  213.6 1.7 fusion.122
  215.3 134.2 %reduce-scatter.4.cloned.1.call-done = f32[8,768]{1,0:T(8,128)} async-done(((f32[512,768]{1,0:T(8,128)}), f32[8,768]{1,0:T(8,128)}) %reduce-scatter.4.cloned.1.call-update) | async-done | bytes 24592 | tf_op jit(solution)/shard_map/reduce_scatter | solution.py:37
  349.6 0.7 add_convert_fusion
  350.3 86.7 %all_gather.7 = bf16[512,768]{1,0:T(8,128)(2,1)S(1)} all-gather(bf16[8,768]{1,0:T(8,128)(2,1)S(1)} %add_convert_fusion), channel_id=1, replica_groups=mesh['wide'=64,'narrow'=8] {'wide'}, dimensions={0}, use_global_device_ids=true | all-gather | bytes 798720 | tf_op jit(solution)/shard_map/all_gather | solution.py:44
  437.0 1.8 convolution_bitcast_fusion.3
  438.8 73.4 %all-reduce.7.cloned.1.call-done = (f32[64,8,16]{2,1,0:T(8,128)}, f32[8,1024]{1,0:T(8,128)}) async-done(((f32[64,8,16]{2,1,0:T(8,128)}, f32[8,1024]{1,0:T(8,128)}), (f32[64,8,16]{2,1,0:T(8,128)}, f32[8,1024]{1,0:T(8,128)})) %all-reduce.7.cloned.1.call-update) | async-done | bytes 65552 | tf_op jit(solution)/shard_map/psum | solution.py:46
  512.2 1.7 reshape.107
  513.9 18.1 %all-to-all-start = ((f32[64,1,128]{2,1,0:T(1,128)}), f32[64,1,128]{2,1,0:T(1,128)}, u32[]{:S(2)}, u32[]{:S(2)}) async-start(f32[64,1,128]{2,1,0:T(1,128)} %reshape.107), calls=%async_computation.1 | async-start | bytes 65536 | tf_op jit(solution)/shard_map/all_to_all | solution.py:47
  532.0 0.6 reshape.84
  532.7 10.9 %all-to-all-done = f32[64,1,128]{2,1,0:T(1,128)} async-done(((f32[64,1,128]{2,1,0:T(1,128)}), f32[64,1,128]{2,1,0:T(1,128)}, u32[]{:S(2)}, u32[]{:S(2)}) %all-to-all-start) | async-done | bytes 32800 | tf_op jit(solution)/shard_map/all_to_all | solution.py:47
  543.5 0.5 broadcast.140
  544.0 1.5 reduce
  545.5 0.8 reshape.108
  546.3 1.7 copy.57
  548.0 1.1 all_to_all.31
  549.2 0.8 multiply_convert_fusion
  549.9 1.1 convolution_convert_fusion.6
  551.1 1.1 fusion.83
  552.2 1.3 fusion.18
  553.5 1.9 fusion.9
  555.5 1.1 fusion.123
  556.8 1.8 fusion.10
  558.7 1.2 copy.63
  559.9 1.2 copy.65
  561.4 0.7 convolution_bitcast_fusion
  562.2 0.7 convolution_bitcast_fusion.1
  562.9 1.3 pad_maximum_fusion
  564.5 16.6 %all_to_all.38 = bf16[8,64,16]{2,0,1:T(8,128)(2,1)S(1)} all-to-all(bf16[8,64,16]{2,0,1:T(8,128)(2,1)S(1)} %copy.66), channel_id=1, replica_groups=mesh['wide'=64,'narrow'=8] {'wide'}, dimensions={1} | all-to-all | bytes 32768 | tf_op jit(solution)/shard_map/all_to_all | solution.py:89
  581.1 0.9 convolution_negate_fusion
  581.9 109.2 %reduce-scatter.8.cloned.1.call-done = f32[128,16]{0,1:T(8,128)} async-done(((f32[128,1024]{0,1:T(8,128)}), f32[128,16]{0,1:T(8,128)}) %reduce-scatter.8.cloned.1.call-update) | async-done | bytes 8208 | tf_op jit(solution)/shard_map/reduce_scatter | solution.py:124
  691.1 153.1 %reduce-scatter.6.cloned.1.call-done = f32[3,16,128]{2,1,0:T(8,128)} async-done(((f32[3,1024,128]{2,1,0:T(8,128)}), f32[3,16,128]{2,1,0:T(8,128)}) %reduce-scatter.6.cloned.1.call-update) | async-done | bytes 24592 | tf_op jit(solution)/shard_map/reduce_scatter | solution.py:123
  (48 shorter events, 3.1 us)
Async XLA Ops:
  7.2 187.9 %copy-start = (bf16[384,768]{1,0:T(8,128)(2,1)S(1)}, bf16[384,768]{1,0:T(8,128)(2,1)}, u32[]{:S(2)}) copy-start(bf16[384,768]{1,0:T(8,128)(2,1)} %param.14) | copy-start | bytes 1769476
  7.2 187.8 %all-reduce.5.cloned.1.call-start = ((), (), s32[]{:S(2)}) async-start(), calls=%async_computation.5 | async-start | bytes 1572864 | tf_op jit(solution)/shard_map/psum | solution.py:35
  100.7 19.0 %copy-start.5 = (s32[4,2]{0,1:T(2,128)S(1)}, s32[4,2]{0,1:T(2,128)}, u32[]{:S(2)}) copy-start(s32[4,2]{0,1:T(2,128)} %param.17) | copy-start | bytes 100
  100.7 19.1 %copy-start.1 = (bf16[4,256,1024]{2,1,0:T(8,128)(2,1)S(1)}, bf16[4,256,1024]{2,1,0:T(8,128)(2,1)}, u32[]{:S(2)}) copy-start(bf16[4,256,1024]{2,1,0:T(8,128)(2,1)} %param.16) | copy-start | bytes 6291460
  119.7 229.9 %reduce-scatter.4.cloned.1.call-start = ((), (), s32[]{:S(2)}) async-start(), calls=%async_computation.6 | async-start | bytes 1597440 | tf_op jit(solution)/shard_map/reduce_scatter | solution.py:37
  199.5 312.7 %all-reduce.7.cloned.1.call-start = ((), (), s32[]{:S(2)}) async-start(), calls=%async_computation.9 | async-start | bytes 589824 | tf_op jit(solution)/shard_map/psum | solution.py:46
  206.8 6.5 copy-start.2
  206.8 142.8 %copy-start.3 = (bf16[8,768]{1,0:T(8,128)(2,1)S(1)}, bf16[8,768]{1,0:T(8,128)(2,1)}, u32[]{:S(2)}) copy-start(bf16[8,768]{1,0:T(8,128)(2,1)} %param.11) | copy-start | bytes 36868
  212.5 137.0 %copy-start.4 = (f32[4,2,2,256]{3,2,1,0:T(2,128)}, f32[4,2,2,256]{3,2,1,0:T(2,128)S(1)}, u32[]{:S(2)}) copy-start(f32[4,2,2,256]{3,2,1,0:T(2,128)S(1)} %convolution_multiply_fusion) | copy-start | bytes 49156
  513.9 29.6 %all-to-all-start = ((f32[64,1,128]{2,1,0:T(1,128)}), f32[64,1,128]{2,1,0:T(1,128)}, u32[]{:S(2)}, u32[]{:S(2)}) async-start(f32[64,1,128]{2,1,0:T(1,128)} %reshape.107), calls=%async_computation.1 | async-start | bytes 65536 | tf_op jit(solution)/shard_map/all_to_all | solution.py:47
  532.0 159.2 %reduce-scatter.8.cloned.1.call-start = ((), (), s32[]{:S(2)}) async-start(), calls=%async_computation.8 | async-start | bytes 532480 | tf_op jit(solution)/shard_map/reduce_scatter | solution.py:124
  556.6 287.7 %reduce-scatter.6.cloned.1.call-start = ((), (), s32[]{:S(2)}) async-start(), calls=%async_computation.7 | async-start | bytes 1597440 | tf_op jit(solution)/shard_map/reduce_scatter | solution.py:123
Sparse Core Ops, SparseCore 0:
  119.8 75.1 all-reduce.4
  200.3 149.1 reduce-scatter.3
  438.9 73.2 all-reduce.6
  556.7 134.4 reduce-scatter.7
  696.9 147.3 reduce-scatter.5
where the time goes:
time: 856 us; the launch traced here: 851 us
  waiting for transfers between devices  555 us (65%)
  blocking collectives  212 us (25%)
  matrix products  28.1 us (3%)
  starting transfers between devices  18.5 us (2%)
  between operations  14 us (2%)
  local copies, waits for them, and re-layouts  13.8 us (2%)
  other arithmetic  8.99 us (1%)
    reduce_scatter x1, waiting for transfers between devices, local(): lax.psum_scatter(stacked, 'wide', scatter_dimension=1, tiled=True)  153 us
    reduce_scatter x1, waiting for transfers between devices, local(): lax.psum_scatter(jnp.dot(hidden, mlp_out, preferred_element_type=f32), 'w...  134 us
    reduce_scatter x1, waiting for transfers between devices, local(): lax.psum_scatter(grad_attn, 'wide', scatter_dimension=1, tiled=True)  109 us
    all_gather x1, blocking collectives, local(): gathered = lax.all_gather(teacher_in, 'wide', axis=0, tiled=True)  92.7 us
    all_gather x1, blocking collectives, local(): teacher_out = lax.all_gather(teacher_local, 'wide', axis=0, tiled=True)  86.7 us
    psum x1, waiting for transfers between devices, local(): pre_full = lax.psum(pre_part, 'narrow')  74.6 us
    psum x1, waiting for transfers between devices, local(): target_cols = lax.psum(target_part, 'narrow')  73.4 us
    all_to_all x1, starting transfers between devices, local(): lax.all_to_all(target_cols, 'wide', split_axis=0, concat_axis=1, tiled=True)  18.1 us
  transfers between devices with their start and end apart: 6, of which 6 were waited for; matrix products, arithmetic and copies ran while one was open for 3% of the time, Pallas kernels for 0%

commit v1 on v0

v1 whole, which is shorter than its diff:
```python
import jax
import jax.numpy as jnp
from jax import lax
from jax.sharding import PartitionSpec as P

HEAD_DIM = 64
LANES = 128
EPSILON = 1e-06
Z_PARTS = 4
CORES = 2

f32 = jnp.float32
bf16 = jnp.bfloat16


def product(left, right, dims=((1,), (0,))):
    return lax.dot_general(left, right, (dims, ((), ())), preferred_element_type=f32)


def wide_groups(z_parts, y_parts, cores):
    def place(z, y, c):
        return (z * y_parts + y) * cores + c

    zs, ys, cs = range(z_parts), range(y_parts), range(cores)
    along_z = [[place(z, y, c) for z in zs] for y in ys for c in cs]
    along_y = [[place(z, y, c) for y in ys] for z in zs for c in cs]
    along_c = [[place(z, y, c) for c in cs] for z in zs for y in ys]
    return along_z, along_y, along_c


def exchange(block, axis, groups=None):
    return lax.all_to_all(block, axis, 0, 0, axis_index_groups=groups)


def spread(block, axis, count, groups=None):
    return exchange(jnp.broadcast_to(block[None], (count,) + block.shape), axis, groups)


def make_local(wide, narrow, z_parts, cores):
    y_parts = wide // (z_parts * cores)
    along_z, along_y, along_c = wide_groups(z_parts, y_parts, cores)

    def gather_rows(block):
        for groups in (along_z, along_y, along_c):
            block = lax.all_gather(block, "wide", axis_index_groups=groups, tiled=True)
        return block

    def spread_rows(block):
        width = block.shape[1]
        for groups in (along_z, along_y, along_c):
            block = spread(block, "wide", len(groups[0]), groups).reshape(-1, width)
        return block

    def sum_to_owners(partial):
        width = partial.shape[1]
        for groups, kind in ((along_c, bf16), (along_y, bf16), (along_z, f32)):
            count = len(groups[0])
            block = partial.astype(kind).reshape(count, -1, width)
            partial = jnp.sum(exchange(block, "wide", groups).astype(f32), axis=0)
        return partial

    def local(
        teacher_in,
        teacher_gain,
        mlp_in,
        mlp_out,
        projector,
        student_in,
        sample_pos,
        w_qkv,
        w_attn_out,
    ):
        rows, features = teacher_in.shape
        d_t = features * narrow
        images, patches, width = student_in.shape
        select = sample_pos.shape[1]
        local_width = w_qkv.shape[2]
        scale = HEAD_DIM ** (-0.5)
        total_rows = rows * wide

        own = teacher_in.astype(f32)
        sums = jnp.concatenate(
            [
                jnp.sum(own, axis=1, keepdims=True),
                jnp.sum(own * own, axis=1, keepdims=True),
            ],
            axis=1,
        )
        sums = jnp.sum(spread(sums, "narrow", narrow), axis=0)
        center = sums[:, 0:1] / d_t
        variance = sums[:, 1:2] / d_t - center * center
        normed = (
            (own - center) * lax.rsqrt(variance + EPSILON) * teacher_gain.astype(f32)
        ).astype(bf16)
        normed = gather_rows(normed)

        pre = product(normed, mlp_in).astype(bf16)
        pre = exchange(pre.reshape(narrow, total_rows // narrow, -1), "narrow")
        pre = jnp.sum(pre.astype(f32), axis=0)
        hidden = jax.nn.gelu(pre, approximate=False).astype(bf16)
        hidden = spread(hidden, "narrow", narrow).reshape(total_rows, -1)
        branch = sum_to_owners(product(hidden, mlp_out))
        teacher_local = (own + branch).astype(bf16)

        flat_in = student_in.reshape(images * patches, width)
        source = flat_in.astype(f32)
        center_s = jnp.mean(source, axis=-1, keepdims=True)
        spread_s = jnp.mean(source * source, axis=-1, keepdims=True) - center_s * center_s
        flat_norm = ((source - center_s) * lax.rsqrt(spread_s + EPSILON)).astype(bf16)
        keys = product(flat_norm, w_qkv[1]).astype(bf16)
        values = product(flat_norm, w_qkv[2]).astype(bf16)
        picks = images * select
        column = lax.broadcasted_iota(jnp.int32, (picks, images * patches), 1)
        pick_image = lax.broadcasted_iota(jnp.int32, (picks, 1), 0) // select
        wanted = pick_image * patches + sample_pos.reshape(picks, 1)
        chosen = (column == wanted).astype(bf16)
        picked_norm = product(chosen, flat_norm).astype(bf16)
        picked_in = product(chosen, flat_in)
        queries = product(picked_norm, w_qkv[0]).astype(bf16)
        lane_head = lax.broadcasted_iota(jnp.int32, (1, local_width), 1) // HEAD_DIM
        heads_here = local_width // HEAD_DIM

        def by_head(block):
            return jnp.concatenate(
                [jnp.where(lane_head == h, block, 0).astype(bf16) for h in range(heads_here)]
            )

        def merge_heads(block):
            merged = block[:picks]
            for h in range(1, heads_here):
                merged = jnp.where(lane_head == h, block[h * picks : (h + 1) * picks], merged)
            return merged.astype(bf16)

        scores = product(by_head(queries), keys, ((1,), (1,))) * scale
        own_image = jnp.tile(column // patches == pick_image, (heads_here, 1))
        probs = jax.nn.softmax(jnp.where(own_image, scores, -jnp.inf), axis=-1)
        probs_low = probs.astype(bf16)
        context = merge_heads(product(probs_low, values))
        value_side = product(probs_low, flat_norm).astype(bf16)
        mixed = product(context, w_attn_out)

        held = spread_rows(jnp.concatenate([teacher_local, queries, context], axis=1))
        target = product(held[:, :features], projector)
        target = target.reshape(cores, y_parts, z_parts, rows, -1).transpose(2, 1, 0, 3, 4)
        target = exchange(target.reshape(wide, rows, -1), "wide")
        target = target.transpose(1, 0, 2).reshape(rows, -1)
        student_out = picked_in + jnp.sum(spread(mixed - target, "narrow", narrow), axis=0)
        delta = (student_out / (select * images)).astype(bf16)

        d_context = product(delta, w_attn_out, ((1,), (1,))).astype(bf16)
        d_probs = product(by_head(d_context), values, ((1,), (1,)))
        d_scores = (
            probs * (d_probs - jnp.sum(probs * d_probs, axis=-1, keepdims=True)) * scale
        ).astype(bf16)
        d_query = merge_heads(product(d_scores, keys))
        key_side = product(d_scores, flat_norm).astype(bf16)

        factors = jnp.concatenate([delta, picked_norm, key_side, value_side], axis=0)
        kinds = factors.shape[0] // rows
        piece = width // wide
        per_tile = LANES // piece
        tiles = width // LANES
        factors = factors.reshape(kinds, rows, tiles, LANES).transpose(2, 1, 0, 3)
        factors = factors.reshape(tiles * rows, kinds * LANES)
        at_in = lax.broadcasted_iota(jnp.int32, (kinds * LANES, per_tile * LANES), 0)
        at_out = lax.broadcasted_iota(jnp.int32, (kinds * LANES, per_tile * LANES), 1)
        lane_in, kind_in = at_in % LANES, at_in // LANES
        lane_out, tile_out = at_out % LANES, at_out // LANES
        move = (
            (lane_in // piece == tile_out)
            & (lane_out // piece == kind_in)
            & (lane_in % piece == lane_out % piece)
        ).astype(bf16)
        packed = product(factors, move).astype(bf16)
        packed = packed.reshape(tiles, rows, per_tile, LANES).transpose(0, 2, 1, 3)
        packed = packed.reshape(wide, rows, LANES)
        late = jnp.concatenate([d_query, d_context], axis=1)
        late = jnp.broadcast_to(late[None], (wide,) + late.shape)
        got = exchange(jnp.concatenate([packed, late], axis=2), "wide")
        got = got.reshape(z_parts, y_parts, cores, rows, -1).transpose(2, 1, 0, 3, 4)
        got = got.reshape(total_rows, -1)
        full = product(
            got[:, :LANES],
            jnp.concatenate([held, got[:, LANES:]], axis=1),
            ((0,), (0,)),
        )

        def part(kind, start, size):
            return full[kind * piece : (kind + 1) * piece, start : start + size]

        at_query = features
        at_context = at_query + local_width
        at_d_query = at_context + local_width
        at_d_context = at_d_query + local_width
        grad_projector = -part(0, 0, features).T
        grad_attn_out = part(0, at_context, local_width).T
        grad_query = part(1, at_d_query, local_width)
        grad_key = part(2, at_query, local_width)
        grad_value = part(2 + heads_here, at_d_context, local_width)
        for h in range(1, heads_here):
            here = lane_head == h
            grad_key = jnp.where(here, part(2 + h, at_query, local_width), grad_key)
            grad_value = jnp.where(
                here, part(2 + heads_here + h, at_d_context, local_width), grad_value
            )
        return (jnp.stack([grad_query, grad_key, grad_value]), grad_attn_out, grad_projector)

    return local


def solution(mesh):
    placed = (
        P("wide", "narrow"),
        P("narrow"),
        P("narrow", "wide"),
        P("wide", "narrow"),
        P("narrow", "wide"),
        P("wide", None, None),
        P("wide", None),
        P(None, None, "narrow"),
        P("narrow", None),
    )
    return jax.shard_map(
        make_local(mesh.shape["wide"], mesh.shape["narrow"], Z_PARTS, CORES),
        mesh=mesh,
        in_specs=placed,
        out_specs=(P(None, "wide", "narrow"), P("narrow", "wide"), P("narrow", "wide")),
        check_vma=False,
    )
```

time: 856 us -> 226 us (0.26)
  waiting for transfers between devices: 555 us -> 52.8 us
  blocking collectives: 212 us -> 94.4 us
  starting transfers between devices: 18.5 us -> 35.4 us
  between operations: 14 us -> 1.3 us
  matrix products: 28.1 us -> 19.4 us
    reduce_scatter x3 -> x0, waiting for transfers between devices: 397 us -> none  [the longest x1 153 us: local(): lax.psum_scatter(stacked, 'wide', scatter_dimension=1, tiled=True)]
    psum x2 -> x0, waiting for transfers between devices: 148 us -> none  [the longest x1 74.6 us: local(): pre_full = lax.psum(pre_part, 'narrow')]
    all_gather x2 -> x3, blocking collectives: 179 us -> 48.9 us  [gather_rows(): block = lax.all_gather(block, 'wide', axis_index_groups=groups, tiled=True)]
    all_to_all x1 -> x8, waiting for transfers between devices: 10.9 us -> 52.8 us  [exchange(): return lax.all_to_all(block, axis, 0, 0, axis_index_groups=groups)]
    all_to_all x1 -> x4, blocking collectives: 16.6 us -> 45.5 us  [exchange(): return lax.all_to_all(block, axis, 0, 0, axis_index_groups=groups)]
    all_to_all x1 -> x8, starting transfers between devices: 18.1 us -> 35.4 us  [exchange(): return lax.all_to_all(block, axis, 0, 0, axis_index_groups=groups)]
    psum x1 -> x0, blocking collectives: 16 us -> none  [local(): lax.psum((jnp.sum(wide_in, axis=1), jnp.sum(wide_in * wide_in, axis=1)),...]
    dot_general x19 -> x18, matrix products: 28.1 us -> 19.4 us  [product(): lax.dot_general(left, right, (dims, ((), ())), preferred_element_type=f32)]
  transfers between devices with their start and end apart: 6 -> 8, of which waited for: 6 -> 8; matrix products, arithmetic and copies ran while one was open for 3% -> 9% of each run, Pallas kernels for 0% -> 0%
where the time goes in v1:
time: 226 us; the launch traced here: 225 us
  blocking collectives  94.4 us (42%)
  waiting for transfers between devices  52.8 us (23%)
  starting transfers between devices  35.4 us (16%)
  matrix products  19.4 us (9%)
  other arithmetic  13.9 us (6%)
  local copies, waits for them, and re-layouts  8 us (4%)
    all_to_all x8, waiting for transfers between devices, exchange(): return lax.all_to_all(block, axis, 0, 0, axis_index_groups=groups)  52.8 us
    all_gather x3, blocking collectives, gather_rows(): block = lax.all_gather(block, 'wide', axis_index_groups=groups, tiled=True)  48.9 us
    all_to_all x4, blocking collectives, exchange(): return lax.all_to_all(block, axis, 0, 0, axis_index_groups=groups)  45.5 us
    all_to_all x8, starting transfers between devices, exchange(): return lax.all_to_all(block, axis, 0, 0, axis_index_groups=groups)  35.4 us
    dot_general x18, matrix products, product(): lax.dot_general(left, right, (dims, ((), ())), preferred_element_type=f32)  19.4 us
  transfers between devices with their start and end apart: 8, of which 8 were waited for; matrix products, arithmetic and copies ran while one was open for 9% of the time, Pallas kernels for 0%

profile of v1, /device:TPU:1, one launch (start us, length us, event | category | flops | bytes accessed | tf_op | source)
XLA Modules:
  0.0 225.1 jit_solution(1020538049066519287)
XLA Ops:
  0.7 1.0 convert_reduce_fusion.3
  1.7 0.6 broadcast_in_dim.122
  2.3 6.7 %all-to-all-start = ((f32[8,8,2]{1,2,0:T(2,128)}), f32[8,8,2]{1,2,0:T(2,128)S(1)}, u32[]{:S(2)}, u32[]{:S(2)}) async-start(f32[8,8,2]{1,2,0:T(2,128)} %broadcast_in_dim.122), calls=%async_computation | async-start | bytes 16384 | tf_op jit(solution)/shard_map/all_to_all | solution.py:32
  9.0 2.3 %convert_reduce_fusion = (f32[4,256]{1,0:T(4,128)S(1)}, f32[4,256]{1,0:T(4,128)S(1)}) fusion(bf16[4,256,1024]{2,1,0:T(8,128)(2,1)} %param.14), kind=kLoop, calls=%fused_computation.10 | loop fusion | flops 4192256 | bytes 2105344 | tf_op jit(solution)/shard_map/reduce_sum | solution.py:107
  11.4 1.9 multiply_convert_fusion
  14.1 15.3 %all_gather.9 = bf16[32,768]{1,0:T(8,128)(2,1)S(1)} all-gather(bf16[8,768]{1,0:T(8,128)(2,1)S(1)} %fusion.73), channel_id=1, replica_groups={{0,128,256,384},{8,136,264,392},{16,144,272,400},{24,152,280,408},{32,1..., dimensions={0}, use_global_device_ids=true | all-gather | bytes 61440 | tf_op jit(solution)/shard_map/all_gather | solution.py:45
  29.5 20.5 %all_gather.10 = bf16[256,768]{1,0:T(8,128)(2,1)S(1)} all-gather(bf16[32,768]{1,0:T(8,128)(2,1)S(1)} %all_gather.9), channel_id=1, replica_groups={{0,16,32,48,64,80,96,112},{8,24,40,56,72,88,104,120},{128,144,160,176,1..., dimensions={0}, use_global_device_ids=true | all-gather | bytes 442368 | tf_op jit(solution)/shard_map/all_gather | solution.py:45
  50.0 13.0 %all_gather.11 = bf16[512,768]{1,0:T(8,128)(2,1)S(1)} all-gather(bf16[256,768]{1,0:T(8,128)(2,1)S(1)} %all_gather.10), channel_id=1, replica_groups={{0,8},{16,24},{32,40},{48,56},{64,72},{80,88},{96,104},{112,120},{128,1..., dimensions={0}, use_global_device_ids=true | all-gather | bytes 1179648 | tf_op jit(solution)/shard_map/all_gather | solution.py:45
  63.0 2.4 %convolution_convert_fusion.1 = bf16[512,384]{1,0:T(8,128)(2,1)} fusion(bf16[512,768]{1,0:T(8,128)(2,1)S(1)} %all_gather.11, bf16[768,384]{1,0:T(8,128)(2,1)} %param.11), kind=kOutput, calls=%fused_computation.60 | convolution fusion | flops 302186496 | bytes 1769472 | tf_op jit(solution)/shard_map/dot_general | solution.py:17
  65.4 3.8 %all-to-all-start.1 = ((bf16[8,64,384]{2,1,0:T(8,128)(2,1)}), bf16[8,64,384]{2,1,0:T(8,128)(2,1)S(1)}, u32[]{:S(2)}, u32[]{:S(2)}) async-start(bf16[8,64,384]{2,1,0:T(8,128)(2,1)} %bitcast.10), calls=%async_computation.1 | async-start | bytes 786432 | tf_op jit(solution)/shard_map/all_to_all | solution.py:32
  69.3 2.0 convolution_convert_fusion.6
  71.3 1.7 broadcast_select_fusion.1
  73.0 4.4 %all-to-all-done.1 = bf16[8,64,384]{2,1,0:T(8,128)(2,1)S(1)} async-done(((bf16[8,64,384]{2,1,0:T(8,128)(2,1)}), bf16[8,64,384]{2,1,0:T(8,128)(2,1)S(1)}, u32[]{:S(2)}, u32[]{:S(2)}) %all-to-all-start.1) | async-done | bytes 393248 | tf_op jit(solution)/shard_map/all_to_all | solution.py:32
  77.6 0.8 broadcast_in_dim.123
  78.4 3.5 %all-to-all-start.2 = ((bf16[8,64,384]{2,1,0:T(8,128)(2,1)}), bf16[8,64,384]{2,1,0:T(8,128)(2,1)S(1)}, u32[]{:S(2)}, u32[]{:S(2)}) async-start(bf16[8,64,384]{2,1,0:T(8,128)(2,1)} %broadcast_in_dim.123), calls=%async_computation.2 | async-start | bytes 786432 | tf_op jit(solution)/shard_map/all_to_all | solution.py:32
  81.9 0.7 select_compare_fusion.2
  83.1 1.3 copy-done.3
  84.4 2.4 %convolution_convert_fusion.3 = bf16[1024,128]{1,0:T(8,128)(2,1)} fusion(bf16[1024,1024]{1,0:T(8,128)(2,1)S(1)} %bitcast.94, bf16[3,1024,128]{2,1,0:T(8,128)(2,1)} %param.16), kind=kOutput, calls=%fused_computation.62 | convolution fusion | flops 268566528 | bytes 2621440 | tf_op jit(solution)/shard_map/dot_general | solution.py:17
  86.8 2.2 all-to-all-done.2
  89.6 6.4 %all_to_all.60 = bf16[2,256,768]{2,1,0:T(8,128)(2,1)S(1)} all-to-all(bf16[2,256,768]{2,1,0:T(8,128)(2,1)S(1)} %bitcast.92), channel_id=1, replica_groups={{0,8},{16,24},{32,40},{48,56},{64,72},{80,88},{96,104},{112,120},{128,1..., dimensions={0} | all-to-all | bytes 1572864 | tf_op jit(solution)/shard_map/all_to_all | solution.py:32
  96.0 1.0 reduce_sum.118
  97.0 5.3 %all-to-all-start.4 = ((bf16[8,32,768]{2,1,0:T(8,128)(2,1)}), bf16[8,32,768]{2,1,0:T(8,128)(2,1)S(1)}, u32[]{:S(2)}, u32[]{:S(2)}) async-start(bf16[8,32,768]{2,1,0:T(8,128)(2,1)} %bitcast.98), calls=%async_computation.4 | async-start | bytes 786432 | tf_op jit(solution)/shard_map/all_to_all | solution.py:32
  102.4 1.2 fusion.118
  103.8 2.3 %convolution_convert_fusion.2 = bf16[1024,128]{1,0:T(8,128)(2,1)S(1)} fusion(bf16[1024,1024]{1,0:T(8,128)(2,1)} %bitcast.95, bf16[3,1024,128]{2,1,0:T(8,128)(2,1)} %param.16), kind=kOutput, calls=%fused_computation.61 | convolution fusion | flops 268566528 | bytes 2621440 | tf_op jit(solution)/shard_map/dot_general | solution.py:17
  106.4 11.1 %all-to-all-done.4 = bf16[8,32,768]{2,1,0:T(8,128)(2,1)S(1)} async-done(((bf16[8,32,768]{2,1,0:T(8,128)(2,1)}), bf16[8,32,768]{2,1,0:T(8,128)(2,1)S(1)}, u32[]{:S(2)}, u32[]{:S(2)}) %all-to-all-start.4) | async-done | bytes 393248 | tf_op jit(solution)/shard_map/all_to_all | solution.py:32
  117.5 0.7 convert_reduce_fusion.1
  118.2 4.6 %all-to-all-start.5 = ((f32[4,8,768]{2,1,0:T(8,128)}), f32[4,8,768]{2,1,0:T(8,128)S(1)}, u32[]{:S(2)}, u32[]{:S(2)}) async-start(f32[4,8,768]{2,1,0:T(8,128)} %bitcast.14), calls=%async_computation.5 | async-start | bytes 196608 | tf_op jit(solution)/shard_map/all_to_all | solution.py:32
  122.8 7.0 %all-to-all-done.5 = f32[4,8,768]{2,1,0:T(8,128)S(1)} async-done(((f32[4,8,768]{2,1,0:T(8,128)}), f32[4,8,768]{2,1,0:T(8,128)S(1)}, u32[]{:S(2)}, u32[]{:S(2)}) %all-to-all-start.5) | async-done | bytes 98336 | tf_op jit(solution)/shard_map/all_to_all | solution.py:32
  129.9 9.3 %all_to_all.61 = bf16[4,8,1024]{2,1,0:T(8,128)(2,1)S(1)} all-to-all(bf16[4,8,1024]{2,1,0:T(8,128)(2,1)S(1)} %broadcast_in_dim.124), channel_id=1, replica_groups={{0,128,256,384},{8,136,264,392},{16,144,272,400},{24,152,280,408},{32,1..., dimensions={0} | all-to-all | bytes 131072 | tf_op jit(solution)/shard_map/all_to_all | solution.py:32
  139.2 0.9 broadcast_in_dim.126
  140.1 3.5 %all-to-all-start.7 = ((bf16[8,32,1024]{2,1,0:T(8,128)(2,1)}), bf16[8,32,1024]{2,1,0:T(8,128)(2,1)S(1)}, u32[]{:S(2)}, u32[]{:S(2)}) async-start(bf16[8,32,1024]{2,1,0:T(8,128)(2,1)} %broadcast_in_dim.126), calls=%async_computation.7 | async-start | bytes 1048576 | tf_op jit(solution)/shard_map/all_to_all | solution.py:32
  145.4 12.0 %all-to-all-done.7 = bf16[8,32,1024]{2,1,0:T(8,128)(2,1)S(1)} async-done(((bf16[8,32,1024]{2,1,0:T(8,128)(2,1)}), bf16[8,32,1024]{2,1,0:T(8,128)(2,1)S(1)}, u32[]{:S(2)}, u32[]{:S(2)}) %all-to-all-start.7) | async-done | bytes 524320 | tf_op jit(solution)/shard_map/all_to_all | solution.py:32
  157.5 8.8 %all_to_all.62 = bf16[2,256,1024]{2,1,0:T(8,128)(2,1)S(1)} all-to-all(bf16[2,256,1024]{2,1,0:T(8,128)(2,1)S(1)} %broadcast_in_dim.128), channel_id=1, replica_groups={{0,8},{16,24},{32,40},{48,56},{64,72},{80,88},{96,104},{112,120},{128,1..., dimensions={0} | all-to-all | bytes 2097152 | tf_op jit(solution)/shard_map/all_to_all | solution.py:32
  166.3 1.0 copy-done.5
  167.3 1.1 fusion.46
  168.4 0.8 reshape.352
  169.1 4.4 %all-to-all-start.9 = ((f32[64,1,128]{2,1,0:T(1,128)}), f32[64,1,128]{2,1,0:T(1,128)S(1)}, u32[]{:S(2)}, u32[]{:S(2)}) async-start(f32[64,1,128]{2,1,0:T(1,128)} %reshape.352), calls=%async_computation.9 | async-start | bytes 65536 | tf_op jit(solution)/shard_map/all_to_all | solution.py:32
  174.1 11.1 %all-to-all-done.9 = f32[64,1,128]{2,1,0:T(1,128)S(1)} async-done(((f32[64,1,128]{2,1,0:T(1,128)}), f32[64,1,128]{2,1,0:T(1,128)S(1)}, u32[]{:S(2)}, u32[]{:S(2)}) %all-to-all-start.9) | async-done | bytes 32800 | tf_op jit(solution)/shard_map/all_to_all | solution.py:32
  185.8 0.7 reduce.3
  187.0 0.7 broadcast_in_dim.129
  187.7 3.6 %all-to-all-start.10 = ((f32[8,8,1024]{2,1,0:T(8,128)}), f32[8,8,1024]{2,1,0:T(8,128)S(1)}, u32[]{:S(2)}, u32[]{:S(2)}) async-start(f32[8,8,1024]{2,1,0:T(8,128)} %broadcast_in_dim.129), calls=%async_computation.10 | async-start | bytes 524288 | tf_op jit(solution)/shard_map/all_to_all | solution.py:32
  191.4 2.0 convolution_convert_fusion.4
  193.4 4.4 %all-to-all-done.10 = f32[8,8,1024]{2,1,0:T(8,128)S(1)} async-done(((f32[8,8,1024]{2,1,0:T(8,128)}), f32[8,8,1024]{2,1,0:T(8,128)S(1)}, u32[]{:S(2)}, u32[]{:S(2)}) %all-to-all-start.10) | async-done | bytes 262176 | tf_op jit(solution)/shard_map/all_to_all | solution.py:32
  200.1 1.5 fusion.40
  201.8 21.0 %all_to_all.63 = bf16[64,8,384]{2,1,0:T(8,128)(2,1)S(1)} all-to-all(bf16[64,8,384]{2,1,0:T(8,128)(2,1)S(1)} %pad_maximum_fusion), channel_id=1, replica_groups=mesh['wide'=64,'narrow'=8] {'wide'}, dimensions={0} | all-to-all | bytes 786432 | tf_op jit(solution)/shard_map/all_to_all | solution.py:32
  223.3 0.6 fusion.81
  223.9 0.6 fusion.69
  224.5 0.6 pad_maximum_fusion.1
  (122 shorter events, 9.0 us)
Async XLA Ops:
  0.6 88.4 %copy-start = (bf16[384,768]{1,0:T(8,128)(2,1)S(1)}, bf16[384,768]{1,0:T(8,128)(2,1)}, u32[]{:S(2)}) copy-start(bf16[384,768]{1,0:T(8,128)(2,1)} %param.12) | copy-start | bytes 1769476
  0.6 10.7 %copy-start.1 = (bf16[4,256,1024]{2,1,0:T(8,128)(2,1)S(1)}, bf16[4,256,1024]{2,1,0:T(8,128)(2,1)}, u32[]{:S(2)}) copy-start(bf16[4,256,1024]{2,1,0:T(8,128)(2,1)} %param.14) | copy-start | bytes 6291460
  2.3 11.7 %all-to-all-start = ((f32[8,8,2]{1,2,0:T(2,128)}), f32[8,8,2]{1,2,0:T(2,128)S(1)}, u32[]{:S(2)}, u32[]{:S(2)}) async-start(f32[8,8,2]{1,2,0:T(2,128)} %broadcast_in_dim.122), calls=%async_computation | async-start | bytes 16384 | tf_op jit(solution)/shard_map/all_to_all | solution.py:32
  9.0 62.3 %copy-start.11 = (pred[128]{0:T(512)(128)(4,1)}, pred[128]{0:T(512)(128)(4,1)S(1)}, u32[]{:S(2)}) copy-start(pred[128]{0:T(512)(128)(4,1)S(1)} %broadcast_compare_fusion.1) | copy-start | bytes 388
  9.0 62.3 %copy-start.24 = (pred[128]{0:T(512)(128)(4,1)}, pred[128]{0:T(512)(128)(4,1)S(1)}, u32[]{:S(2)}) copy-start(pred[128]{0:T(512)(128)(4,1)S(1)} %broadcast_compare_fusion) | copy-start | bytes 388
  11.3 1.9 copy-start.29
  11.4 2.1 copy-start.28
  11.4 2.7 %copy-start.8 = (bf16[8,768]{1,0:T(8,128)(2,1)S(1)}, bf16[8,768]{1,0:T(8,128)(2,1)}, u32[]{:S(2)}) copy-start(bf16[8,768]{1,0:T(8,128)(2,1)} %param.9) | copy-start | bytes 36868
  65.4 11.9 %all-to-all-start.1 = ((bf16[8,64,384]{2,1,0:T(8,128)(2,1)}), bf16[8,64,384]{2,1,0:T(8,128)(2,1)S(1)}, u32[]{:S(2)}, u32[]{:S(2)}) async-start(bf16[8,64,384]{2,1,0:T(8,128)(2,1)} %bitcast.10), calls=%async_computation.1 | async-start | bytes 786432 | tf_op jit(solution)/shard_map/all_to_all | solution.py:32
  69.2 9.2 %copy-start.26 = (s32[8]{0:T(128)}, s32[8]{0:T(128)S(1)}, u32[]{:S(2)}) copy-start(s32[8]{0:T(128)S(1)} %multiply_add_fusion) | copy-start | bytes 100
  71.3 11.8 %copy-start.9 = (bf16[8,1024]{1,0:T(8,128)(2,1)}, bf16[8,1024]{1,0:T(8,128)(2,1)S(1)}, u32[]{:S(2)}) copy-start(bf16[8,1024]{1,0:T(8,128)(2,1)S(1)} %convolution_convert_fusion.6) | copy-start | bytes 49156
  78.4 10.6 %all-to-all-start.2 = ((bf16[8,64,384]{2,1,0:T(8,128)(2,1)}), bf16[8,64,384]{2,1,0:T(8,128)(2,1)S(1)}, u32[]{:S(2)}, u32[]{:S(2)}) async-start(bf16[8,64,384]{2,1,0:T(8,128)(2,1)} %broadcast_in_dim.123), calls=%async_computation.2 | async-start | bytes 786432 | tf_op jit(solution)/shard_map/all_to_all | solution.py:32
  83.1 1.3 copy-start.3
  97.0 20.5 %all-to-all-start.4 = ((bf16[8,32,768]{2,1,0:T(8,128)(2,1)}), bf16[8,32,768]{2,1,0:T(8,128)(2,1)S(1)}, u32[]{:S(2)}, u32[]{:S(2)}) async-start(bf16[8,32,768]{2,1,0:T(8,128)(2,1)} %bitcast.98), calls=%async_computation.4 | async-start | bytes 786432 | tf_op jit(solution)/shard_map/all_to_all | solution.py:32
  102.3 20.5 %copy-start.12 = (pred[128]{0:T(512)(128)(4,1)S(1)}, pred[128]{0:T(512)(128)(4,1)}, u32[]{:S(2)}) copy-start(pred[128]{0:T(512)(128)(4,1)} %copy-done.11) | copy-start | bytes 388
  103.6 35.6 %copy-start.15 = (f32[16]{0:T(128)}, f32[16]{0:T(128)S(1)}, u32[]{:S(2)}) copy-start(f32[16]{0:T(128)S(1)} %get-tuple-element.22) | copy-start | bytes 196
  103.6 26.3 %copy-start.14 = (bf16[8,128]{1,0:T(8,128)(2,1)S(1)}, bf16[8,128]{1,0:T(8,128)(2,1)}, u32[]{:S(2)}) copy-start(bf16[8,128]{1,0:T(8,128)(2,1)} %get-tuple-element.21) | copy-start | bytes 6148
  103.8 35.4 %copy-start.17 = (f32[16]{0:T(128)}, f32[16]{0:T(128)S(1)}, u32[]{:S(2)}) copy-start(f32[16]{0:T(128)S(1)} %fusion.68) | copy-start | bytes 196
  106.1 33.9 %copy-start.32 = (bf16[1024,128]{1,0:T(8,128)(2,1)}, bf16[1024,128]{1,0:T(8,128)(2,1)S(1)}, u32[]{:S(2)}) copy-start(bf16[1024,128]{1,0:T(8,128)(2,1)S(1)} %convolution_convert_fusion.2) | copy-start | bytes 786436
  118.2 11.7 %all-to-all-start.5 = ((f32[4,8,768]{2,1,0:T(8,128)}), f32[4,8,768]{2,1,0:T(8,128)S(1)}, u32[]{:S(2)}, u32[]{:S(2)}) async-start(f32[4,8,768]{2,1,0:T(8,128)} %bitcast.14), calls=%async_computation.5 | async-start | bytes 196608 | tf_op jit(solution)/shard_map/all_to_all | solution.py:32
  140.1 17.3 %all-to-all-start.7 = ((bf16[8,32,1024]{2,1,0:T(8,128)(2,1)}), bf16[8,32,1024]{2,1,0:T(8,128)(2,1)S(1)}, u32[]{:S(2)}, u32[]{:S(2)}) async-start(bf16[8,32,1024]{2,1,0:T(8,128)(2,1)} %broadcast_in_dim.126), calls=%async_computation.7 | async-start | bytes 1048576 | tf_op jit(solution)/shard_map/all_to_all | solution.py:32
  166.3 1.0 copy-start.5
  166.3 20.6 %copy-start.4 = (bf16[128,1024]{1,0:T(8,128)(2,1)S(1)}, bf16[128,1024]{1,0:T(8,128)(2,1)}, u32[]{:S(2)}) copy-start(bf16[128,1024]{1,0:T(8,128)(2,1)} %param.17) | copy-start | bytes 786436
  167.3 24.1 %copy-start.16 = (f32[16]{0:T(128)S(1)}, f32[16]{0:T(128)}, u32[]{:S(2)}) copy-start(f32[16]{0:T(128)} %copy-done.15) | copy-start | bytes 196
  167.3 24.1 %copy-start.18 = (f32[16]{0:T(128)S(1)}, f32[16]{0:T(128)}, u32[]{:S(2)}) copy-start(f32[16]{0:T(128)} %copy-done.17) | copy-start | bytes 196
  169.1 16.1 %all-to-all-start.9 = ((f32[64,1,128]{2,1,0:T(1,128)}), f32[64,1,128]{2,1,0:T(1,128)S(1)}, u32[]{:S(2)}, u32[]{:S(2)}) async-start(f32[64,1,128]{2,1,0:T(1,128)} %reshape.352), calls=%async_computation.9 | async-start | bytes 65536 | tf_op jit(solution)/shard_map/all_to_all | solution.py:32
  186.9 11.0 %copy-start.27 = (s32[8]{0:T(128)S(1)}, s32[8]{0:T(128)}, u32[]{:S(2)}) copy-start(s32[8]{0:T(128)} %copy-done.26) | copy-start | bytes 100
  187.7 10.0 %all-to-all-start.10 = ((f32[8,8,1024]{2,1,0:T(8,128)}), f32[8,8,1024]{2,1,0:T(8,128)S(1)}, u32[]{:S(2)}, u32[]{:S(2)}) async-start(f32[8,8,1024]{2,1,0:T(8,128)} %broadcast_in_dim.129), calls=%async_computation.10 | async-start | bytes 524288 | tf_op jit(solution)/shard_map/all_to_all | solution.py:32
  191.4 6.9 %copy-start.13 = (pred[128]{0:T(512)(128)(4,1)S(1)}, pred[128]{0:T(512)(128)(4,1)}, u32[]{:S(2)}) copy-start(pred[128]{0:T(512)(128)(4,1)} %copy-done.11) | copy-start | bytes 388
  191.4 6.9 %copy-start.25 = (pred[128]{0:T(512)(128)(4,1)S(1)}, pred[128]{0:T(512)(128)(4,1)}, u32[]{:S(2)}) copy-start(pred[128]{0:T(512)(128)(4,1)} %copy-done.24) | copy-start | bytes 388
  197.8 1.0 copy-start.33
  197.8 1.7 copy-start.2
  197.8 2.0 copy-start.7
  198.3 1.8 copy-start.10
  198.3 1.8 copy-start.19
  198.3 1.8 copy-start.20
  198.3 1.8 copy-start.21
  198.3 1.8 copy-start.22
  198.3 1.8 copy-start.23
  198.3 1.8 copy-start.30
  198.4 1.8 copy-start.31
  201.7 21.2 %copy-start.6 = (bf16[2,256,1024]{2,1,0:T(8,128)(2,1)S(1)}, bf16[2,256,1024]{2,1,0:T(8,128)(2,1)}, u32[]{:S(2)}) copy-start(bf16[2,256,1024]{2,1,0:T(8,128)(2,1)} %copy-done.5) | copy-start | bytes 3145732

commit v2 on v1

--- a/solution.py
+++ b/solution.py
@@ -6,7 +6,6 @@
 HEAD_DIM = 64
 LANES = 128
 EPSILON = 1e-06
-Z_PARTS = 4
 CORES = 2
 
 f32 = jnp.float32
@@ -17,15 +16,8 @@
     return lax.dot_general(left, right, (dims, ((), ())), preferred_element_type=f32)
 
 
-def wide_groups(z_parts, y_parts, cores):
-    def place(z, y, c):
-        return (z * y_parts + y) * cores + c
-
-    zs, ys, cs = range(z_parts), range(y_parts), range(cores)
-    along_z = [[place(z, y, c) for z in zs] for y in ys for c in cs]
-    along_y = [[place(z, y, c) for y in ys] for z in zs for c in cs]
-    along_c = [[place(z, y, c) for c in cs] for z in zs for y in ys]
-    return along_z, along_y, along_c
+def chip_groups(wide, cores):
+    return [[chip * cores + c for chip in range(wide // cores)] for c in range(cores)]
 
 
 def exchange(block, axis, groups=None):
@@ -36,28 +28,13 @@
     return exchange(jnp.broadcast_to(block[None], (count,) + block.shape), axis, groups)
 
 
-def make_local(wide, narrow, z_parts, cores):
-    y_parts = wide // (z_parts * cores)
-    along_z, along_y, along_c = wide_groups(z_parts, y_parts, cores)
-
-    def gather_rows(block):
-        for groups in (along_z, along_y, along_c):
-            block = lax.all_gather(block, "wide", axis_index_groups=groups, tiled=True)
-        return block
-
-    def spread_rows(block):
-        width = block.shape[1]
-        for groups in (along_z, along_y, along_c):
-            block = spread(block, "wide", len(groups[0]), groups).reshape(-1, width)
-        return block
-
-    def sum_to_owners(partial):
-        width = partial.shape[1]
-        for groups, kind in ((along_c, bf16), (along_y, bf16), (along_z, f32)):
-            count = len(groups[0])
-            block = partial.astype(kind).reshape(count, -1, width)
-            partial = jnp.sum(exchange(block, "wide", groups).astype(f32), axis=0)
-        return partial
+def make_local(wide, narrow):
+    chips = wide // CORES
+    groups = chip_groups(wide, CORES)
+    pairs = [(i, i ^ 1) for i in range(wide)]
+
+    def swap(block):
+        return lax.ppermute(block, "wide", pairs)
 
     def local(
         teacher_in,
@@ -76,7 +53,8 @@
         select = sample_pos.shape[1]
         local_width = w_qkv.shape[2]
         scale = HEAD_DIM ** (-0.5)
-        total_rows = rows * wide
+        half = rows * chips
+        first_core = lax.axis_index("wide") % CORES == 0
 
         own = teacher_in.astype(f32)
         sums = jnp.concatenate(
@@ -92,15 +70,35 @@
         normed = (
             (own - center) * lax.rsqrt(variance + EPSILON) * teacher_gain.astype(f32)
         ).astype(bf16)
-        normed = gather_rows(normed)
-
-        pre = product(normed, mlp_in).astype(bf16)
-        pre = exchange(pre.reshape(narrow, total_rows // narrow, -1), "narrow")
-        pre = jnp.sum(pre.astype(f32), axis=0)
+        normed = spread(normed, "wide", chips, groups).reshape(half, features)
+        normed_other = swap(normed)
+
+        pre = jnp.concatenate(
+            [
+                product(block, mlp_in).astype(bf16).reshape(narrow, half // narrow, -1)
+                for block in (normed, normed_other)
+            ],
+            axis=1,
+        )
+        pre = jnp.sum(exchange(pre, "narrow").astype(f32), axis=0)
         hidden = jax.nn.gelu(pre, approximate=False).astype(bf16)
-        hidden = spread(hidden, "narrow", narrow).reshape(total_rows, -1)
-        branch = sum_to_owners(product(hidden, mlp_out))
-        teacher_local = (own + branch).astype(bf16)
+        hidden = spread(hidden, "narrow", narrow)
+        hidden_own = hidden[:, : half // narrow].reshape(half, -1)
+        hidden_other = hidden[:, half // narrow :].reshape(half, -1)
+        branch = swap(product(hidden_other, mlp_out).astype(bf16))
+        branch = (product(hidden_own, mlp_out) + branch.astype(f32)).astype(bf16)
+        branch = exchange(branch.reshape(chips, rows, features), "wide", groups)
+        teacher_local = (own + jnp.sum(branch.astype(f32), axis=0)).astype(bf16)
+
+        columns = spread(projector.T, "wide", chips, groups)
+        columns_other = swap(columns)
+        columns = jnp.stack(
+            [
+                jnp.where(first_core, columns, columns_other),
+                jnp.where(first_core, columns_other, columns),
+            ],
+            axis=1,
+        ).reshape(-1, features)
 
         flat_in = student_in.reshape(images * patches, width)
         source = flat_in.astype(f32)
@@ -139,11 +137,7 @@
         value_side = product(probs_low, flat_norm).astype(bf16)
         mixed = product(context, w_attn_out)
 
-        held = spread_rows(jnp.concatenate([teacher_local, queries, context], axis=1))
-        target = product(held[:, :features], projector)
-        target = target.reshape(cores, y_parts, z_parts, rows, -1).transpose(2, 1, 0, 3, 4)
-        target = exchange(target.reshape(wide, rows, -1), "wide")
-        target = target.transpose(1, 0, 2).reshape(rows, -1)
+        target = product(teacher_local, columns, ((1,), (1,)))
         student_out = picked_in + jnp.sum(spread(mixed - target, "narrow", narrow), axis=0)
         delta = (student_out / (select * images)).astype(bf16)
 
@@ -173,17 +167,23 @@
         ).astype(bf16)
         packed = product(factors, move).astype(bf16)
         packed = packed.reshape(tiles, rows, per_tile, LANES).transpose(0, 2, 1, 3)
-        packed = packed.reshape(wide, rows, LANES)
-        late = jnp.concatenate([d_query, d_context], axis=1)
-        late = jnp.broadcast_to(late[None], (wide,) + late.shape)
-        got = exchange(jnp.concatenate([packed, late], axis=2), "wide")
-        got = got.reshape(z_parts, y_parts, cores, rows, -1).transpose(2, 1, 0, 3, 4)
-        got = got.reshape(total_rows, -1)
-        full = product(
-            got[:, :LANES],
-            jnp.concatenate([held, got[:, LANES:]], axis=1),
-            ((0,), (0,)),
-        )
+        packed = packed.reshape(chips, CORES, rows, LANES)
+        shared = jnp.concatenate([teacher_local, queries, context, d_query, d_context], axis=1)
+        shared_width = shared.shape[1]
+        shared = jnp.broadcast_to(shared[None], (chips,) + shared.shape)
+        got = jnp.concatenate([shared] + [packed[:, c] for c in range(CORES)], axis=2)
+        got = exchange(got, "wide", groups).reshape(half, -1)
+        got_other = swap(got)
+
+        def rows_product(block):
+            ours = jnp.where(
+                first_core,
+                block[:, shared_width : shared_width + LANES],
+                block[:, shared_width + LANES :],
+            )
+            return product(ours, block[:, :shared_width], ((0,), (0,)))
+
+        full = rows_product(got) + rows_product(got_other)
 
         def part(kind, start, size):
             return full[kind * piece : (kind + 1) * piece, start : start + size]
@@ -221,7 +221,7 @@
         P("narrow", None),
     )
     return jax.shard_map(
-        make_local(mesh.shape["wide"], mesh.shape["narrow"], Z_PARTS, CORES),
+        make_local(mesh.shape["wide"], mesh.shape["narrow"]),
         mesh=mesh,
         in_specs=placed,
         out_specs=(P(None, "wide", "narrow"), P("narrow", "wide"), P("narrow", "wide")),

time: 226 us -> 197 us (0.87)
  blocking collectives: 94.4 us -> 54.3 us
  starting transfers between devices: 35.4 us -> 52.9 us
  waiting for transfers between devices: 52.8 us -> 40 us
  other arithmetic: 13.9 us -> 18.3 us
  matrix products: 19.4 us -> 21.8 us
    all_gather x3 -> x0, blocking collectives: 48.9 us -> none  [gather_rows(): block = lax.all_gather(block, 'wide', axis_index_groups=groups, tiled=True)]
    ppermute x0 -> x4, starting transfers between devices: none -> 24.9 us  [swap(): return lax.ppermute(block, 'wide', pairs)]
    all_to_all x8 -> x6, waiting for transfers between devices: 52.8 us -> 38.4 us  [exchange(): return lax.all_to_all(block, axis, 0, 0, axis_index_groups=groups)]
    all_to_all x4 -> x2, blocking collectives: 45.5 us -> 54.3 us  [exchange(): return lax.all_to_all(block, axis, 0, 0, axis_index_groups=groups)]
    all_to_all x8 -> x6, starting transfers between devices: 35.4 us -> 28 us  [exchange(): return lax.all_to_all(block, axis, 0, 0, axis_index_groups=groups)]
    another operation x0 -> x2, other arithmetic: none -> 2.55 us  [local(): jnp.stack([jnp.where(first_core, columns, columns_other), jnp.where(first...]
    dot_general x18 -> x21, matrix products: 19.4 us -> 21.8 us  [product(): lax.dot_general(left, right, (dims, ((), ())), preferred_element_type=f32)]
  transfers between devices with their start and end apart: 8 -> 10, of which waited for: 8 -> 7; matrix products, arithmetic and copies ran while one was open for 9% -> 13% of each run, Pallas kernels for 0% -> 0%
where the time goes in v2:
time: 197 us; the launch traced here: 195 us
  blocking collectives  54.3 us (28%)
  starting transfers between devices  52.9 us (27%)
  waiting for transfers between devices  40 us (20%)
  matrix products  21.8 us (11%)
  other arithmetic  18.3 us (9%)
  local copies, waits for them, and re-layouts  6.37 us (3%)
    all_to_all x2, blocking collectives, exchange(): return lax.all_to_all(block, axis, 0, 0, axis_index_groups=groups)  54.3 us
    all_to_all x6, waiting for transfers between devices, exchange(): return lax.all_to_all(block, axis, 0, 0, axis_index_groups=groups)  38.4 us
    all_to_all x6, starting transfers between devices, exchange(): return lax.all_to_all(block, axis, 0, 0, axis_index_groups=groups)  28 us
    ppermute x4, starting transfers between devices, swap(): return lax.ppermute(block, 'wide', pairs)  24.9 us
    dot_general x21, matrix products, product(): lax.dot_general(left, right, (dims, ((), ())), preferred_element_type=f32)  21.8 us
  transfers between devices with their start and end apart: 10, of which 7 were waited for; matrix products, arithmetic and copies ran while one was open for 13% of the time, Pallas kernels for 0%

profile of v2, /device:TPU:1, one launch (start us, length us, event | category | flops | bytes accessed | tf_op | source)
XLA Modules:
  0.0 195.1 jit_solution(16712894288567218141)
XLA Ops:
  0.7 0.9 convert_reduce_fusion.3
  1.6 0.6 broadcast_in_dim.110
  2.2 6.7 %all-to-all-start = ((f32[8,8,2]{1,2,0:T(2,128)}), f32[8,8,2]{1,2,0:T(2,128)S(1)}, u32[]{:S(2)}, u32[]{:S(2)}) async-start(f32[8,8,2]{1,2,0:T(2,128)} %broadcast_in_dim.110), calls=%async_computation | async-start | bytes 16384 | tf_op jit(solution)/shard_map/all_to_all | solution.py:24
  8.9 0.7 convert_element_type.105
  9.6 4.4 %all-to-all-done = f32[8,8,2]{1,2,0:T(2,128)S(1)} async-done(((f32[8,8,2]{1,2,0:T(2,128)}), f32[8,8,2]{1,2,0:T(2,128)S(1)}, u32[]{:S(2)}, u32[]{:S(2)}) %all-to-all-start) | async-done | bytes 544 | tf_op jit(solution)/shard_map/all_to_all | solution.py:24
  14.0 0.8 fusion.74
  14.8 27.7 %all_to_all.40 = bf16[32,8,768]{2,1,0:T(8,128)(2,1)S(1)} all-to-all(bf16[32,8,768]{2,1,0:T(8,128)(2,1)S(1)} %broadcast_in_dim.111), channel_id=1, replica_groups={{0,16,32,48,64,80,96,112,128,144,160,176,192,208,224,240,256,272,288,30..., dimensions={0} | all-to-all | bytes 786432 | tf_op jit(solution)/shard_map/all_to_all | solution.py:24
  42.5 6.7 %collective-permute-start = (bf16[256,768]{1,0:T(8,128)(2,1)S(1)}, bf16[256,768]{1,0:T(8,128)(2,1)S(1)}, u32[]{:S(2)}, u32[]{:S(2)}) collective-permute-start(bf16[256,768]{1,0:T(8,128)(2,1)S(1)} %bitcast.105), channel_id=1, source_target_pairs={{0,8},{8,0},{16,24},{24,16},{32,40},{40,32},{48,56},{56,48},{64,72... | collective-permute-start | bytes 1179656 | tf_op jit(solution)/shard_map/ppermute | solution.py:37
  49.2 2.3 %convert_reduce_fusion = (f32[4,256]{1,0:T(4,128)S(1)}, f32[4,256]{1,0:T(4,128)S(1)}) fusion(bf16[4,256,1024]{2,1,0:T(8,128)(2,1)} %param.14), kind=kLoop, calls=%fused_computation.10 | loop fusion | flops 4192256 | bytes 2105344 | tf_op jit(solution)/shard_map/reduce_sum | solution.py:105
  52.3 0.8 pad_maximum_fusion.2
  53.1 3.5 %all-to-all-start.2 = ((bf16[8,64,384]{2,1,0:T(8,128)(2,1)}), bf16[8,64,384]{2,1,0:T(8,128)(2,1)S(1)}, u32[]{:S(2)}, u32[]{:S(2)}) async-start(bf16[8,64,384]{2,1,0:T(8,128)(2,1)} %pad_maximum_fusion.2), calls=%async_computation.2 | async-start | bytes 786432 | tf_op jit(solution)/shard_map/all_to_all | solution.py:24
  57.4 8.0 %all-to-all-done.2 = bf16[8,64,384]{2,1,0:T(8,128)(2,1)S(1)} async-done(((bf16[8,64,384]{2,1,0:T(8,128)(2,1)}), bf16[8,64,384]{2,1,0:T(8,128)(2,1)S(1)}, u32[]{:S(2)}, u32[]{:S(2)}) %all-to-all-start.2) | async-done | bytes 393248 | tf_op jit(solution)/shard_map/all_to_all | solution.py:24
  65.6 0.8 broadcast_in_dim.112
  66.4 3.5 %all-to-all-start.3 = ((bf16[8,64,384]{2,1,0:T(8,128)(2,1)}), bf16[8,64,384]{2,1,0:T(8,128)(2,1)S(1)}, u32[]{:S(2)}, u32[]{:S(2)}) async-start(bf16[8,64,384]{2,1,0:T(8,128)(2,1)} %broadcast_in_dim.112), calls=%async_computation.3 | async-start | bytes 786432 | tf_op jit(solution)/shard_map/all_to_all | solution.py:24
  71.1 1.4 copy-done.2
  72.8 4.9 %all-to-all-done.3 = bf16[8,64,384]{2,1,0:T(8,128)(2,1)S(1)} async-done(((bf16[8,64,384]{2,1,0:T(8,128)(2,1)}), bf16[8,64,384]{2,1,0:T(8,128)(2,1)S(1)}, u32[]{:S(2)}, u32[]{:S(2)}) %all-to-all-start.3) | async-done | bytes 393248 | tf_op jit(solution)/shard_map/all_to_all | solution.py:24
  77.8 1.0 broadcast_in_dim.117
  78.8 4.5 %all-to-all-start.5 = ((bf16[32,16,768]{2,1,0:T(8,128)(2,1)}), bf16[32,16,768]{2,1,0:T(8,128)(2,1)S(1)}, u32[]{:S(2)}, u32[]{:S(2)}) async-start(bf16[32,16,768]{2,1,0:T(8,128)(2,1)} %broadcast_in_dim.117), calls=%async_computation.5 | async-start | bytes 1572864 | tf_op jit(solution)/shard_map/all_to_all | solution.py:24
  84.5 2.6 %convolution_convert_fusion.2 = bf16[1024,128]{1,0:T(8,128)(2,1)} fusion(bf16[1024,1024]{1,0:T(8,128)(2,1)S(1)} %bitcast.103, bf16[3,1024,128]{2,1,0:T(8,128)(2,1)} %param.16), kind=kOutput, calls=%fused_computation.59 | convolution fusion | flops 268566528 | bytes 2621440 | tf_op jit(solution)/shard_map/dot_general | solution.py:16
  87.1 0.7 fusion.121
  87.8 1.1 convolution_convert_fusion
  89.0 3.9 %collective-permute-start.1 = (bf16[256,768]{1,0:T(8,128)(2,1)}, bf16[256,768]{1,0:T(8,128)(2,1)}, u32[]{:S(2)}, u32[]{:S(2)}) collective-permute-start(bf16[256,768]{1,0:T(8,128)(2,1)} %convolution_convert_fusion), channel_id=1, source_target_pairs={{0,8},{8,0},{16,24},{24,16},{32,40},{40,32},{48,56},{56,48},{64,72... | collective-permute-start | bytes 1179656 | tf_op jit(solution)/shard_map/ppermute | solution.py:37
  93.5 9.6 %all-to-all-done.5 = bf16[32,16,768]{2,1,0:T(8,128)(2,1)S(1)} async-done(((bf16[32,16,768]{2,1,0:T(8,128)(2,1)}), bf16[32,16,768]{2,1,0:T(8,128)(2,1)S(1)}, u32[]{:S(2)}, u32[]{:S(2)}) %all-to-all-start.5) | async-done | bytes 786464 | tf_op jit(solution)/shard_map/all_to_all | solution.py:24
  103.1 7.2 %collective-permute-start.2 = (bf16[32,16,768]{2,1,0:T(8,128)(2,1)S(1)}, bf16[32,16,768]{2,1,0:T(8,128)(2,1)}, u32[]{:S(2)}, u32[]{:S(2)}) collective-permute-start(bf16[32,16,768]{2,1,0:T(8,128)(2,1)S(1)} %all-to-all-done.5), channel_id=1, source_target_pairs={{0,8},{8,0},{16,24},{24,16},{32,40},{40,32},{48,56},{56,48},{64,72... | collective-permute-start | bytes 2359304 | tf_op jit(solution)/shard_map/ppermute | solution.py:37
  110.3 0.7 select_compare_fusion.2
  111.0 2.2 %fusion.45 = bf16[32,8,768]{2,1,0:T(8,128)(2,1)} fusion(bf16[256,768]{1,0:T(8,128)(2,1)} %collective-permute-done.1, bf16[256,384]{1,0:T(8,128)(2,1)} %bitcast.106, bf16[384,768]{1,0:T(8,128)(2,1)S(1)} %copy-done), kind=kOutput, calls=%fused_computation.83 | convolution fusion | flops 151584768 | bytes 1572864 | tf_op jit(solution)/shard_map/dot_general | solution.py:16
  113.2 6.5 %all-to-all-start.4 = ((bf16[32,8,768]{2,1,0:T(8,128)(2,1)}), bf16[32,8,768]{2,1,0:T(8,128)(2,1)}, u32[]{:S(2)}, u32[]{:S(2)}) async-start(bf16[32,8,768]{2,1,0:T(8,128)(2,1)} %fusion.45), calls=%async_computation.4 | async-start | bytes 786432 | tf_op jit(solution)/shard_map/all_to_all | solution.py:24
  119.8 3.0 %convolution_convert_fusion.1 = bf16[1024,128]{1,0:T(8,128)(2,1)} fusion(bf16[1024,1024]{1,0:T(8,128)(2,1)} %bitcast.104, bf16[3,1024,128]{2,1,0:T(8,128)(2,1)} %param.16), kind=kOutput, calls=%fused_computation.58 | convolution fusion | flops 268566528 | bytes 2621440 | tf_op jit(solution)/shard_map/dot_general | solution.py:16
  122.8 1.2 select_bitcast_fusion.1
  124.1 1.3 pad_maximum_fusion
  125.4 9.3 %all-to-all-done.4 = bf16[32,8,768]{2,1,0:T(8,128)(2,1)} async-done(((bf16[32,8,768]{2,1,0:T(8,128)(2,1)}), bf16[32,8,768]{2,1,0:T(8,128)(2,1)}, u32[]{:S(2)}, u32[]{:S(2)}) %all-to-all-start.4) | async-done | bytes 393248 | tf_op jit(solution)/shard_map/all_to_all | solution.py:24
  134.7 1.1 convert_reduce_fusion.1
  135.8 1.1 constant_dynamic-update-slice_fusion.3
  137.4 1.2 fusion.77
  138.6 0.7 constant_dynamic-update-slice_fusion.2
  140.0 1.9 convolution_subtract_fusion
  141.9 0.7 broadcast_in_dim.118
  142.7 3.4 %all-to-all-start.6 = ((f32[8,8,1024]{2,1,0:T(8,128)}), f32[8,8,1024]{2,1,0:T(8,128)S(1)}, u32[]{:S(2)}, u32[]{:S(2)}) async-start(f32[8,8,1024]{2,1,0:T(8,128)} %broadcast_in_dim.118), calls=%async_computation.6 | async-start | bytes 524288 | tf_op jit(solution)/shard_map/all_to_all | solution.py:24
  147.3 2.7 %convolution_convert_fusion.5 = bf16[16,1024]{1,0:T(8,128)(2,1)} fusion(bf16[1024,1024]{1,0:T(8,128)(2,1)} %copy-done.2, f32[16,1024]{1,0:T(8,128)S(1)} %get-tuple-element.31, f32[16]{0:T(128)} %copy-done.20, f32[16]{0:T(128)} %copy-done.18), kind=kOutput, calls=%fused_computation.65 | convolution fusion | flops 33619968 | bytes 2195584 | tf_op jit(solution)/shard_map/dot_general | solution.py:16
  149.9 2.2 %all-to-all-done.6 = f32[8,8,1024]{2,1,0:T(8,128)S(1)} async-done(((f32[8,8,1024]{2,1,0:T(8,128)}), f32[8,8,1024]{2,1,0:T(8,128)S(1)}, u32[]{:S(2)}, u32[]{:S(2)}) %all-to-all-start.6) | async-done | bytes 262176 | tf_op jit(solution)/shard_map/all_to_all | solution.py:24
  152.2 0.6 reduce_sum.98
  152.8 1.3 fusion.41
  155.6 1.5 fusion.36
  157.3 26.6 %all_to_all.41 = bf16[32,8,1536]{2,1,0:T(8,128)(2,1)S(1)} all-to-all(bf16[32,8,1536]{2,1,0:T(8,128)(2,1)S(1)} %pad_maximum_fusion.1), channel_id=1, replica_groups={{0,16,32,48,64,80,96,112,128,144,160,176,192,208,224,240,256,272,288,30..., dimensions={0} | all-to-all | bytes 1572864 | tf_op jit(solution)/shard_map/all_to_all | solution.py:24
  184.0 7.1 %collective-permute-start.3 = (bf16[256,1536]{1,0:T(8,128)(2,1)S(1)}, bf16[256,1536]{1,0:T(8,128)(2,1)S(1)}, u32[]{:S(2)}, u32[]{:S(2)}) collective-permute-start(bf16[256,1536]{1,0:T(8,128)(2,1)S(1)} %bitcast.101), channel_id=1, source_target_pairs={{0,8},{8,0},{16,24},{24,16},{32,40},{40,32},{48,56},{56,48},{64,72... | collective-permute-start | bytes 2359304 | tf_op jit(solution)/shard_map/ppermute | solution.py:37
  191.4 1.6 collective-permute-done.3
  193.9 0.6 fusion.70
  194.5 0.6 pad_maximum_fusion.3
  (125 shorter events, 10.3 us)
Async XLA Ops:
  0.6 87.2 %copy-start = (bf16[384,768]{1,0:T(8,128)(2,1)S(1)}, bf16[384,768]{1,0:T(8,128)(2,1)}, u32[]{:S(2)}) copy-start(bf16[384,768]{1,0:T(8,128)(2,1)} %param.12) | copy-start | bytes 1769476
  0.6 50.8 %copy-start.4 = (bf16[768,384]{1,0:T(8,128)(2,1)S(1)}, bf16[768,384]{1,0:T(8,128)(2,1)}, u32[]{:S(2)}) copy-start(bf16[768,384]{1,0:T(8,128)(2,1)} %param.11) | copy-start | bytes 1769476
  2.2 11.7 %all-to-all-start = ((f32[8,8,2]{1,2,0:T(2,128)}), f32[8,8,2]{1,2,0:T(2,128)S(1)}, u32[]{:S(2)}, u32[]{:S(2)}) async-start(f32[8,8,2]{1,2,0:T(2,128)} %broadcast_in_dim.110), calls=%async_computation | async-start | bytes 16384 | tf_op jit(solution)/shard_map/all_to_all | solution.py:24
  42.5 9.4 %collective-permute-start = (bf16[256,768]{1,0:T(8,128)(2,1)S(1)}, bf16[256,768]{1,0:T(8,128)(2,1)S(1)}, u32[]{:S(2)}, u32[]{:S(2)}) collective-permute-start(bf16[256,768]{1,0:T(8,128)(2,1)S(1)} %bitcast.105), channel_id=1, source_target_pairs={{0,8},{8,0},{16,24},{24,16},{32,40},{40,32},{48,56},{56,48},{64,72... | collective-permute-start | bytes 1179656 | tf_op jit(solution)/shard_map/ppermute | solution.py:37
  51.5 5.1 %copy-start.33 = (s32[4,2]{0,1:T(2,128)S(1)}, s32[4,2]{0,1:T(2,128)}, u32[]{:S(2)}) copy-start(s32[4,2]{0,1:T(2,128)} %param.15) | copy-start | bytes 100
  51.9 18.6 %copy-start.1 = (bf16[4,256,1024]{2,1,0:T(8,128)(2,1)S(1)}, bf16[4,256,1024]{2,1,0:T(8,128)(2,1)}, u32[]{:S(2)}) copy-start(bf16[4,256,1024]{2,1,0:T(8,128)(2,1)} %param.14) | copy-start | bytes 6291460
  53.1 12.3 %all-to-all-start.2 = ((bf16[8,64,384]{2,1,0:T(8,128)(2,1)}), bf16[8,64,384]{2,1,0:T(8,128)(2,1)S(1)}, u32[]{:S(2)}, u32[]{:S(2)}) async-start(bf16[8,64,384]{2,1,0:T(8,128)(2,1)} %pad_maximum_fusion.2), calls=%async_computation.2 | async-start | bytes 786432 | tf_op jit(solution)/shard_map/all_to_all | solution.py:24
  57.4 13.7 %copy-start.30 = (s32[8]{0:T(128)}, s32[8]{0:T(128)S(1)}, u32[]{:S(2)}) copy-start(s32[8]{0:T(128)S(1)} %multiply_add_fusion) | copy-start | bytes 100
  66.4 11.3 %all-to-all-start.3 = ((bf16[8,64,384]{2,1,0:T(8,128)(2,1)}), bf16[8,64,384]{2,1,0:T(8,128)(2,1)S(1)}, u32[]{:S(2)}, u32[]{:S(2)}) async-start(bf16[8,64,384]{2,1,0:T(8,128)(2,1)} %broadcast_in_dim.112), calls=%async_computation.3 | async-start | bytes 786432 | tf_op jit(solution)/shard_map/all_to_all | solution.py:24
  71.1 1.4 copy-start.2
  72.4 5.4 %copy-start.15 = (bf16[768,16]{0,1:T(8,128)(2,1)S(1)}, bf16[768,16]{0,1:T(8,128)(2,1)}, u32[]{:S(2)}) copy-start(bf16[768,16]{0,1:T(8,128)(2,1)} %param.13) | copy-start | bytes 73732
  77.8 1.1 copy-start.6
  78.8 24.2 %all-to-all-start.5 = ((bf16[32,16,768]{2,1,0:T(8,128)(2,1)}), bf16[32,16,768]{2,1,0:T(8,128)(2,1)S(1)}, u32[]{:S(2)}, u32[]{:S(2)}) async-start(bf16[32,16,768]{2,1,0:T(8,128)(2,1)} %broadcast_in_dim.117), calls=%async_computation.5 | async-start | bytes 1572864 | tf_op jit(solution)/shard_map/all_to_all | solution.py:24
  84.5 4.5 %copy-start.5 = (bf16[4,256,1024]{2,1,0:T(8,128)(2,1)}, bf16[4,256,1024]{2,1,0:T(8,128)(2,1)S(1)}, u32[]{:S(2)}) copy-start(bf16[4,256,1024]{2,1,0:T(8,128)(2,1)S(1)} %fusion.2) | copy-start | bytes 6291460
  84.5 2.6 %copy-start.7 = (bf16[8,64,384]{2,1,0:T(8,128)(2,1)S(1)}, bf16[8,64,384]{2,1,0:T(8,128)(2,1)}, u32[]{:S(2)}) copy-start(bf16[8,64,384]{2,1,0:T(8,128)(2,1)} %copy-done.6) | copy-start | bytes 1179652
  89.0 22.0 %collective-permute-start.1 = (bf16[256,768]{1,0:T(8,128)(2,1)}, bf16[256,768]{1,0:T(8,128)(2,1)}, u32[]{:S(2)}, u32[]{:S(2)}) collective-permute-start(bf16[256,768]{1,0:T(8,128)(2,1)} %convolution_convert_fusion), channel_id=1, source_target_pairs={{0,8},{8,0},{16,24},{24,16},{32,40},{40,32},{48,56},{56,48},{64,72... | collective-permute-start | bytes 1179656 | tf_op jit(solution)/shard_map/ppermute | solution.py:37
  103.1 19.7 %collective-permute-start.2 = (bf16[32,16,768]{2,1,0:T(8,128)(2,1)S(1)}, bf16[32,16,768]{2,1,0:T(8,128)(2,1)}, u32[]{:S(2)}, u32[]{:S(2)}) collective-permute-start(bf16[32,16,768]{2,1,0:T(8,128)(2,1)S(1)} %all-to-all-done.5), channel_id=1, source_target_pairs={{0,8},{8,0},{16,24},{24,16},{32,40},{40,32},{48,56},{56,48},{64,72... | collective-permute-start | bytes 2359304 | tf_op jit(solution)/shard_map/ppermute | solution.py:37
  113.2 21.5 %all-to-all-start.4 = ((bf16[32,8,768]{2,1,0:T(8,128)(2,1)}), bf16[32,8,768]{2,1,0:T(8,128)(2,1)}, u32[]{:S(2)}, u32[]{:S(2)}) async-start(bf16[32,8,768]{2,1,0:T(8,128)(2,1)} %fusion.45), calls=%async_computation.4 | async-start | bytes 786432 | tf_op jit(solution)/shard_map/all_to_all | solution.py:24
  119.7 16.1 %copy-start.16 = (pred[128]{0:T(512)(128)(4,1)}, pred[128]{0:T(512)(128)(4,1)S(1)}, u32[]{:S(2)}) copy-start(pred[128]{0:T(512)(128)(4,1)S(1)} %get-tuple-element.36) | copy-start | bytes 388
  119.8 16.1 %copy-start.31 = (pred[128]{0:T(512)(128)(4,1)}, pred[128]{0:T(512)(128)(4,1)S(1)}, u32[]{:S(2)}) copy-start(pred[128]{0:T(512)(128)(4,1)S(1)} %get-tuple-element.35) | copy-start | bytes 388
  124.0 11.7 %copy-start.10 = (bf16[8,768]{1,0:T(8,128)(2,1)S(1)}, bf16[8,768]{1,0:T(8,128)(2,1)}, u32[]{:S(2)}) copy-start(bf16[8,768]{1,0:T(8,128)(2,1)} %param.9) | copy-start | bytes 36868
  124.0 12.9 %copy-start.9 = (bf16[1024,128]{1,0:T(8,128)(2,1)S(1)}, bf16[1024,128]{1,0:T(8,128)(2,1)}, u32[]{:S(2)}) copy-start(bf16[1024,128]{1,0:T(8,128)(2,1)} %convolution_convert_fusion.2) | copy-start | bytes 786436
  124.1 12.9 %copy-start.14 = (pred[8,1024]{1,0:T(8,128)(4,1)S(1)}, pred[8,1024]{1,0:T(8,128)(4,1)}, u32[]{:S(2)}) copy-start(pred[8,1024]{1,0:T(8,128)(4,1)} %select_compare_fusion.2) | copy-start | bytes 24580
  124.1 15.8 %copy-start.8 = (bf16[128,1024]{1,0:T(8,128)(2,1)S(1)}, bf16[128,1024]{1,0:T(8,128)(2,1)}, u32[]{:S(2)}) copy-start(bf16[128,1024]{1,0:T(8,128)(2,1)} %param.17) | copy-start | bytes 786436
  137.2 2.8 %copy-start.18 = (f32[16]{0:T(128)}, f32[16]{0:T(128)S(1)}, u32[]{:S(2)}) copy-start(f32[16]{0:T(128)S(1)} %get-tuple-element.30) | copy-start | bytes 196
  137.4 1.8 copy-start.20
  142.7 9.5 %all-to-all-start.6 = ((f32[8,8,1024]{2,1,0:T(8,128)}), f32[8,8,1024]{2,1,0:T(8,128)S(1)}, u32[]{:S(2)}, u32[]{:S(2)}) async-start(f32[8,8,1024]{2,1,0:T(8,128)} %broadcast_in_dim.118), calls=%async_computation.6 | async-start | bytes 524288 | tf_op jit(solution)/shard_map/all_to_all | solution.py:24
  152.8 1.4 copy-start.17
  152.8 1.4 copy-start.32
  152.8 1.7 copy-start.19
  152.8 1.7 copy-start.21
  152.8 1.7 copy-start.38
  152.8 2.2 %copy-start.3 = (bf16[1024,1024]{1,0:T(8,128)(2,1)S(1)}, bf16[1024,1024]{1,0:T(8,128)(2,1)}, u32[]{:S(2)}) copy-start(bf16[1024,1024]{1,0:T(8,128)(2,1)} %copy-done.2) | copy-start | bytes 6291460
  154.2 1.3 copy-start.13
  154.2 1.3 copy-start.22
  154.2 1.3 copy-start.23
  154.2 1.3 copy-start.24
  154.2 1.3 copy-start.25
  154.2 1.3 copy-start.26
  154.2 1.3 copy-start.27
  154.2 1.3 copy-start.28
  154.3 1.3 copy-start.29
  154.3 1.3 copy-start.34
  154.3 1.3 copy-start.35
  154.3 1.3 copy-start.36
  154.3 1.3 copy-start.37
  155.6 1.6 copy-start.12
  184.0 9.0 %collective-permute-start.3 = (bf16[256,1536]{1,0:T(8,128)(2,1)S(1)}, bf16[256,1536]{1,0:T(8,128)(2,1)S(1)}, u32[]{:S(2)}, u32[]{:S(2)}) collective-permute-start(bf16[256,1536]{1,0:T(8,128)(2,1)S(1)} %bitcast.101), channel_id=1, source_target_pairs={{0,8},{8,0},{16,24},{24,16},{32,40},{40,32},{48,56},{56,48},{64,72... | collective-permute-start | bytes 2359304 | tf_op jit(solution)/shard_map/ppermute | solution.py:37
  (1 other events, 0.6 us)

commit v3 on v2

v3 whole, which is shorter than its diff:
```python
import functools

import jax
import jax.numpy as jnp
import numpy as np
from jax import lax
from jax.experimental import pallas as pl
from jax.experimental.pallas import tpu as pltpu
from jax.sharding import PartitionSpec as P

HEAD_DIM = 64
LANES = 128
EPSILON = 1e-06
CORES = 2

f32 = jnp.float32
bf16 = jnp.bfloat16


def product(left, right, dims=((1,), (0,))):
    return lax.dot_general(left, right, (dims, ((), ())), preferred_element_type=f32)


def chip_groups(wide, cores):
    return [[chip * cores + c for chip in range(wide // cores)] for c in range(cores)]


def exchange(block, axis, groups=None):
    return lax.all_to_all(block, axis, 0, 0, axis_index_groups=groups)


def spread(block, axis, count, groups=None):
    return exchange(jnp.broadcast_to(block[None], (count,) + block.shape), axis, groups)


def by_head(block, heads):
    lane_head = lax.broadcasted_iota(jnp.int32, block.shape, 1) // HEAD_DIM
    return jnp.concatenate([jnp.where(lane_head == h, block, 0.0) for h in range(heads)], axis=0)


def merge_heads(block, heads):
    picks = block.shape[0] // heads
    merged = block[:picks]
    lane_head = lax.broadcasted_iota(jnp.int32, merged.shape, 1) // HEAD_DIM
    for h in range(1, heads):
        merged = jnp.where(lane_head == h, block[h * picks : (h + 1) * picks], merged)
    return merged


def rounded(block):
    return block.astype(bf16).astype(f32)


def forward_kernel(
    patches,
    wanted_ref,
    first_ref,
    student_ref,
    w_qkv_ref,
    w_out_ref,
    norm_ref,
    keys_ref,
    values_ref,
    probs_ref,
    side_ref,
    early_ref,
    picked_norm_ref,
    picked_in_ref,
    mixed_ref,
):
    total, width = student_ref.shape
    heads = keys_ref.shape[1] // HEAD_DIM
    for start in range(0, total, patches):
        at = pl.ds(start, patches)
        source = student_ref[at, :].astype(f32)
        center = jnp.mean(source, axis=1, keepdims=True)
        spread_s = jnp.mean(source * source, axis=1, keepdims=True) - center * center
        norm = ((source - center) * lax.rsqrt(spread_s + EPSILON)).astype(bf16)
        norm_ref[at, :] = norm
        keys_ref[at, :] = product(norm, w_qkv_ref[1]).astype(bf16)
        values_ref[at, :] = product(norm, w_qkv_ref[2]).astype(bf16)
    norm = norm_ref[...]
    picks = wanted_ref.shape[0]
    column = lax.broadcasted_iota(jnp.int32, (picks, total), 1)
    chosen = jnp.where(column == wanted_ref[...], 1.0, 0.0).astype(bf16)
    picked_norm = product(chosen, norm)
    picked_norm_ref[...] = picked_norm
    picked_in_ref[...] = product(chosen, student_ref[...])
    queries = product(picked_norm.astype(bf16), w_qkv_ref[0])
    scores = product(by_head(queries, heads).astype(bf16), keys_ref[...], ((1,), (1,)))
    column = lax.broadcasted_iota(jnp.int32, scores.shape, 1)
    first = first_ref[...]
    inside = (column >= first) & (column < first + patches)
    scores = jnp.where(inside, scores * HEAD_DIM ** (-0.5), -jnp.inf)
    top = jnp.max(scores, axis=1, keepdims=True)
    powers = jnp.where(inside, jnp.exp(scores - top), 0.0)
    probs = powers / jnp.sum(powers, axis=1, keepdims=True)
    probs_ref[...] = probs
    probs_low = probs.astype(bf16)
    context = merge_heads(product(probs_low, values_ref[...]), heads)
    side_ref[...] = product(probs_low, norm)
    early_ref[...] = jnp.concatenate([queries, context], axis=1)
    mixed_ref[...] = product(context.astype(bf16), w_out_ref[...])


def backward_kernel(
    divisor,
    terms_ref,
    picked_in_ref,
    probs_ref,
    keys_ref,
    values_ref,
    norm_ref,
    w_out_ref,
    picked_norm_ref,
    side_ref,
    early_ref,
    teacher_ref,
    move_ref,
    send_ref,
):
    picks, width = picked_in_ref.shape
    local_width = keys_ref.shape[1]
    heads = local_width // HEAD_DIM
    delta = (picked_in_ref[...] + jnp.sum(terms_ref[...], axis=0)) / divisor
    d_context = product(delta.astype(bf16), w_out_ref[...], ((1,), (1,)))
    d_probs = product(by_head(d_context, heads).astype(bf16), values_ref[...], ((1,), (1,)))
    probs = probs_ref[...]
    held = jnp.sum(probs * d_probs, axis=1, keepdims=True)
    d_scores = (probs * (d_probs - held) * HEAD_DIM ** (-0.5)).astype(bf16)
    d_query = merge_heads(product(d_scores, keys_ref[...]), heads)
    key_side = product(d_scores, norm_ref[...])
    shared = jnp.concatenate(
        [teacher_ref[...].astype(f32), early_ref[...], d_query, d_context], axis=1
    )
    shared_width = shared.shape[1]
    twice = jnp.concatenate([shared, shared], axis=0).astype(bf16)
    for start in range(0, send_ref.shape[0], 2 * picks):
        send_ref[pl.ds(start, 2 * picks), pl.ds(0, shared_width)] = twice

    side = side_ref[...]
    factors = [delta, picked_norm_ref[...]]
    factors += [key_side[h * picks : (h + 1) * picks] for h in range(heads)]
    factors += [side[h * picks : (h + 1) * picks] for h in range(heads)]
    lines = [
        jnp.concatenate([factor[:, at : at + LANES] for factor in factors], axis=1)
        for at in range(0, width, LANES)
    ]
    packed = product(jnp.concatenate(lines, axis=0).astype(bf16), move_ref[...])
    per_tile = packed.shape[1] // LANES
    chips_per_tile = per_tile // CORES
    for chip in range(0, send_ref.shape[0] // picks, 2):
        tile, place = chip // chips_per_tile, chip % chips_per_tile
        for core in range(CORES):
            pieces = []
            for spot in (place, place + 1):
                lane = (spot * CORES + core) * LANES
                pieces.append(packed[tile * picks : (tile + 1) * picks, lane : lane + LANES])
            send_ref[
                pl.ds(chip * picks, 2 * picks), pl.ds(shared_width + core * LANES, LANES)
            ] = jnp.concatenate(pieces, axis=0).astype(bf16)


def call_kernel(kernel, out_shape, flops, *operands):
    whole = pl.BlockSpec(memory_space=pltpu.VMEM)
    moved = sum(x.size * x.dtype.itemsize for x in operands)
    return pl.pallas_call(
        kernel,
        out_shape=out_shape,
        in_specs=[whole] * len(operands),
        out_specs=jax.tree.map(lambda _: whole, out_shape),
        compiler_params=pltpu.CompilerParams(vmem_limit_bytes=40 * 2**20),
        cost_estimate=pl.CostEstimate(flops=flops, bytes_accessed=moved, transcendentals=0),
    )(*operands)


def lane_moves(kinds, piece):
    per_tile = LANES // piece
    move = np.zeros((kinds, LANES, per_tile, LANES), np.float32)
    for kind in range(kinds):
        for tile in range(per_tile):
            for lane in range(piece):
                move[kind, tile * piece + lane, tile, kind * piece + lane] = 1.0
    return move.reshape(kinds * LANES, per_tile * LANES)


def make_local(wide, narrow):
    chips = wide // CORES
    groups = chip_groups(wide, CORES)
    pairs = [(i, i ^ 1) for i in range(wide)]

    def swap(block):
        return lax.ppermute(block, "wide", pairs)

    def doubled(blocks, bit):
        other = lax.ppermute(blocks, "wide", [(i, i ^ bit) for i in range(wide)])
        mine = (lax.axis_index("wide") & bit != 0).astype(jnp.int32)
        place = lax.broadcasted_iota(jnp.int32, (1, 2) + blocks.shape[1:], 1)
        both = jnp.where(place == mine, blocks[:, None], other[:, None])
        return both.reshape((-1,) + blocks.shape[1:])

    bits = []
    while 2 ** len(bits) < wide:
        bits.insert(0, 2 ** len(bits))

    def local(
        teacher_in,
        teacher_gain,
        mlp_in,
        mlp_out,
        projector,
        student_in,
        sample_pos,
        w_qkv,
        w_attn_out,
    ):
        rows, features = teacher_in.shape
        d_t = features * narrow
        images, patches, width = student_in.shape
        select = sample_pos.shape[1]
        local_width = w_qkv.shape[2]
        half = rows * chips
        first_core = lax.axis_index("wide") % CORES == 0
        heads_here = local_width // HEAD_DIM
        picks = images * select

        image_first = np.repeat(np.arange(images, dtype=np.int32) * patches, select)[:, None]
        flat_in = student_in.reshape(images * patches, width)
        norm_shape = jax.ShapeDtypeStruct(flat_in.shape, bf16)
        head_shape = jax.ShapeDtypeStruct((flat_in.shape[0], local_width), bf16)
        score_shape = jax.ShapeDtypeStruct((heads_here * picks, flat_in.shape[0]), f32)
        side_shape = jax.ShapeDtypeStruct((heads_here * picks, width), f32)
        early_shape = jax.ShapeDtypeStruct((picks, 2 * local_width), f32)
        row_shape = jax.ShapeDtypeStruct((picks, width), f32)
        student = call_kernel(
            functools.partial(forward_kernel, patches),
            [norm_shape, head_shape, head_shape, score_shape, side_shape, early_shape]
            + [row_shape] * 3,
            2 * flat_in.size * (2 * local_width + 4 * picks),
            sample_pos.reshape(picks, 1) + image_first,
            jnp.asarray(np.tile(image_first, (heads_here, 1))),
            flat_in,
            w_qkv,
            w_attn_out,
        )

        own = teacher_in.astype(f32)
        sums = jnp.concatenate(
            [
                jnp.sum(own, axis=1, keepdims=True),
                jnp.sum(own * own, axis=1, keepdims=True),
            ],
            axis=1,
        )
        sums = jnp.sum(spread(sums, "narrow", narrow), axis=0)
        center = sums[:, 0:1] / d_t
        variance = sums[:, 1:2] / d_t - center * center
        normed = (
            (own - center) * lax.rsqrt(variance + EPSILON) * teacher_gain.astype(f32)
        ).astype(bf16)
        normed = spread(normed, "wide", chips, groups).reshape(half, features)
        columns = projector.T[None]
        for bit in bits[:-3]:
            columns = doubled(columns, bit)
        normed, columns, student = lax.optimization_barrier((normed, columns, student))
        norm, keys, values, probs, side, early, picked_norm, picked_in, mixed = student
        normed_other = swap(normed)

        pre = jnp.concatenate(
            [
                product(block, mlp_in).astype(bf16).reshape(narrow, half // narrow, -1)
                for block in (normed, normed_other)
            ],
            axis=1,
        )
        pre = exchange(pre, "narrow")
        columns = doubled(columns, bits[-3])
        pre, columns = lax.optimization_barrier((pre, columns))
        pre = jnp.sum(pre.astype(f32), axis=0)
        hidden = jax.nn.gelu(pre, approximate=False).astype(bf16)
        hidden = spread(hidden, "narrow", narrow)
        columns = doubled(columns, bits[-2])
        hidden, columns = lax.optimization_barrier((hidden, columns))
        hidden_own = hidden[:, : half // narrow].reshape(half, -1)
        hidden_other = hidden[:, half // narrow :].reshape(half, -1)
        branch = swap(product(hidden_other, mlp_out).astype(bf16))
        branch = (product(hidden_own, mlp_out) + branch.astype(f32)).astype(bf16)
        branch = exchange(branch.reshape(chips, rows, features), "wide", groups)
        teacher_local = (own + jnp.sum(branch.astype(f32), axis=0)).astype(bf16)

        columns = doubled(columns, bits[-1]).reshape(-1, features)
        target = product(teacher_local, columns, ((1,), (1,)))
        terms = spread(mixed - target, "narrow", narrow)

        piece = width // wide
        kinds = 2 + 2 * heads_here
        shared_width = features + 4 * local_width
        got = call_kernel(
            functools.partial(backward_kernel, float(select * images)),
            jax.ShapeDtypeStruct((half, shared_width + CORES * LANES), bf16),
            2 * norm.size * heads_here * picks,
            terms,
            picked_in,
            probs,
            keys,
            values,
            norm,
            w_attn_out,
            picked_norm,
            side,
            early,
            teacher_local,
            jnp.asarray(lane_moves(kinds, piece), bf16),
        )
        got = exchange(got.reshape(chips, rows, -1), "wide", groups).reshape(half, -1)
        got_other = swap(got)

        def rows_product(block):
            ours = jnp.where(
                first_core,
                block[:, shared_width : shared_width + LANES],
                block[:, shared_width + LANES :],
            )
            return product(ours, block[:, :shared_width], ((0,), (0,)))

        full = rows_product(got) + rows_product(got_other)

        def part(kind, start, size):
            return full[kind * piece : (kind + 1) * piece, start : start + size]

        at_query = features
        at_context = at_query + local_width
        at_d_query = at_context + local_width
        at_d_context = at_d_query + local_width
        grad_projector = -part(0, 0, features).T
        grad_attn_out = part(0, at_context, local_width).T
        grad_query = part(1, at_d_query, local_width)
        grad_key = part(2, at_query, local_width)
        grad_value = part(2 + heads_here, at_d_context, local_width)
        for h in range(1, heads_here):
            here = lax.broadcasted_iota(jnp.int32, grad_key.shape, 1) // HEAD_DIM == h
            grad_key = jnp.where(here, part(2 + h, at_query, local_width), grad_key)
            grad_value = jnp.where(
                here, part(2 + heads_here + h, at_d_context, local_width), grad_value
            )
        return (jnp.stack([grad_query, grad_key, grad_value]), grad_attn_out, grad_projector)

    return local


def solution(mesh):
    placed = (
        P("wide", "narrow"),
        P("narrow"),
        P("narrow", "wide"),
        P("wide", "narrow"),
        P("narrow", "wide"),
        P("wide", None, None),
        P("wide", None),
        P(None, None, "narrow"),
        P("narrow", None),
    )
    return jax.shard_map(
        make_local(mesh.shape["wide"], mesh.shape["narrow"]),
        mesh=mesh,
        in_specs=placed,
        out_specs=(P(None, "wide", "narrow"), P("narrow", "wide"), P("narrow", "wide")),
        check_vma=False,
    )
```

time: 197 us -> 203 us (1.030)
  starting transfers between devices: 52.9 us -> 74.4 us
  blocking collectives: 54.3 us -> 37.1 us
  matrix products: 21.8 us -> 6.93 us
  waiting for transfers between devices: 40 us -> 47.1 us
  local copies, waits for them, and re-layouts: 6.37 us -> 11.2 us
  Pallas kernels: 0 us -> 4.3 us
    ppermute x0 -> x6, waiting for transfers between devices: none -> 30.6 us  [doubled(): other = lax.ppermute(blocks, 'wide', [(i, i ^ bit) for i in range(wide)])]
    all_to_all x6 -> x5, waiting for transfers between devices: 38.4 us -> 14.9 us  [exchange(): return lax.all_to_all(block, axis, 0, 0, axis_index_groups=groups)]
    ppermute x0 -> x6, starting transfers between devices: none -> 22.9 us  [doubled(): other = lax.ppermute(blocks, 'wide', [(i, i ^ bit) for i in range(wide)])]
    all_to_all x2, blocking collectives: 54.3 us -> 37.1 us  [exchange(): return lax.all_to_all(block, axis, 0, 0, axis_index_groups=groups)]
    dot_general x21 -> x7, matrix products: 21.8 us -> 6.93 us  [product(): lax.dot_general(left, right, (dims, ((), ())), preferred_element_type=f32)]
    select_n x1 -> x6, other arithmetic: 0.01 us -> 9.95 us  [doubled(): both = jnp.where(place == mine, blocks[:, None], other[:, None])]
    ppermute x4 -> x3, starting transfers between devices: 24.9 us -> 16.4 us  [swap(): return lax.ppermute(block, 'wide', pairs)]
    all_to_all x6 -> x5, starting transfers between devices: 28 us -> 35.2 us  [exchange(): return lax.all_to_all(block, axis, 0, 0, axis_index_groups=groups)]
  transfers between devices with their start and end apart: 10 -> 14, of which waited for: 7 -> 7; matrix products, arithmetic and copies ran while one was open for 13% -> 8% of each run, Pallas kernels for 0% -> 2%
where the time goes in v3:
time: 203 us; the launch traced here: 200 us
  starting transfers between devices  74.4 us (37%)
  waiting for transfers between devices  47.1 us (23%)
  blocking collectives  37.1 us (18%)
  other arithmetic  18.3 us (9%)
  local copies, waits for them, and re-layouts  11.2 us (6%)
  matrix products  6.93 us (3%)
  Pallas kernels  4.3 us (2%)
    all_to_all x2, blocking collectives, exchange(): return lax.all_to_all(block, axis, 0, 0, axis_index_groups=groups)  37.1 us
    all_to_all x5, starting transfers between devices, exchange(): return lax.all_to_all(block, axis, 0, 0, axis_index_groups=groups)  35.2 us
    ppermute x6, waiting for transfers between devices, doubled(): other = lax.ppermute(blocks, 'wide', [(i, i ^ bit) for i in range(wide)])  30.6 us
    ppermute x6, starting transfers between devices, doubled(): other = lax.ppermute(blocks, 'wide', [(i, i ^ bit) for i in range(wide)])  22.9 us
    ppermute x3, starting transfers between devices, swap(): return lax.ppermute(block, 'wide', pairs)  16.4 us
    all_to_all x5, waiting for transfers between devices, exchange(): return lax.all_to_all(block, axis, 0, 0, axis_index_groups=groups)  14.9 us
    select_n x6, other arithmetic, doubled(): both = jnp.where(place == mine, blocks[:, None], other[:, None])  9.95 us
    dot_general x7, matrix products, product(): lax.dot_general(left, right, (dims, ((), ())), preferred_element_type=f32)  6.93 us
  transfers between devices with their start and end apart: 14, of which 7 were waited for; matrix products, arithmetic and copies ran while one was open for 8% of the time, Pallas kernels for 2%

profile of v3, /device:TPU:1, one launch (start us, length us, event | category | flops | bytes accessed | tf_op | source)
XLA Modules:
  0.0 200.4 jit_solution(17733148312221020592)
XLA Ops:
  0.7 0.9 convert_reduce_fusion.2
  2.2 6.7 %all-to-all-start = ((f32[8,8,2]{1,2,0:T(2,128)}), f32[8,8,2]{1,2,0:T(2,128)S(1)}, u32[]{:S(2)}, u32[]{:S(2)}) async-start(f32[8,8,2]{1,2,0:T(2,128)} %broadcast_in_dim.223), calls=%async_computation | async-start | bytes 16384 | tf_op jit(solution)/shard_map/all_to_all | solution.py:29
  9.6 4.4 %all-to-all-done = f32[8,8,2]{1,2,0:T(2,128)S(1)} async-done(((f32[8,8,2]{1,2,0:T(2,128)}), f32[8,8,2]{1,2,0:T(2,128)S(1)}, u32[]{:S(2)}, u32[]{:S(2)}) %all-to-all-start) | async-done | bytes 544 | tf_op jit(solution)/shard_map/all_to_all | solution.py:29
  14.0 0.8 fusion.22
  14.7 0.8 broadcast_in_dim.224
  15.5 14.9 %all-to-all-start.1 = ((bf16[32,8,768]{2,1,0:T(8,128)(2,1)}), bf16[32,8,768]{2,1,0:T(8,128)(2,1)}, u32[]{:S(2)}, u32[]{:S(2)}) async-start(bf16[32,8,768]{2,1,0:T(8,128)(2,1)} %broadcast_in_dim.224), calls=%async_computation.1 | async-start | bytes 786432 | tf_op jit(solution)/shard_map/all_to_all | solution.py:29
  30.4 7.0 %collective-permute-start = (bf16[1,16,768]{2,1,0:T(8,128)(2,1)}, bf16[1,16,768]{2,1,0:T(8,128)(2,1)S(1)}, u32[]{:S(2)}, u32[]{:S(2)}) collective-permute-start(bf16[1,16,768]{2,1,0:T(8,128)(2,1)} %bitcast.68), channel_id=1, source_target_pairs={{0,256},{8,264},{16,272},{24,280},{32,288},{40,296},{48,304},{56,3... | collective-permute-start | bytes 73736 | tf_op jit(solution)/shard_map/ppermute | solution.py:196
  37.4 7.8 %collective-permute-done = bf16[1,16,768]{2,1,0:T(8,128)(2,1)S(1)} collective-permute-done((bf16[1,16,768]{2,1,0:T(8,128)(2,1)}, bf16[1,16,768]{2,1,0:T(8,128)(2,1)S(1)}, u32[]{:S(2)}, u32[]{:S(2)}) %collective-permute-start) | collective-permute-done | bytes 24608 | tf_op jit(solution)/shard_map/ppermute | solution.py:196
  45.2 0.8 broadcast_select_fusion
  46.0 3.8 %collective-permute-start.1 = (bf16[2,16,768]{2,1,0:T(8,128)(2,1)S(1)}, bf16[2,16,768]{2,1,0:T(8,128)(2,1)S(1)}, u32[]{:S(2)}, u32[]{:S(2)}) collective-permute-start(bf16[2,16,768]{2,1,0:T(8,128)(2,1)S(1)} %broadcast_select_fusion), channel_id=1, source_target_pairs={{0,128},{8,136},{16,144},{24,152},{32,160},{40,168},{48,176},{56,1... | collective-permute-start | bytes 147464 | tf_op jit(solution)/shard_map/ppermute | solution.py:196
  50.0 1.8 collective-permute-done.1
  51.8 0.7 bitcast_select_fusion.4
  52.5 6.3 %collective-permute-start.2 = (bf16[4,16,768]{2,1,0:T(8,128)(2,1)}, bf16[4,16,768]{2,1,0:T(8,128)(2,1)}, u32[]{:S(2)}, u32[]{:S(2)}) collective-permute-start(bf16[4,16,768]{2,1,0:T(8,128)(2,1)} %bitcast_select_fusion.4), channel_id=1, source_target_pairs={{0,64},{8,72},{16,80},{24,88},{32,96},{40,104},{48,112},{56,120},{... | collective-permute-start | bytes 294920 | tf_op jit(solution)/shard_map/ppermute | solution.py:196
  59.1 1.6 copy-done.1
  60.7 1.1 copy-done.4
  61.9 0.7 copy-done.12
  62.6 3.1 %shard_map.139 = (bf16[1024,1024]{1,0:T(8,128)(2,1)S(1)}, bf16[1024,128]{1,0:T(8,128)(2,1)S(1)}, bf16[1024,128]{1,0:T(8,128)(2,1)S(1)}, f32[16,1024]{1,0:T(8,128...) custom-call(s32[8,1]{1,0:T(8,128)S(1)} %reshape.182.wanted_ref, ...), custom_call_target="tpu_custom_call" | custom-call | flops 603979776 | bytes 3145824 | tf_op jit(solution)/shard_map/pallas_call | solution.py:167
  68.1 1.7 bitcast_select_fusion.3
  69.8 5.1 %collective-permute-start.3 = (bf16[256,768]{1,0:T(8,128)(2,1)}, bf16[256,768]{1,0:T(8,128)(2,1)S(1)}, u32[]{:S(2)}, u32[]{:S(2)}) collective-permute-start(bf16[256,768]{1,0:T(8,128)(2,1)} %bitcast.4), channel_id=1, source_target_pairs={{0,8},{8,0},{16,24},{24,16},{32,40},{40,32},{48,56},{56,48},{64,72... | collective-permute-start | bytes 1179656 | tf_op jit(solution)/shard_map/ppermute | solution.py:193
  74.8 1.6 convolution_convert_fusion.2
  76.4 1.4 convolution_convert_fusion.1
  77.8 0.8 pad_maximum_fusion
  78.6 4.1 %all-to-all-start.2 = ((bf16[8,64,384]{2,1,0:T(8,128)(2,1)}), bf16[8,64,384]{2,1,0:T(8,128)(2,1)}, u32[]{:S(2)}, u32[]{:S(2)}) async-start(bf16[8,64,384]{2,1,0:T(8,128)(2,1)} %pad_maximum_fusion), calls=%async_computation.2 | async-start | bytes 786432 | tf_op jit(solution)/shard_map/all_to_all | solution.py:29
  82.7 1.9 collective-permute-start.4
  84.8 11.5 %collective-permute-done.4 = bf16[8,16,768]{2,1,0:T(8,128)(2,1)} collective-permute-done((bf16[8,16,768]{2,1,0:T(8,128)(2,1)}, bf16[8,16,768]{2,1,0:T(8,128)(2,1)}, u32[]{:S(2)}, u32[]{:S(2)}) %collective-permute-start.4) | collective-permute-done | bytes 196640 | tf_op jit(solution)/shard_map/ppermute | solution.py:196
  96.3 1.9 bitcast_select_fusion.2
  98.2 1.1 convert_reduce_fusion.1
  99.5 0.8 broadcast_in_dim.250
  100.3 5.0 %all-to-all-start.3 = ((bf16[8,64,384]{2,1,0:T(8,128)(2,1)}), bf16[8,64,384]{2,1,0:T(8,128)(2,1)}, u32[]{:S(2)}, u32[]{:S(2)}) async-start(bf16[8,64,384]{2,1,0:T(8,128)(2,1)} %broadcast_in_dim.250), calls=%async_computation.3 | async-start | bytes 786432 | tf_op jit(solution)/shard_map/all_to_all | solution.py:29
  105.3 1.9 collective-permute-start.5
  107.3 9.4 %collective-permute-done.5 = bf16[16,16,768]{2,1,0:T(8,128)(2,1)} collective-permute-done((bf16[16,16,768]{2,1,0:T(8,128)(2,1)}, bf16[16,16,768]{2,1,0:T(8,128)(2,1)}, u32[]{:S(2)}, u32[]{:S(2)}) %collective-permute-start.5) | collective-permute-done | bytes 393248 | tf_op jit(solution)/shard_map/ppermute | solution.py:196
  116.7 2.1 %bitcast_select_fusion.1 = bf16[32,16,768]{2,1,0:T(8,128)(2,1)} fusion(pred[32]{0:T(512)(128)(4,1)S(1)} %broadcast_in_dim.252, bf16[16,16,768]{2,1,0:T(8,128)(2,1)} %collective-permute-done.5, bf16[16,16,768]{2,1,0:T(8,128)(2,1)} %bitcast_select_fusion.2), kind=kLoop, calls=%fused_computation.6 | loop fusion | flops 393216 | bytes 1572896 | tf_op jit(solution)/shard_map/jit(_where)/select_n | solution.py:199
  118.8 1.1 fusion.27
  120.3 4.2 %collective-permute-start.6 = (bf16[256,768]{1,0:T(8,128)(2,1)S(1)}, bf16[256,768]{1,0:T(8,128)(2,1)S(1)}, u32[]{:S(2)}, u32[]{:S(2)}) collective-permute-start(bf16[256,768]{1,0:T(8,128)(2,1)S(1)} %convolution_convert_fusion), channel_id=1, source_target_pairs={{0,8},{8,0},{16,24},{24,16},{32,40},{40,32},{48,56},{56,48},{64,72... | collective-permute-start | bytes 1179656 | tf_op jit(solution)/shard_map/ppermute | solution.py:193
  124.5 1.9 collective-permute-start.7
  126.4 1.1 fusion.3
  127.6 4.6 %all-to-all-start.4 = ((bf16[32,8,768]{2,1,0:T(8,128)(2,1)}), bf16[32,8,768]{2,1,0:T(8,128)(2,1)}, u32[]{:S(2)}, u32[]{:S(2)}) async-start(bf16[32,8,768]{2,1,0:T(8,128)(2,1)} %fusion.3), calls=%async_computation.4 | async-start | bytes 786432 | tf_op jit(solution)/shard_map/all_to_all | solution.py:29
  132.9 0.8 broadcast_in_dim.259
  133.7 2.7 %bitcast_select_fusion = bf16[1024,768]{1,0:T(8,128)(2,1)} fusion(pred[1024]{0:T(1024)(128)(4,1)S(1)} %broadcast_in_dim.259, bf16[32,16,768]{2,1,0:T(8,128)(2,1)} %collective-permute-done.7, bf16[32,16,768]{2,1,0:T(8,128)(2,1)} %bitcast_select_fusion.1), kind=kLoop, calls=%fused_computation.1 | loop fusion | flops 786432 | bytes 3146752 | tf_op jit(solution)/shard_map/jit(_where)/select_n | solution.py:199
  136.4 10.6 %all-to-all-done.4 = bf16[32,8,768]{2,1,0:T(8,128)(2,1)} async-done(((bf16[32,8,768]{2,1,0:T(8,128)(2,1)}), bf16[32,8,768]{2,1,0:T(8,128)(2,1)}, u32[]{:S(2)}, u32[]{:S(2)}) %all-to-all-start.4) | async-done | bytes 393248 | tf_op jit(solution)/shard_map/all_to_all | solution.py:29
  147.0 1.2 convert_reduce_fusion
  148.2 0.7 fusion.23.teacher_ref
  148.9 1.9 convolution_subtract_fusion
  150.8 11.0 %all_to_all.35.terms_ref = f32[8,8,1024]{2,1,0:T(8,128)S(1)} all-to-all(f32[8,8,1024]{2,1,0:T(8,128)S(1)} %broadcast_in_dim.265), channel_id=1, replica_groups=mesh['wide'=64,'narrow'=8] {'narrow'}, dimensions={0} | all-to-all | bytes 524288 | tf_op jit(solution)/shard_map/all_to_all | solution.py:29
  161.9 1.2 shard_map.140
  163.1 26.2 %all_to_all.36 = bf16[32,8,1536]{2,1,0:T(8,128)(2,1)S(1)} all-to-all(bf16[32,8,1536]{2,1,0:T(8,128)(2,1)S(1)} %bitcast.60), channel_id=1, replica_groups={{0,16,32,48,64,80,96,112,128,144,160,176,192,208,224,240,256,272,288,30..., dimensions={0} | all-to-all | bytes 1572864 | tf_op jit(solution)/shard_map/all_to_all | solution.py:29
  189.3 7.1 %collective-permute-start.8 = (bf16[256,1536]{1,0:T(8,128)(2,1)S(1)}, bf16[256,1536]{1,0:T(8,128)(2,1)S(1)}, u32[]{:S(2)}, u32[]{:S(2)}) collective-permute-start(bf16[256,1536]{1,0:T(8,128)(2,1)S(1)} %bitcast.62), channel_id=1, source_target_pairs={{0,8},{8,0},{16,24},{24,16},{32,40},{40,32},{48,56},{56,48},{64,72... | collective-permute-start | bytes 2359304 | tf_op jit(solution)/shard_map/ppermute | solution.py:193
  196.7 1.6 collective-permute-done.8
  (67 shorter events, 8.1 us)
Async XLA Ops:
  0.6 119.3 %copy-start = (bf16[384,768]{1,0:T(8,128)(2,1)S(1)}, bf16[384,768]{1,0:T(8,128)(2,1)}, u32[]{:S(2)}) copy-start(bf16[384,768]{1,0:T(8,128)(2,1)} %param.15) | copy-start | bytes 1769476
  0.6 58.3 %copy-start.14 = (s32[4,2]{0,1:T(2,128)S(1)}, s32[4,2]{0,1:T(2,128)}, u32[]{:S(2)}) copy-start(s32[4,2]{0,1:T(2,128)} %constant.128) | copy-start | bytes 100
  0.7 58.3 %copy-start.13 = (s32[4,2]{0,1:T(2,128)S(1)}, s32[4,2]{0,1:T(2,128)}, u32[]{:S(2)}) copy-start(s32[4,2]{0,1:T(2,128)} %param.18) | copy-start | bytes 100
  0.7 58.5 %copy-start.3 = (bf16[128,1024]{1,0:T(8,128)(2,1)S(1)}, bf16[128,1024]{1,0:T(8,128)(2,1)}, u32[]{:S(2)}) copy-start(bf16[128,1024]{1,0:T(8,128)(2,1)} %w_out_ref.3) | copy-start | bytes 786436
  2.2 11.7 %all-to-all-start = ((f32[8,8,2]{1,2,0:T(2,128)}), f32[8,8,2]{1,2,0:T(2,128)S(1)}, u32[]{:S(2)}, u32[]{:S(2)}) async-start(f32[8,8,2]{1,2,0:T(2,128)} %broadcast_in_dim.223), calls=%async_computation | async-start | bytes 16384 | tf_op jit(solution)/shard_map/all_to_all | solution.py:29
  15.5 54.3 %all-to-all-start.1 = ((bf16[32,8,768]{2,1,0:T(8,128)(2,1)}), bf16[32,8,768]{2,1,0:T(8,128)(2,1)}, u32[]{:S(2)}, u32[]{:S(2)}) async-start(bf16[32,8,768]{2,1,0:T(8,128)(2,1)} %broadcast_in_dim.224), calls=%async_computation.1 | async-start | bytes 786432 | tf_op jit(solution)/shard_map/all_to_all | solution.py:29
  30.4 14.8 %collective-permute-start = (bf16[1,16,768]{2,1,0:T(8,128)(2,1)}, bf16[1,16,768]{2,1,0:T(8,128)(2,1)S(1)}, u32[]{:S(2)}, u32[]{:S(2)}) collective-permute-start(bf16[1,16,768]{2,1,0:T(8,128)(2,1)} %bitcast.68), channel_id=1, source_target_pairs={{0,256},{8,264},{16,272},{24,280},{32,288},{40,296},{48,304},{56,3... | collective-permute-start | bytes 73736 | tf_op jit(solution)/shard_map/ppermute | solution.py:196
  46.0 5.7 %collective-permute-start.1 = (bf16[2,16,768]{2,1,0:T(8,128)(2,1)S(1)}, bf16[2,16,768]{2,1,0:T(8,128)(2,1)S(1)}, u32[]{:S(2)}, u32[]{:S(2)}) collective-permute-start(bf16[2,16,768]{2,1,0:T(8,128)(2,1)S(1)} %broadcast_select_fusion), channel_id=1, source_target_pairs={{0,128},{8,136},{16,144},{24,152},{32,160},{40,168},{48,176},{56,1... | collective-permute-start | bytes 147464 | tf_op jit(solution)/shard_map/ppermute | solution.py:196
  52.5 15.6 %collective-permute-start.2 = (bf16[4,16,768]{2,1,0:T(8,128)(2,1)}, bf16[4,16,768]{2,1,0:T(8,128)(2,1)}, u32[]{:S(2)}, u32[]{:S(2)}) collective-permute-start(bf16[4,16,768]{2,1,0:T(8,128)(2,1)} %bitcast_select_fusion.4), channel_id=1, source_target_pairs={{0,64},{8,72},{16,80},{24,88},{32,96},{40,104},{48,112},{56,120},{... | collective-permute-start | bytes 294920 | tf_op jit(solution)/shard_map/ppermute | solution.py:196
  59.1 1.6 copy-start.1
  60.7 1.1 copy-start.4
  61.9 0.7 copy-start.12
  65.6 0.6 copy-start.5
  66.2 0.6 copy-start.7
  66.8 0.6 copy-start.9
  67.4 0.6 copy-start.11
  69.8 6.6 %collective-permute-start.3 = (bf16[256,768]{1,0:T(8,128)(2,1)}, bf16[256,768]{1,0:T(8,128)(2,1)S(1)}, u32[]{:S(2)}, u32[]{:S(2)}) collective-permute-start(bf16[256,768]{1,0:T(8,128)(2,1)} %bitcast.4), channel_id=1, source_target_pairs={{0,8},{8,0},{16,24},{24,16},{32,40},{40,32},{48,56},{56,48},{64,72... | collective-permute-start | bytes 1179656 | tf_op jit(solution)/shard_map/ppermute | solution.py:193
  78.6 19.6 %all-to-all-start.2 = ((bf16[8,64,384]{2,1,0:T(8,128)(2,1)}), bf16[8,64,384]{2,1,0:T(8,128)(2,1)}, u32[]{:S(2)}, u32[]{:S(2)}) async-start(bf16[8,64,384]{2,1,0:T(8,128)(2,1)} %pad_maximum_fusion), calls=%async_computation.2 | async-start | bytes 786432 | tf_op jit(solution)/shard_map/all_to_all | solution.py:29
  82.7 13.6 %collective-permute-start.4 = (bf16[8,16,768]{2,1,0:T(8,128)(2,1)}, bf16[8,16,768]{2,1,0:T(8,128)(2,1)}, u32[]{:S(2)}, u32[]{:S(2)}) collective-permute-start(bf16[8,16,768]{2,1,0:T(8,128)(2,1)} %bitcast_select_fusion.3), channel_id=1, source_target_pairs={{0,32},{8,40},{16,48},{24,56},{32,0},{40,8},{48,16},{56,24},{64,96... | collective-permute-start | bytes 589832 | tf_op jit(solution)/shard_map/ppermute | solution.py:196
  100.3 18.6 %all-to-all-start.3 = ((bf16[8,64,384]{2,1,0:T(8,128)(2,1)}), bf16[8,64,384]{2,1,0:T(8,128)(2,1)}, u32[]{:S(2)}, u32[]{:S(2)}) async-start(bf16[8,64,384]{2,1,0:T(8,128)(2,1)} %broadcast_in_dim.250), calls=%async_computation.3 | async-start | bytes 786432 | tf_op jit(solution)/shard_map/all_to_all | solution.py:29
  105.3 11.4 %collective-permute-start.5 = (bf16[16,16,768]{2,1,0:T(8,128)(2,1)}, bf16[16,16,768]{2,1,0:T(8,128)(2,1)}, u32[]{:S(2)}, u32[]{:S(2)}) collective-permute-start(bf16[16,16,768]{2,1,0:T(8,128)(2,1)} %bitcast_select_fusion.2), channel_id=1, source_target_pairs={{0,16},{8,24},{16,0},{24,8},{32,48},{40,56},{48,32},{56,40},{64,80... | collective-permute-start | bytes 1179656 | tf_op jit(solution)/shard_map/ppermute | solution.py:196
  120.3 6.1 %collective-permute-start.6 = (bf16[256,768]{1,0:T(8,128)(2,1)S(1)}, bf16[256,768]{1,0:T(8,128)(2,1)S(1)}, u32[]{:S(2)}, u32[]{:S(2)}) collective-permute-start(bf16[256,768]{1,0:T(8,128)(2,1)S(1)} %convolution_convert_fusion), channel_id=1, source_target_pairs={{0,8},{8,0},{16,24},{24,16},{32,40},{40,32},{48,56},{56,48},{64,72... | collective-permute-start | bytes 1179656 | tf_op jit(solution)/shard_map/ppermute | solution.py:193
  124.5 9.2 %collective-permute-start.7 = (bf16[32,16,768]{2,1,0:T(8,128)(2,1)}, bf16[32,16,768]{2,1,0:T(8,128)(2,1)}, u32[]{:S(2)}, u32[]{:S(2)}) collective-permute-start(bf16[32,16,768]{2,1,0:T(8,128)(2,1)} %bitcast_select_fusion.1), channel_id=1, source_target_pairs={{0,8},{8,0},{16,24},{24,16},{32,40},{40,32},{48,56},{56,48},{64,72... | collective-permute-start | bytes 2359304 | tf_op jit(solution)/shard_map/ppermute | solution.py:196
  127.6 19.4 %all-to-all-start.4 = ((bf16[32,8,768]{2,1,0:T(8,128)(2,1)}), bf16[32,8,768]{2,1,0:T(8,128)(2,1)}, u32[]{:S(2)}, u32[]{:S(2)}) async-start(bf16[32,8,768]{2,1,0:T(8,128)(2,1)} %fusion.3), calls=%async_computation.4 | async-start | bytes 786432 | tf_op jit(solution)/shard_map/all_to_all | solution.py:29
  147.0 14.9 %copy-start.2 = (bf16[768,1024]{1,0:T(8,128)(2,1)S(1)}, bf16[768,1024]{1,0:T(8,128)(2,1)}, u32[]{:S(2)}) copy-start(bf16[768,1024]{1,0:T(8,128)(2,1)} %constant.123.clone.move_ref) | copy-start | bytes 4718596
  147.0 14.9 %copy-start.6 = (f32[16,1024]{1,0:T(8,128)S(1)}, f32[16,1024]{1,0:T(8,128)}, u32[]{:S(2)}) copy-start(f32[16,1024]{1,0:T(8,128)} %copy-done.5) | copy-start | bytes 196612
  147.0 14.9 %copy-start.8 = (f32[8,1024]{1,0:T(8,128)S(1)}, f32[8,1024]{1,0:T(8,128)}, u32[]{:S(2)}) copy-start(f32[8,1024]{1,0:T(8,128)} %copy-done.7) | copy-start | bytes 98308
  147.0 14.9 %copy-start.10 = (f32[8,1024]{1,0:T(8,128)S(1)}, f32[8,1024]{1,0:T(8,128)}, u32[]{:S(2)}) copy-start(f32[8,1024]{1,0:T(8,128)} %copy-done.9) | copy-start | bytes 98308
  189.3 9.0 %collective-permute-start.8 = (bf16[256,1536]{1,0:T(8,128)(2,1)S(1)}, bf16[256,1536]{1,0:T(8,128)(2,1)S(1)}, u32[]{:S(2)}, u32[]{:S(2)}) collective-permute-start(bf16[256,1536]{1,0:T(8,128)(2,1)S(1)} %bitcast.62), channel_id=1, source_target_pairs={{0,8},{8,0},{16,24},{24,16},{32,40},{40,32},{48,56},{56,48},{64,72... | collective-permute-start | bytes 2359304 | tf_op jit(solution)/shard_map/ppermute | solution.py:193

commit v4 on v3

--- a/solution.py
+++ b/solution.py
@@ -161,6 +161,48 @@
             ] = jnp.concatenate(pieces, axis=0).astype(bf16)
 
 
+def up_kernel(own_ref, other_ref, weight_ref, send_ref):
+    count = own_ref.shape[0] * 2 // send_ref.shape[1]
+    size = send_ref.shape[1] // 2
+    for place, rows_ref in enumerate((own_ref, other_ref)):
+        part = product(rows_ref[...], weight_ref[...]).astype(bf16)
+        for n in range(count):
+            send_ref[n, pl.ds(place * size, size), :] = part[n * size : (n + 1) * size]
+
+
+def gelu_kernel(parts_ref, send_ref):
+    pre = parts_ref[0].astype(f32)
+    for n in range(1, parts_ref.shape[0]):
+        pre = pre + parts_ref[n].astype(f32)
+    hidden = (0.5 * pre * (1.0 + lax.erf(pre * 0.5**0.5))).astype(bf16)
+    for n in range(send_ref.shape[0]):
+        send_ref[n] = hidden
+
+
+def hidden_half(hidden_ref, place):
+    size = hidden_ref.shape[1] // 2
+    parts = [hidden_ref[n, pl.ds(place * size, size), :] for n in range(hidden_ref.shape[0])]
+    return jnp.concatenate(parts, axis=0)
+
+
+def down_other_kernel(hidden_ref, weight_ref, out_ref):
+    out_ref[...] = product(hidden_half(hidden_ref, 1), weight_ref[...]).astype(bf16)
+
+
+def down_own_kernel(hidden_ref, weight_ref, add_ref, out_ref):
+    own = product(hidden_half(hidden_ref, 0), weight_ref[...])
+    out_ref[...] = (own + add_ref[...].astype(f32)).astype(bf16)
+
+
+def target_kernel(branch_ref, teacher_ref, columns_ref, mixed_ref, local_ref, terms_ref):
+    teacher = teacher_ref[...].astype(f32) + jnp.sum(branch_ref[...].astype(f32), axis=0)
+    teacher = teacher.astype(bf16)
+    local_ref[...] = teacher
+    term = mixed_ref[...] - product(teacher, columns_ref[...], ((1,), (1,)))
+    for n in range(terms_ref.shape[0]):
+        terms_ref[n] = term
+
+
 def call_kernel(kernel, out_shape, flops, *operands):
     whole = pl.BlockSpec(memory_space=pltpu.VMEM)
     moved = sum(x.size * x.dtype.itemsize for x in operands)
@@ -198,10 +240,6 @@
         place = lax.broadcasted_iota(jnp.int32, (1, 2) + blocks.shape[1:], 1)
         both = jnp.where(place == mine, blocks[:, None], other[:, None])
         return both.reshape((-1,) + blocks.shape[1:])
-
-    bits = []
-    while 2 ** len(bits) < wide:
-        bits.insert(0, 2 ** len(bits))
 
     def local(
         teacher_in,
@@ -258,39 +296,39 @@
         normed = (
             (own - center) * lax.rsqrt(variance + EPSILON) * teacher_gain.astype(f32)
         ).astype(bf16)
-        normed = spread(normed, "wide", chips, groups).reshape(half, features)
-        columns = projector.T[None]
-        for bit in bits[:-3]:
-            columns = doubled(columns, bit)
-        normed, columns, student = lax.optimization_barrier((normed, columns, student))
+        first = jnp.concatenate([normed, projector.T], axis=0)
+        first = spread(first, "wide", chips, groups)
+        first, student = lax.optimization_barrier((first, student))
         norm, keys, values, probs, side, early, picked_norm, picked_in, mixed = student
+        normed = first[:, :rows].reshape(half, features)
         normed_other = swap(normed)
 
-        pre = jnp.concatenate(
+        hidden_shape = jax.ShapeDtypeStruct((narrow, 2 * half // narrow, mlp_in.shape[1]), bf16)
+        rows_shape = jax.ShapeDtypeStruct((half, features), bf16)
+        up_flops = 4 * half * mlp_in.size
+        pre = call_kernel(up_kernel, hidden_shape, up_flops, normed, normed_other, mlp_in)
+        columns = doubled(first[:, rows:], 1).reshape(-1, features)
+        pre = exchange(pre, "narrow")
+        hidden = exchange(call_kernel(gelu_kernel, hidden_shape, 8 * pre.size, pre), "narrow")
+        hidden, columns = lax.optimization_barrier((hidden, columns))
+        branch = swap(call_kernel(down_other_kernel, rows_shape, up_flops // 2, hidden, mlp_out))
+        branch = call_kernel(
+            down_own_kernel, rows_shape, up_flops // 2, hidden, mlp_out, branch
+        )
+        branch = exchange(branch.reshape(chips, rows, features), "wide", groups)
+        teacher_local, terms = call_kernel(
+            target_kernel,
             [
-                product(block, mlp_in).astype(bf16).reshape(narrow, half // narrow, -1)
-                for block in (normed, normed_other)
+                jax.ShapeDtypeStruct((rows, features), bf16),
+                jax.ShapeDtypeStruct((narrow, picks, width), f32),
             ],
-            axis=1,
+            2 * rows * columns.size,
+            branch,
+            teacher_in,
+            columns,
+            mixed,
         )
-        pre = exchange(pre, "narrow")
-        columns = doubled(columns, bits[-3])
-        pre, columns = lax.optimization_barrier((pre, columns))
-        pre = jnp.sum(pre.astype(f32), axis=0)
-        hidden = jax.nn.gelu(pre, approximate=False).astype(bf16)
-        hidden = spread(hidden, "narrow", narrow)
-        columns = doubled(columns, bits[-2])
-        hidden, columns = lax.optimization_barrier((hidden, columns))
-        hidden_own = hidden[:, : half // narrow].reshape(half, -1)
-        hidden_other = hidden[:, half // narrow :].reshape(half, -1)
-        branch = swap(product(hidden_other, mlp_out).astype(bf16))
-        branch = (product(hidden_own, mlp_out) + branch.astype(f32)).astype(bf16)
-        branch = exchange(branch.reshape(chips, rows, features), "wide", groups)
-        teacher_local = (own + jnp.sum(branch.astype(f32), axis=0)).astype(bf16)
-
-        columns = doubled(columns, bits[-1]).reshape(-1, features)
-        target = product(teacher_local, columns, ((1,), (1,)))
-        terms = spread(mixed - target, "narrow", narrow)
+        terms = exchange(terms, "narrow")
 
         piece = width // wide
         kinds = 2 + 2 * heads_here

time: 203 us -> 172 us (0.85)
  starting transfers between devices: 74.4 us -> 48.3 us
  blocking collectives: 37.1 us -> 56.5 us
  other arithmetic: 18.3 us -> 6.6 us
  waiting for transfers between devices: 47.1 us -> 40.2 us
  matrix products: 6.93 us -> 0.55 us
  Pallas kernels: 4.3 us -> 7.74 us
  local copies, waits for them, and re-layouts: 11.2 us -> 8.79 us
    ppermute x6 -> x1, waiting for transfers between devices: 30.6 us -> 0.01 us  [doubled(): other = lax.ppermute(blocks, 'wide', [(i, i ^ bit) for i in range(wide)])]
    all_to_all x5 -> x4, waiting for transfers between devices: 14.9 us -> 35.9 us  [exchange(): return lax.all_to_all(block, axis, 0, 0, axis_index_groups=groups)]
    ppermute x6 -> x1, starting transfers between devices: 22.9 us -> 2.28 us  [doubled(): other = lax.ppermute(blocks, 'wide', [(i, i ^ bit) for i in range(wide)])]
    all_to_all x2 -> x3, blocking collectives: 37.1 us -> 56.5 us  [exchange(): return lax.all_to_all(block, axis, 0, 0, axis_index_groups=groups)]
    select_n x6 -> x1, other arithmetic: 9.95 us -> 1.63 us  [doubled(): both = jnp.where(place == mine, blocks[:, None], other[:, None])]
    all_to_all x5 -> x4, starting transfers between devices: 35.2 us -> 28.6 us  [exchange(): return lax.all_to_all(block, axis, 0, 0, axis_index_groups=groups)]
    dot_general x7 -> x2, matrix products: 6.93 us -> 0.55 us  [product(): lax.dot_general(left, right, (dims, ((), ())), preferred_element_type=f32)]
    pallas_call x2 -> x7, Pallas kernels: 4.3 us -> 7.74 us  [call_kernel(): pl.pallas_call(kernel, out_shape=out_shape, in_specs=[whole] * len(operan...]
  transfers between devices with their start and end apart: 14 -> 8, of which waited for: 7 -> 7; matrix products, arithmetic and copies ran while one was open for 8% -> 2% of each run, Pallas kernels for 2% -> 2%
where the time goes in v4:
time: 172 us; the launch traced here: 170 us
  blocking collectives  56.5 us (33%)
  starting transfers between devices  48.3 us (28%)
  waiting for transfers between devices  40.2 us (23%)
  local copies, waits for them, and re-layouts  8.79 us (5%)
  Pallas kernels  7.74 us (4%)
  other arithmetic  6.6 us (4%)
    all_to_all x3, blocking collectives, exchange(): return lax.all_to_all(block, axis, 0, 0, axis_index_groups=groups)  56.5 us
    all_to_all x4, waiting for transfers between devices, exchange(): return lax.all_to_all(block, axis, 0, 0, axis_index_groups=groups)  35.9 us
    all_to_all x4, starting transfers between devices, exchange(): return lax.all_to_all(block, axis, 0, 0, axis_index_groups=groups)  28.6 us
    ppermute x3, starting transfers between devices, swap(): return lax.ppermute(block, 'wide', pairs)  17.5 us
    pallas_call x7, Pallas kernels, call_kernel(): pl.pallas_call(kernel, out_shape=out_shape, in_specs=[whole] * len(operan...  7.74 us
    unnamed x46, local copies, waits for them, and re-layouts  4.52 us
    ppermute x3, waiting for transfers between devices, swap(): return lax.ppermute(block, 'wide', pairs)  4.23 us
  transfers between devices with their start and end apart: 8, of which 7 were waited for; matrix products, arithmetic and copies ran while one was open for 2% of the time, Pallas kernels for 2%

profile of v4, /device:TPU:1, one launch (start us, length us, event | category | flops | bytes accessed | tf_op | source)
XLA Modules:
  0.0 169.7 jit_solution(1280173108408041567)
XLA Ops:
  0.6 0.9 convert_reduce_fusion
  1.5 0.6 broadcast_in_dim.55
  2.1 6.7 %all-to-all-start = ((f32[8,8,2]{1,2,0:T(2,128)}), f32[8,8,2]{1,2,0:T(2,128)S(1)}, u32[]{:S(2)}, u32[]{:S(2)}) async-start(f32[8,8,2]{1,2,0:T(2,128)} %broadcast_in_dim.55), calls=%async_computation | async-start | bytes 16384 | tf_op jit(solution)/shard_map/all_to_all | solution.py:29
  8.8 0.7 convert_element_type.13
  9.5 4.4 %all-to-all-done = f32[8,8,2]{1,2,0:T(2,128)S(1)} async-done(((f32[8,8,2]{1,2,0:T(2,128)}), f32[8,8,2]{1,2,0:T(2,128)S(1)}, u32[]{:S(2)}, u32[]{:S(2)}) %all-to-all-start) | async-done | bytes 544 | tf_op jit(solution)/shard_map/all_to_all | solution.py:29
  13.8 0.8 fusion.11
  14.6 0.7 pad_maximum_fusion
  15.4 1.1 broadcast_in_dim.56
  16.5 15.0 %all-to-all-start.1 = ((bf16[32,24,768]{2,1,0:T(8,128)(2,1)}), bf16[32,24,768]{2,1,0:T(8,128)(2,1)}, u32[]{:S(2)}, u32[]{:S(2)}) async-start(bf16[32,24,768]{2,1,0:T(8,128)(2,1)} %broadcast_in_dim.56), calls=%async_computation.1 | async-start | bytes 2359296 | tf_op jit(solution)/shard_map/all_to_all | solution.py:29
  31.6 0.1 copy.21
  31.7 0.1 reshape.41.wanted_ref
  31.8 1.1 copy-done.6
  32.9 3.1 %shard_map.139 = (bf16[1024,1024]{1,0:T(8,128)(2,1)S(1)}, bf16[1024,128]{1,0:T(8,128)(2,1)S(1)}, bf16[1024,128]{1,0:T(8,128)(2,1)S(1)}, f32[16,1024]{1,0:T(8,128...) custom-call(s32[8,1]{1,0:T(8,128)S(1)} %reshape.41.wanted_ref, ...), custom_call_target="tpu_custom_call" | custom-call | flops 603979776 | bytes 3145824 | tf_op jit(solution)/shard_map/pallas_call | solution.py:209
  36.0 1.4 copy-done.2
  37.3 0.7 copy-done.10
  38.1 0.6 copy-done.13
  38.7 0.6 copy-done.15
  39.3 21.6 %all-to-all-done.1 = bf16[32,24,768]{2,1,0:T(8,128)(2,1)} async-done(((bf16[32,24,768]{2,1,0:T(8,128)(2,1)}), bf16[32,24,768]{2,1,0:T(8,128)(2,1)}, u32[]{:S(2)}, u32[]{:S(2)}) %all-to-all-start.1) | async-done | bytes 1179680 | tf_op jit(solution)/shard_map/all_to_all | solution.py:29
  60.9 1.0 slice_bitcast_fusion.own_ref
  61.9 6.1 %collective-permute-start = (bf16[256,768]{1,0:T(8,128)(2,1)S(1)}, bf16[256,768]{1,0:T(8,128)(2,1)S(1)}, u32[]{:S(2)}, u32[]{:S(2)}) collective-permute-start(bf16[256,768]{1,0:T(8,128)(2,1)S(1)} %slice_bitcast_fusion.own_ref), channel_id=1, source_target_pairs={{0,8},{8,0},{16,24},{24,16},{32,40},{40,32},{48,56},{56,48},{64,72... | collective-permute-start | bytes 1179656 | tf_op jit(solution)/shard_map/ppermute | solution.py:235
  68.0 1.3 collective-permute-done.other_ref
  69.3 1.3 shard_map.140
  70.6 3.5 %all-to-all-start.2 = ((bf16[8,64,384]{2,1,0:T(8,128)(2,1)}), bf16[8,64,384]{2,1,0:T(8,128)(2,1)S(1)}, u32[]{:S(2)}, u32[]{:S(2)}) async-start(bf16[8,64,384]{2,1,0:T(8,128)(2,1)} %shard_map.140), calls=%async_computation.2 | async-start | bytes 786432 | tf_op jit(solution)/shard_map/all_to_all | solution.py:29
  74.1 1.2 slice.54
  75.3 2.3 %collective-permute-start.1 = (bf16[32,16,768]{2,1,0:T(8,128)(2,1)S(1)}, bf16[32,16,768]{2,1,0:T(8,128)(2,1)}, u32[]{:S(2)}, u32[]{:S(2)}) collective-permute-start(bf16[32,16,768]{2,1,0:T(8,128)(2,1)S(1)} %slice.54), channel_id=1, source_target_pairs={{0,8},{8,0},{16,24},{24,16},{32,40},{40,32},{48,56},{56,48},{64,72... | collective-permute-start | bytes 2359304 | tf_op jit(solution)/shard_map/ppermute | solution.py:238
  77.6 4.7 %all-to-all-done.2.parts_ref = bf16[8,64,384]{2,1,0:T(8,128)(2,1)S(1)} async-done(((bf16[8,64,384]{2,1,0:T(8,128)(2,1)}), bf16[8,64,384]{2,1,0:T(8,128)(2,1)S(1)}, u32[]{:S(2)}, u32[]{:S(2)}) %all-to-all-start.2) | async-done | bytes 393248 | tf_op jit(solution)/shard_map/all_to_all | solution.py:29
  82.3 0.8 shard_map.141
  83.1 3.5 %all-to-all-start.3 = ((bf16[8,64,384]{2,1,0:T(8,128)(2,1)}), bf16[8,64,384]{2,1,0:T(8,128)(2,1)S(1)}, u32[]{:S(2)}, u32[]{:S(2)}) async-start(bf16[8,64,384]{2,1,0:T(8,128)(2,1)} %shard_map.141), calls=%async_computation.3 | async-start | bytes 786432 | tf_op jit(solution)/shard_map/all_to_all | solution.py:29
  86.6 0.1 broadcast_in_dim.57
  86.6 0.1 broadcast_in_dim.58
  86.8 1.6 bitcast_select_fusion.columns_ref
  88.4 5.4 %all-to-all-done.3.hidden_ref = bf16[8,64,384]{2,1,0:T(8,128)(2,1)S(1)} async-done(((bf16[8,64,384]{2,1,0:T(8,128)(2,1)}), bf16[8,64,384]{2,1,0:T(8,128)(2,1)S(1)}, u32[]{:S(2)}, u32[]{:S(2)}) %all-to-all-start.3) | async-done | bytes 393248 | tf_op jit(solution)/shard_map/all_to_all | solution.py:29
  93.8 0.4 shard_map.142
  94.2 4.2 %collective-permute-start.2 = (bf16[256,768]{1,0:T(8,128)(2,1)S(1)}, bf16[256,768]{1,0:T(8,128)(2,1)S(1)}, u32[]{:S(2)}, u32[]{:S(2)}) collective-permute-start(bf16[256,768]{1,0:T(8,128)(2,1)S(1)} %shard_map.142), channel_id=1, source_target_pairs={{0,8},{8,0},{16,24},{24,16},{32,40},{40,32},{48,56},{56,48},{64,72... | collective-permute-start | bytes 1179656 | tf_op jit(solution)/shard_map/ppermute | solution.py:235
  98.4 1.3 collective-permute-done.2.add_ref
  99.8 0.4 shard_map.143
  100.2 21.9 %all_to_all.35.branch_ref = bf16[32,8,768]{2,1,0:T(8,128)(2,1)S(1)} all-to-all(bf16[32,8,768]{2,1,0:T(8,128)(2,1)S(1)} %bitcast.29), channel_id=1, replica_groups={{0,16,32,48,64,80,96,112,128,144,160,176,192,208,224,240,256,272,288,30..., dimensions={0} | all-to-all | bytes 786432 | tf_op jit(solution)/shard_map/all_to_all | solution.py:29
  122.0 0.5 shard_map.144
  122.6 8.7 %all_to_all.36.terms_ref = f32[8,8,1024]{2,1,0:T(8,128)S(1)} all-to-all(f32[8,8,1024]{2,1,0:T(8,128)S(1)} %get-tuple-element.39), channel_id=1, replica_groups=mesh['wide'=64,'narrow'=8] {'narrow'}, dimensions={0} | all-to-all | bytes 524288 | tf_op jit(solution)/shard_map/all_to_all | solution.py:29
  131.3 1.2 shard_map.145
  132.5 26.0 %all_to_all.37 = bf16[32,8,1536]{2,1,0:T(8,128)(2,1)S(1)} all-to-all(bf16[32,8,1536]{2,1,0:T(8,128)(2,1)S(1)} %bitcast.27), channel_id=1, replica_groups={{0,16,32,48,64,80,96,112,128,144,160,176,192,208,224,240,256,272,288,30..., dimensions={0} | all-to-all | bytes 1572864 | tf_op jit(solution)/shard_map/all_to_all | solution.py:29
  158.5 7.1 %collective-permute-start.3 = (bf16[256,1536]{1,0:T(8,128)(2,1)S(1)}, bf16[256,1536]{1,0:T(8,128)(2,1)S(1)}, u32[]{:S(2)}, u32[]{:S(2)}) collective-permute-start(bf16[256,1536]{1,0:T(8,128)(2,1)S(1)} %bitcast.30), channel_id=1, source_target_pairs={{0,8},{8,0},{16,24},{24,16},{32,40},{40,32},{48,56},{56,48},{64,72... | collective-permute-start | bytes 2359304 | tf_op jit(solution)/shard_map/ppermute | solution.py:235
  165.7 0.3 fusion.1
  166.0 1.6 collective-permute-done.3
  167.5 0.3 convolution_add_fusion
  167.8 0.6 fusion.7
  168.4 0.6 fusion.13
  169.0 0.6 pad_maximum_fusion.1
  (49 shorter events, 0.2 us)
Async XLA Ops:
  2.1 11.7 %all-to-all-start = ((f32[8,8,2]{1,2,0:T(2,128)}), f32[8,8,2]{1,2,0:T(2,128)S(1)}, u32[]{:S(2)}, u32[]{:S(2)}) async-start(f32[8,8,2]{1,2,0:T(2,128)} %broadcast_in_dim.55), calls=%async_computation | async-start | bytes 16384 | tf_op jit(solution)/shard_map/all_to_all | solution.py:29
  15.4 16.2 %copy-start.21 = (s32[4,2]{0,1:T(2,128)S(1)}, s32[4,2]{0,1:T(2,128)}, u32[]{:S(2)}) copy-start(s32[4,2]{0,1:T(2,128)} %param.18) | copy-start | bytes 100
  15.4 16.2 %copy-start.22 = (s32[4,2]{0,1:T(2,128)S(1)}, s32[4,2]{0,1:T(2,128)}, u32[]{:S(2)}) copy-start(s32[4,2]{0,1:T(2,128)} %constant.61) | copy-start | bytes 100
  15.4 16.4 %copy-start.1 = (bf16[4,256,1024]{2,1,0:T(8,128)(2,1)S(1)}, bf16[4,256,1024]{2,1,0:T(8,128)(2,1)}, u32[]{:S(2)}) copy-start(bf16[4,256,1024]{2,1,0:T(8,128)(2,1)} %param.17) | copy-start | bytes 6291460
  15.4 16.4 %copy-start.5 = (bf16[128,1024]{1,0:T(8,128)(2,1)S(1)}, bf16[128,1024]{1,0:T(8,128)(2,1)}, u32[]{:S(2)}) copy-start(bf16[128,1024]{1,0:T(8,128)(2,1)} %w_out_ref.3) | copy-start | bytes 786436
  15.4 16.4 %copy-start.19 = (s32[16,1]{1,0:T(8,128)S(1)}, s32[16,1]{1,0:T(8,128)}, u32[]{:S(2)}) copy-start(s32[16,1]{1,0:T(8,128)} %constant.55.clone.first_ref) | copy-start | bytes 196
  16.5 44.4 %all-to-all-start.1 = ((bf16[32,24,768]{2,1,0:T(8,128)(2,1)}), bf16[32,24,768]{2,1,0:T(8,128)(2,1)}, u32[]{:S(2)}, u32[]{:S(2)}) async-start(bf16[32,24,768]{2,1,0:T(8,128)(2,1)} %broadcast_in_dim.56), calls=%async_computation.1 | async-start | bytes 2359296 | tf_op jit(solution)/shard_map/all_to_all | solution.py:29
  31.7 1.1 copy-start.6
  32.9 36.4 %copy-start.7 = (bf16[768,384]{1,0:T(8,128)(2,1)S(1)}, bf16[768,384]{1,0:T(8,128)(2,1)}, u32[]{:S(2)}) copy-start(bf16[768,384]{1,0:T(8,128)(2,1)} %weight_ref.3) | copy-start | bytes 1769476
  36.0 1.4 copy-start.2
  37.3 0.7 copy-start.10
  38.1 0.6 copy-start.13
  38.7 0.6 copy-start.15
  39.3 31.4 %copy-start.8 = (bf16[1024,128]{1,0:T(8,128)(2,1)}, bf16[1024,128]{1,0:T(8,128)(2,1)S(1)}, u32[]{:S(2)}) copy-start(bf16[1024,128]{1,0:T(8,128)(2,1)S(1)} %get-tuple-element.42.keys_ref) | copy-start | bytes 786436
  39.3 31.4 %copy-start.17 = (f32[8,1024]{1,0:T(8,128)}, f32[8,1024]{1,0:T(8,128)S(1)}, u32[]{:S(2)}) copy-start(f32[8,1024]{1,0:T(8,128)S(1)} %get-tuple-element.38.mixed_ref) | copy-start | bytes 98308
  61.9 7.4 %collective-permute-start = (bf16[256,768]{1,0:T(8,128)(2,1)S(1)}, bf16[256,768]{1,0:T(8,128)(2,1)S(1)}, u32[]{:S(2)}, u32[]{:S(2)}) collective-permute-start(bf16[256,768]{1,0:T(8,128)(2,1)S(1)} %slice_bitcast_fusion.own_ref), channel_id=1, source_target_pairs={{0,8},{8,0},{16,24},{24,16},{32,40},{40,32},{48,56},{56,48},{64,72... | collective-permute-start | bytes 1179656 | tf_op jit(solution)/shard_map/ppermute | solution.py:235
  70.6 11.6 %all-to-all-start.2 = ((bf16[8,64,384]{2,1,0:T(8,128)(2,1)}), bf16[8,64,384]{2,1,0:T(8,128)(2,1)S(1)}, u32[]{:S(2)}, u32[]{:S(2)}) async-start(bf16[8,64,384]{2,1,0:T(8,128)(2,1)} %shard_map.140), calls=%async_computation.2 | async-start | bytes 786432 | tf_op jit(solution)/shard_map/all_to_all | solution.py:29
  75.3 11.4 %copy-start.20 = (bf16[32,16,768]{2,1,0:T(8,128)(2,1)}, bf16[32,16,768]{2,1,0:T(8,128)(2,1)S(1)}, u32[]{:S(2)}) copy-start(bf16[32,16,768]{2,1,0:T(8,128)(2,1)S(1)} %slice.54) | copy-start | bytes 2359300
  75.3 11.4 %collective-permute-start.1 = (bf16[32,16,768]{2,1,0:T(8,128)(2,1)S(1)}, bf16[32,16,768]{2,1,0:T(8,128)(2,1)}, u32[]{:S(2)}, u32[]{:S(2)}) collective-permute-start(bf16[32,16,768]{2,1,0:T(8,128)(2,1)S(1)} %slice.54), channel_id=1, source_target_pairs={{0,8},{8,0},{16,24},{24,16},{32,40},{40,32},{48,56},{56,48},{64,72... | collective-permute-start | bytes 2359304 | tf_op jit(solution)/shard_map/ppermute | solution.py:238
  83.1 10.7 %all-to-all-start.3 = ((bf16[8,64,384]{2,1,0:T(8,128)(2,1)}), bf16[8,64,384]{2,1,0:T(8,128)(2,1)S(1)}, u32[]{:S(2)}, u32[]{:S(2)}) async-start(bf16[8,64,384]{2,1,0:T(8,128)(2,1)} %shard_map.141), calls=%async_computation.3 | async-start | bytes 786432 | tf_op jit(solution)/shard_map/all_to_all | solution.py:29
  86.7 7.0 %copy-start = (bf16[384,768]{1,0:T(8,128)(2,1)S(1)}, bf16[384,768]{1,0:T(8,128)(2,1)}, u32[]{:S(2)}) copy-start(bf16[384,768]{1,0:T(8,128)(2,1)} %weight_ref.5) | copy-start | bytes 1769476
  94.1 27.9 %copy-start.12 = (bf16[8,768]{1,0:T(8,128)(2,1)S(1)}, bf16[8,768]{1,0:T(8,128)(2,1)}, u32[]{:S(2)}) copy-start(bf16[8,768]{1,0:T(8,128)(2,1)} %teacher_ref.1) | copy-start | bytes 36868
  94.2 27.9 %copy-start.18 = (f32[8,1024]{1,0:T(8,128)S(1)}, f32[8,1024]{1,0:T(8,128)}, u32[]{:S(2)}) copy-start(f32[8,1024]{1,0:T(8,128)} %copy-done.17) | copy-start | bytes 98308
  94.2 5.6 %collective-permute-start.2 = (bf16[256,768]{1,0:T(8,128)(2,1)S(1)}, bf16[256,768]{1,0:T(8,128)(2,1)S(1)}, u32[]{:S(2)}, u32[]{:S(2)}) collective-permute-start(bf16[256,768]{1,0:T(8,128)(2,1)S(1)} %shard_map.142), channel_id=1, source_target_pairs={{0,8},{8,0},{16,24},{24,16},{32,40},{40,32},{48,56},{56,48},{64,72... | collective-permute-start | bytes 1179656 | tf_op jit(solution)/shard_map/ppermute | solution.py:235
  99.8 31.5 %copy-start.4 = (bf16[768,1024]{1,0:T(8,128)(2,1)S(1)}, bf16[768,1024]{1,0:T(8,128)(2,1)}, u32[]{:S(2)}) copy-start(bf16[768,1024]{1,0:T(8,128)(2,1)} %constant.56.clone.move_ref) | copy-start | bytes 4718596
  100.1 31.1 %copy-start.3 = (bf16[1024,1024]{1,0:T(8,128)(2,1)S(1)}, bf16[1024,1024]{1,0:T(8,128)(2,1)}, u32[]{:S(2)}) copy-start(bf16[1024,1024]{1,0:T(8,128)(2,1)} %copy-done.2) | copy-start | bytes 6291460
  100.1 31.1 %copy-start.9 = (bf16[1024,128]{1,0:T(8,128)(2,1)S(1)}, bf16[1024,128]{1,0:T(8,128)(2,1)}, u32[]{:S(2)}) copy-start(bf16[1024,128]{1,0:T(8,128)(2,1)} %copy-done.8) | copy-start | bytes 786436
  100.1 31.1 %copy-start.11 = (bf16[1024,128]{1,0:T(8,128)(2,1)S(1)}, bf16[1024,128]{1,0:T(8,128)(2,1)}, u32[]{:S(2)}) copy-start(bf16[1024,128]{1,0:T(8,128)(2,1)} %copy-done.10) | copy-start | bytes 786436
  100.2 31.1 %copy-start.14 = (f32[8,1024]{1,0:T(8,128)S(1)}, f32[8,1024]{1,0:T(8,128)}, u32[]{:S(2)}) copy-start(f32[8,1024]{1,0:T(8,128)} %copy-done.13) | copy-start | bytes 98308
  100.2 31.1 %copy-start.16 = (f32[8,1024]{1,0:T(8,128)S(1)}, f32[8,1024]{1,0:T(8,128)}, u32[]{:S(2)}) copy-start(f32[8,1024]{1,0:T(8,128)} %copy-done.15) | copy-start | bytes 98308
  158.5 9.0 %collective-permute-start.3 = (bf16[256,1536]{1,0:T(8,128)(2,1)S(1)}, bf16[256,1536]{1,0:T(8,128)(2,1)S(1)}, u32[]{:S(2)}, u32[]{:S(2)}) collective-permute-start(bf16[256,1536]{1,0:T(8,128)(2,1)S(1)} %bitcast.30), channel_id=1, source_target_pairs={{0,8},{8,0},{16,24},{24,16},{32,40},{40,32},{48,56},{56,48},{64,72... | collective-permute-start | bytes 2359304 | tf_op jit(solution)/shard_map/ppermute | solution.py:235

commit v5 on v4

--- a/solution.py
+++ b/solution.py
@@ -122,7 +122,7 @@
     picks, width = picked_in_ref.shape
     local_width = keys_ref.shape[1]
     heads = local_width // HEAD_DIM
-    delta = (picked_in_ref[...] + jnp.sum(terms_ref[...], axis=0)) / divisor
+    delta = (picked_in_ref[...] + jnp.sum(terms_ref[...].astype(f32), axis=0)) / divisor
     d_context = product(delta.astype(bf16), w_out_ref[...], ((1,), (1,)))
     d_probs = product(by_head(d_context, heads).astype(bf16), values_ref[...], ((1,), (1,)))
     probs = probs_ref[...]
@@ -161,21 +161,75 @@
             ] = jnp.concatenate(pieces, axis=0).astype(bf16)
 
 
-def up_kernel(own_ref, other_ref, weight_ref, send_ref):
-    count = own_ref.shape[0] * 2 // send_ref.shape[1]
-    size = send_ref.shape[1] // 2
-    for place, rows_ref in enumerate((own_ref, other_ref)):
-        part = product(rows_ref[...], weight_ref[...]).astype(bf16)
-        for n in range(count):
-            send_ref[n, pl.ds(place * size, size), :] = part[n * size : (n + 1) * size]
-
-
-def gelu_kernel(parts_ref, send_ref):
-    pre = parts_ref[0].astype(f32)
-    for n in range(1, parts_ref.shape[0]):
-        pre = pre + parts_ref[n].astype(f32)
+def thirds(block):
+    high = rounded(block)
+    middle = rounded(block - high)
+    return [high, middle, block - high - middle]
+
+
+def first_kernel(rows_ref, columns_ref, send_ref):
+    block = jnp.concatenate([rows_ref[...].astype(f32), columns_ref[...].astype(f32)], axis=0)
+    block = block.astype(bf16)
+    for n in range(send_ref.shape[0]):
+        send_ref[n] = block
+
+
+def up_kernel(own_ref, other_ref, gain_ref, weight_ref, send_ref):
+    parts, _, hidden = send_ref.shape
+    size = own_ref.shape[0] // parts
+    features = own_ref.shape[1]
+    pieces = []
+    for n in range(parts):
+        pieces += [own_ref[pl.ds(n * size, size), :], other_ref[pl.ds(n * size, size), :]]
+    low = jnp.concatenate(pieces, axis=0)
+    rows = low.astype(f32)
+    gain = gain_ref[...].astype(f32)
+    center = jnp.mean(rows, axis=1, keepdims=True)
+    pre = product(((rows - center) * gain).astype(bf16), weight_ref[...]).astype(bf16)
+    squares = rows * rows
+    square_high = squares.astype(bf16)
+    square_low = (squares - square_high.astype(f32)).astype(bf16)
+    ones = jnp.ones((8, features), bf16)
+    flat = ((1,), (1,))
+    means = product(ones, low, flat)[0:1] / features
+    totals = (product(ones, square_high, flat) + product(ones, square_low, flat))[0:1]
+    stats = jnp.concatenate(thirds(means) + thirds(totals), axis=0)
+    gains = product(jnp.broadcast_to(gain, (8, features)).astype(bf16), weight_ref[...])[0:1]
+    gains = jnp.concatenate(thirds(gains), axis=0)
+    span = 2 * size
+    for n in range(parts):
+        send_ref[n, pl.ds(0, span), :] = pre[n * span : (n + 1) * span]
+        tile = n * span // LANES * LANES
+        mine = stats[:, tile : tile + LANES]
+        if n * span % LANES:
+            mine = pltpu.roll(mine, LANES - n * span % LANES, 1)
+        lines = [mine] + [jnp.zeros_like(mine)] * (hidden // LANES - 1)
+        extra = jnp.concatenate([gains, jnp.concatenate(lines, axis=1)], axis=0)
+        extra = jnp.concatenate([extra, jnp.zeros((16 - extra.shape[0], hidden), f32)], axis=0)
+        send_ref[n, pl.ds(span, 16), :] = extra.astype(bf16)
+
+
+def gelu_kernel(d_t, parts_ref, send_ref):
+    parts, span, _ = send_ref.shape
+    pre = parts_ref[0, pl.ds(0, span), :].astype(f32)
+    for n in range(1, parts):
+        pre = pre + parts_ref[n, pl.ds(0, span), :].astype(f32)
+    extra = [parts_ref[n, pl.ds(span, 16), :].astype(f32) for n in range(parts)]
+
+    def joined(block, at):
+        return block[at : at + 1] + block[at + 1 : at + 2] + block[at + 2 : at + 3]
+
+    means = [joined(block, 3)[:, :LANES] for block in extra]
+    center = sum(means) / parts
+    variance = sum(joined(block, 6)[:, :LANES] for block in extra) / d_t - center * center
+    lines = [mean - center for mean in means] + [lax.rsqrt(variance + EPSILON)]
+    lines = jnp.concatenate(lines + [jnp.zeros((LANES - parts - 1, LANES), f32)], axis=0)
+    lines = lines.T[:span]
+    for n in range(parts):
+        pre = pre + lines[:, n : n + 1] * joined(extra[n], 0)
+    pre = pre * lines[:, parts : parts + 1]
     hidden = (0.5 * pre * (1.0 + lax.erf(pre * 0.5**0.5))).astype(bf16)
-    for n in range(send_ref.shape[0]):
+    for n in range(parts):
         send_ref[n] = hidden
 
 
@@ -199,8 +253,56 @@
     teacher = teacher.astype(bf16)
     local_ref[...] = teacher
     term = mixed_ref[...] - product(teacher, columns_ref[...], ((1,), (1,)))
+    term = term.astype(bf16)
     for n in range(terms_ref.shape[0]):
         terms_ref[n] = term
+
+
+def partial_kernel(piece, features, local_width, core_ref, got_ref, mine_ref, theirs_ref):
+    heads = local_width // HEAD_DIM
+    shared_width = got_ref.shape[1] - CORES * LANES
+    shared = got_ref[:, :shared_width]
+    starts = [features + n * local_width for n in range(4)]
+    both = []
+    for core in range(CORES):
+        factors = got_ref[:, shared_width + core * LANES : shared_width + (core + 1) * LANES]
+        full = product(factors, shared, ((0,), (0,)))
+
+        def part(kind, start, size):
+            return full[kind * piece : (kind + 1) * piece, start : start + size]
+
+        def per_head(kind, start):
+            block = part(kind, start, local_width)
+            head = lax.broadcasted_iota(jnp.int32, block.shape, 1) // HEAD_DIM
+            for h in range(1, heads):
+                block = jnp.where(head == h, part(kind + h, start, local_width), block)
+            return block
+
+        both.append(
+            jnp.concatenate(
+                [
+                    -part(0, 0, features),
+                    part(0, starts[1], local_width),
+                    part(1, starts[2], local_width),
+                    per_head(2, starts[0]),
+                    per_head(2 + heads, starts[3]),
+                ],
+                axis=1,
+            )
+        )
+    first = core_ref[...] == 0
+    mine_ref[...] = jnp.where(first, both[0], both[1])
+    theirs_ref[...] = jnp.where(first, both[1], both[0])
+
+
+def total_kernel(mine_ref, other_ref, projector_ref, attn_ref, qkv_ref):
+    total = mine_ref[...] + other_ref[...]
+    features, local_width = projector_ref.shape[1], attn_ref.shape[1]
+    projector_ref[...] = total[:, :features]
+    attn_ref[...] = total[:, features : features + local_width]
+    for n in range(3):
+        start = features + (n + 1) * local_width
+        qkv_ref[n] = total[:, start : start + local_width]
 
 
 def call_kernel(kernel, out_shape, flops, *operands):
@@ -258,7 +360,6 @@
         select = sample_pos.shape[1]
         local_width = w_qkv.shape[2]
         half = rows * chips
-        first_core = lax.axis_index("wide") % CORES == 0
         heads_here = local_width // HEAD_DIM
         picks = images * select
 
@@ -282,34 +383,36 @@
             w_attn_out,
         )
 
-        own = teacher_in.astype(f32)
-        sums = jnp.concatenate(
-            [
-                jnp.sum(own, axis=1, keepdims=True),
-                jnp.sum(own * own, axis=1, keepdims=True),
-            ],
-            axis=1,
-        )
-        sums = jnp.sum(spread(sums, "narrow", narrow), axis=0)
-        center = sums[:, 0:1] / d_t
-        variance = sums[:, 1:2] / d_t - center * center
-        normed = (
-            (own - center) * lax.rsqrt(variance + EPSILON) * teacher_gain.astype(f32)
-        ).astype(bf16)
-        first = jnp.concatenate([normed, projector.T], axis=0)
-        first = spread(first, "wide", chips, groups)
+        piece = width // wide
+        first = call_kernel(
+            first_kernel,
+            jax.ShapeDtypeStruct((chips, rows + piece, features), bf16),
+            chips * (rows + piece) * features,
+            teacher_in,
+            projector.T,
+        )
+        first = exchange(first, "wide", groups)
         first, student = lax.optimization_barrier((first, student))
         norm, keys, values, probs, side, early, picked_norm, picked_in, mixed = student
-        normed = first[:, :rows].reshape(half, features)
-        normed_other = swap(normed)
+        raw = first[:, :rows].reshape(half, features)
+        raw_other = swap(raw)
 
         hidden_shape = jax.ShapeDtypeStruct((narrow, 2 * half // narrow, mlp_in.shape[1]), bf16)
         rows_shape = jax.ShapeDtypeStruct((half, features), bf16)
         up_flops = 4 * half * mlp_in.size
-        pre = call_kernel(up_kernel, hidden_shape, up_flops, normed, normed_other, mlp_in)
+        pre = call_kernel(
+            up_kernel,
+            jax.ShapeDtypeStruct((narrow, 2 * half // narrow + 16, mlp_in.shape[1]), bf16),
+            up_flops,
+            raw,
+            raw_other,
+            teacher_gain.reshape(1, features),
+            mlp_in,
+        )
         columns = doubled(first[:, rows:], 1).reshape(-1, features)
         pre = exchange(pre, "narrow")
-        hidden = exchange(call_kernel(gelu_kernel, hidden_shape, 8 * pre.size, pre), "narrow")
+        hidden = call_kernel(functools.partial(gelu_kernel, d_t), hidden_shape, 8 * pre.size, pre)
+        hidden = exchange(hidden, "narrow")
         hidden, columns = lax.optimization_barrier((hidden, columns))
         branch = swap(call_kernel(down_other_kernel, rows_shape, up_flops // 2, hidden, mlp_out))
         branch = call_kernel(
@@ -320,7 +423,7 @@
             target_kernel,
             [
                 jax.ShapeDtypeStruct((rows, features), bf16),
-                jax.ShapeDtypeStruct((narrow, picks, width), f32),
+                jax.ShapeDtypeStruct((narrow, picks, width), bf16),
             ],
             2 * rows * columns.size,
             branch,
@@ -330,7 +433,6 @@
         )
         terms = exchange(terms, "narrow")
 
-        piece = width // wide
         kinds = 2 + 2 * heads_here
         shared_width = features + 4 * local_width
         got = call_kernel(
@@ -351,37 +453,26 @@
             jnp.asarray(lane_moves(kinds, piece), bf16),
         )
         got = exchange(got.reshape(chips, rows, -1), "wide", groups).reshape(half, -1)
-        got_other = swap(got)
-
-        def rows_product(block):
-            ours = jnp.where(
-                first_core,
-                block[:, shared_width : shared_width + LANES],
-                block[:, shared_width + LANES :],
-            )
-            return product(ours, block[:, :shared_width], ((0,), (0,)))
-
-        full = rows_product(got) + rows_product(got_other)
-
-        def part(kind, start, size):
-            return full[kind * piece : (kind + 1) * piece, start : start + size]
-
-        at_query = features
-        at_context = at_query + local_width
-        at_d_query = at_context + local_width
-        at_d_context = at_d_query + local_width
-        grad_projector = -part(0, 0, features).T
-        grad_attn_out = part(0, at_context, local_width).T
-        grad_query = part(1, at_d_query, local_width)
-        grad_key = part(2, at_query, local_width)
-        grad_value = part(2 + heads_here, at_d_context, local_width)
-        for h in range(1, heads_here):
-            here = lax.broadcasted_iota(jnp.int32, grad_key.shape, 1) // HEAD_DIM == h
-            grad_key = jnp.where(here, part(2 + h, at_query, local_width), grad_key)
-            grad_value = jnp.where(
-                here, part(2 + heads_here + h, at_d_context, local_width), grad_value
-            )
-        return (jnp.stack([grad_query, grad_key, grad_value]), grad_attn_out, grad_projector)
+        totals_shape = jax.ShapeDtypeStruct((piece, shared_width), f32)
+        mine, theirs = call_kernel(
+            functools.partial(partial_kernel, piece, features, local_width),
+            [totals_shape, totals_shape],
+            4 * LANES * half * shared_width,
+            (lax.axis_index("wide") % CORES).reshape(1, 1),
+            got,
+        )
+        grad_projector, grad_attn_out, grad_qkv = call_kernel(
+            total_kernel,
+            [
+                jax.ShapeDtypeStruct((piece, features), f32),
+                jax.ShapeDtypeStruct((piece, local_width), f32),
+                jax.ShapeDtypeStruct((3, piece, local_width), f32),
+            ],
+            mine.size,
+            mine,
+            swap(theirs),
+        )
+        return (grad_qkv, grad_attn_out.T, grad_projector.T)
 
     return local
 

time: 172 us -> 162 us (0.942)
  blocking collectives: 56.5 us -> 30 us
  waiting for transfers between devices: 40.2 us -> 54.6 us
  other arithmetic: 6.6 us -> 1.64 us
  starting transfers between devices: 48.3 us -> 52.4 us
  Pallas kernels: 7.74 us -> 11.8 us
    all_to_all x3 -> x2, blocking collectives: 56.5 us -> 30 us  [exchange(): return lax.all_to_all(block, axis, 0, 0, axis_index_groups=groups)]
    all_to_all x4, waiting for transfers between devices: 35.9 us -> 51.1 us  [exchange(): return lax.all_to_all(block, axis, 0, 0, axis_index_groups=groups)]
    pallas_call x7 -> x10, Pallas kernels: 7.74 us -> 11.8 us  [call_kernel(): pl.pallas_call(kernel, out_shape=out_shape, in_specs=[whole] * len(operan...]
    all_to_all x4, starting transfers between devices: 28.6 us -> 31.7 us  [exchange(): return lax.all_to_all(block, axis, 0, 0, axis_index_groups=groups)]
    unnamed x46 -> x52, local copies, waits for them, and re-layouts: 4.52 us -> 5.9 us
  transfers between devices with their start and end apart: 8 -> 8, of which waited for: 7 -> 7; matrix products, arithmetic and copies ran while one was open for 2% -> 2% of each run, Pallas kernels for 2% -> 3%
where the time goes in v5:
time: 162 us; the launch traced here: 160 us
  waiting for transfers between devices  54.6 us (34%)
  starting transfers between devices  52.4 us (32%)
  blocking collectives  30 us (19%)
  Pallas kernels  11.8 us (7%)
  local copies, waits for them, and re-layouts  8.47 us (5%)
  other arithmetic  1.64 us (1%)
    all_to_all x4, waiting for transfers between devices, exchange(): return lax.all_to_all(block, axis, 0, 0, axis_index_groups=groups)  51.1 us
    all_to_all x4, starting transfers between devices, exchange(): return lax.all_to_all(block, axis, 0, 0, axis_index_groups=groups)  31.7 us
    all_to_all x2, blocking collectives, exchange(): return lax.all_to_all(block, axis, 0, 0, axis_index_groups=groups)  30 us
    ppermute x3, starting transfers between devices, swap(): return lax.ppermute(block, 'wide', pairs)  18.1 us
    pallas_call x10, Pallas kernels, call_kernel(): pl.pallas_call(kernel, out_shape=out_shape, in_specs=[whole] * len(operan...  11.8 us
    unnamed x52, local copies, waits for them, and re-layouts  5.9 us
    ppermute x3, waiting for transfers between devices, swap(): return lax.ppermute(block, 'wide', pairs)  3.53 us
  transfers between devices with their start and end apart: 8, of which 7 were waited for; matrix products, arithmetic and copies ran while one was open for 2% of the time, Pallas kernels for 3%

profile of v5, /device:TPU:1, one launch (start us, length us, event | category | flops | bytes accessed | tf_op | source)
XLA Modules:
  0.0 159.8 jit_solution(18423350849296241689)
XLA Ops:
  0.6 0.0 copy-start.12
  0.6 0.7 copy-done.12
  1.3 0.7 copy-done.20
  2.1 0.0 copy-start.21
  2.1 1.1 shard_map.139
  3.2 16.8 %all-to-all-start = ((bf16[32,24,768]{2,1,0:T(8,128)(2,1)}), bf16[32,24,768]{2,1,0:T(8,128)(2,1)}, u32[]{:S(2)}, u32[]{:S(2)}) async-start(bf16[32,24,768]{2,1,0:T(8,128)(2,1)} %shard_map.139), calls=%async_computation | async-start | bytes 2359296 | tf_op jit(solution)/shard_map/all_to_all | solution.py:29
  20.0 0.1 copy.17
  20.1 0.1 reshape.46.wanted_ref
  20.2 0.0 copy-done.5
  20.2 1.1 copy-done.6
  21.3 3.1 %shard_map.140 = (bf16[1024,1024]{1,0:T(8,128)(2,1)S(1)}, bf16[1024,128]{1,0:T(8,128)(2,1)S(1)}, bf16[1024,128]{1,0:T(8,128)(2,1)S(1)}, f32[16,1024]{1,0:T(8,128...) custom-call(s32[8,1]{1,0:T(8,128)S(1)} %reshape.46.wanted_ref, ...), custom_call_target="tpu_custom_call" | custom-call | flops 603979776 | bytes 3145824 | tf_op jit(solution)/shard_map/pallas_call | solution.py:311
  24.5 1.4 copy-done.2
  25.8 0.7 copy-done.10
  26.5 0.6 copy-done.14
  27.1 0.6 copy-done.16
  27.7 21.2 %all-to-all-done = bf16[32,24,768]{2,1,0:T(8,128)(2,1)} async-done(((bf16[32,24,768]{2,1,0:T(8,128)(2,1)}), bf16[32,24,768]{2,1,0:T(8,128)(2,1)}, u32[]{:S(2)}, u32[]{:S(2)}) %all-to-all-start) | async-done | bytes 1179680 | tf_op jit(solution)/shard_map/all_to_all | solution.py:29
  48.9 1.0 slice_bitcast_fusion.own_ref
  49.9 6.4 %collective-permute-start = (bf16[256,768]{1,0:T(8,128)(2,1)S(1)}, bf16[256,768]{1,0:T(8,128)(2,1)S(1)}, u32[]{:S(2)}, u32[]{:S(2)}) collective-permute-start(bf16[256,768]{1,0:T(8,128)(2,1)S(1)} %slice_bitcast_fusion.own_ref), channel_id=1, source_target_pairs={{0,8},{8,0},{16,24},{24,16},{32,40},{40,32},{48,56},{56,48},{64,72... | collective-permute-start | bytes 1179656 | tf_op jit(solution)/shard_map/ppermute | solution.py:337
  56.3 1.3 collective-permute-done.other_ref
  57.6 0.0 copy-done.7
  57.6 2.1 %shard_map.141 = bf16[8,80,384]{2,1,0:T(8,128)(2,1)} custom-call(bf16[256,768]{1,0:T(8,128)(2,1)S(1)} %slice_bitcast_fusion.own_ref, bf16[256,768]{1,0:T(8,128)(2,1)S(1)} %collective-permute-done.other_ref, bf16[1,768]{1,0:T(2,128)(2,1)S(1)} %reshape.40.gain_ref, bf16[768,384]{1,0:T(8,128)(2,1)S(1)} %copy-done.7), custom_call_target="tpu_custom_call" | custom-call | flops 301989888 | bytes 1377792 | tf_op jit(solution)/shard_map/pallas_call | solution.py:311
  59.7 4.9 %all-to-all-start.1 = ((bf16[8,80,384]{2,1,0:T(8,128)(2,1)}), bf16[8,80,384]{2,1,0:T(8,128)(2,1)S(1)}, u32[]{:S(2)}, u32[]{:S(2)}) async-start(bf16[8,80,384]{2,1,0:T(8,128)(2,1)} %shard_map.141), calls=%async_computation.1 | async-start | bytes 983040 | tf_op jit(solution)/shard_map/all_to_all | solution.py:29
  64.7 1.2 slice.7
  65.9 2.6 %collective-permute-start.1 = (bf16[32,16,768]{2,1,0:T(8,128)(2,1)S(1)}, bf16[32,16,768]{2,1,0:T(8,128)(2,1)}, u32[]{:S(2)}, u32[]{:S(2)}) collective-permute-start(bf16[32,16,768]{2,1,0:T(8,128)(2,1)S(1)} %slice.7), channel_id=1, source_target_pairs={{0,8},{8,0},{16,24},{24,16},{32,40},{40,32},{48,56},{56,48},{64,72... | collective-permute-start | bytes 2359304 | tf_op jit(solution)/shard_map/ppermute | solution.py:340
  68.4 5.3 %all-to-all-done.1.parts_ref = bf16[8,80,384]{2,1,0:T(8,128)(2,1)S(1)} async-done(((bf16[8,80,384]{2,1,0:T(8,128)(2,1)}), bf16[8,80,384]{2,1,0:T(8,128)(2,1)S(1)}, u32[]{:S(2)}, u32[]{:S(2)}) %all-to-all-start.1) | async-done | bytes 491552 | tf_op jit(solution)/shard_map/all_to_all | solution.py:29
  73.7 1.1 shard_map.142
  74.8 3.5 %all-to-all-start.2 = ((bf16[8,64,384]{2,1,0:T(8,128)(2,1)}), bf16[8,64,384]{2,1,0:T(8,128)(2,1)S(1)}, u32[]{:S(2)}, u32[]{:S(2)}) async-start(bf16[8,64,384]{2,1,0:T(8,128)(2,1)} %shard_map.142), calls=%async_computation.2 | async-start | bytes 786432 | tf_op jit(solution)/shard_map/all_to_all | solution.py:29
  78.3 0.1 broadcast_in_dim.34
  78.4 0.1 broadcast_in_dim.35
  78.5 0.0 collective-permute-done.1
  78.5 1.6 %bitcast_select_fusion.columns_ref = bf16[1024,768]{1,0:T(8,128)(2,1)S(1)} fusion(pred[1024]{0:T(1024)(128)(4,1)S(1)} %broadcast_in_dim.35, bf16[32,16,768]{2,1,0:T(8,128)(2,1)} %collective-permute-done.1, bf16[32,16,768]{2,1,0:T(8,128)(2,1)} %copy-done.22), kind=kLoop, calls=%fused_computation | loop fusion | flops 786432 | bytes 3146752 | tf_op jit(solution)/shard_map/jit(_where)/select_n | solution.py:343
  80.1 5.0 %all-to-all-done.2.hidden_ref = bf16[8,64,384]{2,1,0:T(8,128)(2,1)S(1)} async-done(((bf16[8,64,384]{2,1,0:T(8,128)(2,1)}), bf16[8,64,384]{2,1,0:T(8,128)(2,1)S(1)}, u32[]{:S(2)}, u32[]{:S(2)}) %all-to-all-start.2) | async-done | bytes 393248 | tf_op jit(solution)/shard_map/all_to_all | solution.py:29
  85.1 0.4 shard_map.143
  85.5 0.0 copy-start.13
  85.5 0.0 copy-start.19
  85.5 4.6 %collective-permute-start.2 = (bf16[256,768]{1,0:T(8,128)(2,1)S(1)}, bf16[256,768]{1,0:T(8,128)(2,1)S(1)}, u32[]{:S(2)}, u32[]{:S(2)}) collective-permute-start(bf16[256,768]{1,0:T(8,128)(2,1)S(1)} %shard_map.143), channel_id=1, source_target_pairs={{0,8},{8,0},{16,24},{24,16},{32,40},{40,32},{48,56},{56,48},{64,72... | collective-permute-start | bytes 1179656 | tf_op jit(solution)/shard_map/ppermute | solution.py:337
  90.2 1.3 collective-permute-done.2.add_ref
  91.5 0.4 shard_map.144
  91.9 21.9 %all_to_all.30.branch_ref = bf16[32,8,768]{2,1,0:T(8,128)(2,1)S(1)} all-to-all(bf16[32,8,768]{2,1,0:T(8,128)(2,1)S(1)} %bitcast.16), channel_id=1, replica_groups={{0,16,32,48,64,80,96,112,128,144,160,176,192,208,224,240,256,272,288,30..., dimensions={0} | all-to-all | bytes 786432 | tf_op jit(solution)/shard_map/all_to_all | solution.py:29
  113.8 0.5 shard_map.145
  114.3 8.1 %all_to_all.31.terms_ref = bf16[8,8,1024]{2,1,0:T(8,128)(2,1)S(1)} all-to-all(bf16[8,8,1024]{2,1,0:T(8,128)(2,1)S(1)} %get-tuple-element.44), channel_id=1, replica_groups=mesh['wide'=64,'narrow'=8] {'narrow'}, dimensions={0} | all-to-all | bytes 262144 | tf_op jit(solution)/shard_map/all_to_all | solution.py:29
  122.5 2.1 %shard_map.146 = bf16[256,1536]{1,0:T(8,128)(2,1)} custom-call(bf16[8,8,1024]{2,1,0:T(8,128)(2,1)S(1)} %all_to_all.31.terms_ref, f32[8,1024]{1,0:T(8,128)S(1)} %copy-done.17, f32[16,1024]{1,0:T(8,128)S(1)} %get-tuple-element.46.probs_ref, bf16[1024,128]{1,0:T(8,128)(2,1)S(1)} %copy-done.9, bf16[1024,128]{1,0:T(8,128)(2,1)S(1)} %copy-done.11, ...), custom_call_target="tpu_custom_call" | custom-call | flops 33554432 | bytes 4804608 | tf_op jit(solution)/shard_map/pallas_call | solution.py:311
  124.6 6.5 %all-to-all-start.5 = ((bf16[32,8,1536]{2,1,0:T(8,128)(2,1)}), bf16[32,8,1536]{2,1,0:T(8,128)(2,1)S(1)}, u32[]{:S(2)}, u32[]{:S(2)}) async-start(bf16[32,8,1536]{2,1,0:T(8,128)(2,1)} %bitcast.7), calls=%async_computation.5 | async-start | bytes 1572864 | tf_op jit(solution)/shard_map/all_to_all | solution.py:29
  131.2 19.6 %all-to-all-done.5 = bf16[32,8,1536]{2,1,0:T(8,128)(2,1)S(1)} async-done(((bf16[32,8,1536]{2,1,0:T(8,128)(2,1)}), bf16[32,8,1536]{2,1,0:T(8,128)(2,1)S(1)}, u32[]{:S(2)}, u32[]{:S(2)}) %all-to-all-start.5) | async-done | bytes 786464 | tf_op jit(solution)/shard_map/all_to_all | solution.py:29
  150.8 0.4 shard_map.147
  151.1 7.1 %collective-permute-start.3 = (f32[16,1280]{1,0:T(8,128)S(1)}, f32[16,1280]{1,0:T(8,128)S(1)}, u32[]{:S(2)}, u32[]{:S(2)}) collective-permute-start(f32[16,1280]{1,0:T(8,128)S(1)} %get-tuple-element.55), channel_id=1, source_target_pairs={{0,8},{8,0},{16,24},{24,16},{32,40},{40,32},{48,56},{56,48},{64,72... | collective-permute-start | bytes 245768 | tf_op jit(solution)/shard_map/ppermute | solution.py:337
  158.3 0.9 collective-permute-done.3.other_ref
  159.2 0.6 shard_map.148
  (42 shorter events, 0.1 us)
Async XLA Ops:
  0.6 0.7 copy-start.12
  1.3 0.7 copy-start.20
  2.1 17.9 %copy-start.24 = (s32[4,2]{0,1:T(2,128)S(1)}, s32[4,2]{0,1:T(2,128)}, u32[]{:S(2)}) copy-start(s32[4,2]{0,1:T(2,128)} %param.18) | copy-start | bytes 100
  2.1 17.9 %copy-start.25 = (s32[4,2]{0,1:T(2,128)S(1)}, s32[4,2]{0,1:T(2,128)}, u32[]{:S(2)}) copy-start(s32[4,2]{0,1:T(2,128)} %constant.34) | copy-start | bytes 100
  2.1 18.1 %copy-start.1 = (bf16[4,256,1024]{2,1,0:T(8,128)(2,1)S(1)}, bf16[4,256,1024]{2,1,0:T(8,128)(2,1)}, u32[]{:S(2)}) copy-start(bf16[4,256,1024]{2,1,0:T(8,128)(2,1)} %param.17) | copy-start | bytes 6291460
  2.1 18.1 %copy-start.5 = (bf16[128,1024]{1,0:T(8,128)(2,1)S(1)}, bf16[128,1024]{1,0:T(8,128)(2,1)}, u32[]{:S(2)}) copy-start(bf16[128,1024]{1,0:T(8,128)(2,1)} %w_out_ref.3) | copy-start | bytes 786436
  2.1 18.1 %copy-start.21 = (s32[16,1]{1,0:T(8,128)S(1)}, s32[16,1]{1,0:T(8,128)}, u32[]{:S(2)}) copy-start(s32[16,1]{1,0:T(8,128)} %constant.28.clone.first_ref) | copy-start | bytes 196
  3.2 45.7 %all-to-all-start = ((bf16[32,24,768]{2,1,0:T(8,128)(2,1)}), bf16[32,24,768]{2,1,0:T(8,128)(2,1)}, u32[]{:S(2)}, u32[]{:S(2)}) async-start(bf16[32,24,768]{2,1,0:T(8,128)(2,1)} %shard_map.139), calls=%async_computation | async-start | bytes 2359296 | tf_op jit(solution)/shard_map/all_to_all | solution.py:29
  20.2 1.1 copy-start.6
  21.3 35.0 %copy-start.23 = (bf16[768]{0:T(1024)(128)(2,1)S(1)}, bf16[768]{0:T(1024)(128)(2,1)}, u32[]{:S(2)}) copy-start(bf16[768]{0:T(1024)(128)(2,1)} %param.13) | copy-start | bytes 4612
  21.3 36.3 %copy-start.7 = (bf16[768,384]{1,0:T(8,128)(2,1)S(1)}, bf16[768,384]{1,0:T(8,128)(2,1)}, u32[]{:S(2)}) copy-start(bf16[768,384]{1,0:T(8,128)(2,1)} %weight_ref.3) | copy-start | bytes 1769476
  24.5 1.4 copy-start.2
  25.8 0.7 copy-start.10
  26.5 0.6 copy-start.14
  27.1 0.6 copy-start.16
  27.7 32.0 %copy-start.8 = (bf16[1024,128]{1,0:T(8,128)(2,1)}, bf16[1024,128]{1,0:T(8,128)(2,1)S(1)}, u32[]{:S(2)}) copy-start(bf16[1024,128]{1,0:T(8,128)(2,1)S(1)} %get-tuple-element.47.keys_ref) | copy-start | bytes 786436
  27.7 32.0 %copy-start.18 = (f32[8,1024]{1,0:T(8,128)}, f32[8,1024]{1,0:T(8,128)S(1)}, u32[]{:S(2)}) copy-start(f32[8,1024]{1,0:T(8,128)S(1)} %get-tuple-element.43.mixed_ref) | copy-start | bytes 98308
  49.9 7.7 %collective-permute-start = (bf16[256,768]{1,0:T(8,128)(2,1)S(1)}, bf16[256,768]{1,0:T(8,128)(2,1)S(1)}, u32[]{:S(2)}, u32[]{:S(2)}) collective-permute-start(bf16[256,768]{1,0:T(8,128)(2,1)S(1)} %slice_bitcast_fusion.own_ref), channel_id=1, source_target_pairs={{0,8},{8,0},{16,24},{24,16},{32,40},{40,32},{48,56},{56,48},{64,72... | collective-permute-start | bytes 1179656 | tf_op jit(solution)/shard_map/ppermute | solution.py:337
  59.7 14.0 %all-to-all-start.1 = ((bf16[8,80,384]{2,1,0:T(8,128)(2,1)}), bf16[8,80,384]{2,1,0:T(8,128)(2,1)S(1)}, u32[]{:S(2)}, u32[]{:S(2)}) async-start(bf16[8,80,384]{2,1,0:T(8,128)(2,1)} %shard_map.141), calls=%async_computation.1 | async-start | bytes 983040 | tf_op jit(solution)/shard_map/all_to_all | solution.py:29
  65.9 12.6 %copy-start.22 = (bf16[32,16,768]{2,1,0:T(8,128)(2,1)}, bf16[32,16,768]{2,1,0:T(8,128)(2,1)S(1)}, u32[]{:S(2)}) copy-start(bf16[32,16,768]{2,1,0:T(8,128)(2,1)S(1)} %slice.7) | copy-start | bytes 2359300
  65.9 12.6 %collective-permute-start.1 = (bf16[32,16,768]{2,1,0:T(8,128)(2,1)S(1)}, bf16[32,16,768]{2,1,0:T(8,128)(2,1)}, u32[]{:S(2)}, u32[]{:S(2)}) collective-permute-start(bf16[32,16,768]{2,1,0:T(8,128)(2,1)S(1)} %slice.7), channel_id=1, source_target_pairs={{0,8},{8,0},{16,24},{24,16},{32,40},{40,32},{48,56},{56,48},{64,72... | collective-permute-start | bytes 2359304 | tf_op jit(solution)/shard_map/ppermute | solution.py:340
  74.8 10.3 %all-to-all-start.2 = ((bf16[8,64,384]{2,1,0:T(8,128)(2,1)}), bf16[8,64,384]{2,1,0:T(8,128)(2,1)S(1)}, u32[]{:S(2)}, u32[]{:S(2)}) async-start(bf16[8,64,384]{2,1,0:T(8,128)(2,1)} %shard_map.142), calls=%async_computation.2 | async-start | bytes 786432 | tf_op jit(solution)/shard_map/all_to_all | solution.py:29
  78.5 6.6 %copy-start = (bf16[384,768]{1,0:T(8,128)(2,1)S(1)}, bf16[384,768]{1,0:T(8,128)(2,1)}, u32[]{:S(2)}) copy-start(bf16[384,768]{1,0:T(8,128)(2,1)} %weight_ref.5) | copy-start | bytes 1769476
  85.5 28.3 %copy-start.13 = (bf16[8,768]{1,0:T(8,128)(2,1)S(1)}, bf16[8,768]{1,0:T(8,128)(2,1)}, u32[]{:S(2)}) copy-start(bf16[8,768]{1,0:T(8,128)(2,1)} %teacher_ref.1) | copy-start | bytes 36868
  85.5 28.3 %copy-start.19 = (f32[8,1024]{1,0:T(8,128)S(1)}, f32[8,1024]{1,0:T(8,128)}, u32[]{:S(2)}) copy-start(f32[8,1024]{1,0:T(8,128)} %copy-done.18) | copy-start | bytes 98308
  85.5 6.0 %collective-permute-start.2 = (bf16[256,768]{1,0:T(8,128)(2,1)S(1)}, bf16[256,768]{1,0:T(8,128)(2,1)S(1)}, u32[]{:S(2)}, u32[]{:S(2)}) collective-permute-start(bf16[256,768]{1,0:T(8,128)(2,1)S(1)} %shard_map.143), channel_id=1, source_target_pairs={{0,8},{8,0},{16,24},{24,16},{32,40},{40,32},{48,56},{56,48},{64,72... | collective-permute-start | bytes 1179656 | tf_op jit(solution)/shard_map/ppermute | solution.py:337
  91.5 30.9 %copy-start.4 = (bf16[768,1024]{1,0:T(8,128)(2,1)S(1)}, bf16[768,1024]{1,0:T(8,128)(2,1)}, u32[]{:S(2)}) copy-start(bf16[768,1024]{1,0:T(8,128)(2,1)} %constant.29.clone.move_ref) | copy-start | bytes 4718596
  91.9 30.6 %copy-start.3 = (bf16[1024,1024]{1,0:T(8,128)(2,1)S(1)}, bf16[1024,1024]{1,0:T(8,128)(2,1)}, u32[]{:S(2)}) copy-start(bf16[1024,1024]{1,0:T(8,128)(2,1)} %copy-done.2) | copy-start | bytes 6291460
  91.9 30.6 %copy-start.9 = (bf16[1024,128]{1,0:T(8,128)(2,1)S(1)}, bf16[1024,128]{1,0:T(8,128)(2,1)}, u32[]{:S(2)}) copy-start(bf16[1024,128]{1,0:T(8,128)(2,1)} %copy-done.8) | copy-start | bytes 786436
  91.9 30.6 %copy-start.11 = (bf16[1024,128]{1,0:T(8,128)(2,1)S(1)}, bf16[1024,128]{1,0:T(8,128)(2,1)}, u32[]{:S(2)}) copy-start(bf16[1024,128]{1,0:T(8,128)(2,1)} %copy-done.10) | copy-start | bytes 786436
  91.9 30.6 %copy-start.15 = (f32[8,1024]{1,0:T(8,128)S(1)}, f32[8,1024]{1,0:T(8,128)}, u32[]{:S(2)}) copy-start(f32[8,1024]{1,0:T(8,128)} %copy-done.14) | copy-start | bytes 98308
  91.9 30.6 %copy-start.17 = (f32[8,1024]{1,0:T(8,128)S(1)}, f32[8,1024]{1,0:T(8,128)}, u32[]{:S(2)}) copy-start(f32[8,1024]{1,0:T(8,128)} %copy-done.16) | copy-start | bytes 98308
  124.6 26.2 %all-to-all-start.5 = ((bf16[32,8,1536]{2,1,0:T(8,128)(2,1)}), bf16[32,8,1536]{2,1,0:T(8,128)(2,1)S(1)}, u32[]{:S(2)}, u32[]{:S(2)}) async-start(bf16[32,8,1536]{2,1,0:T(8,128)(2,1)} %bitcast.7), calls=%async_computation.5 | async-start | bytes 1572864 | tf_op jit(solution)/shard_map/all_to_all | solution.py:29
  151.1 8.0 %collective-permute-start.3 = (f32[16,1280]{1,0:T(8,128)S(1)}, f32[16,1280]{1,0:T(8,128)S(1)}, u32[]{:S(2)}, u32[]{:S(2)}) collective-permute-start(f32[16,1280]{1,0:T(8,128)S(1)} %get-tuple-element.55), channel_id=1, source_target_pairs={{0,8},{8,0},{16,24},{24,16},{32,40},{40,32},{48,56},{56,48},{64,72... | collective-permute-start | bytes 245768 | tf_op jit(solution)/shard_map/ppermute | solution.py:337

commit v6 on v5

--- a/solution.py
+++ b/solution.py
@@ -186,13 +186,10 @@
     gain = gain_ref[...].astype(f32)
     center = jnp.mean(rows, axis=1, keepdims=True)
     pre = product(((rows - center) * gain).astype(bf16), weight_ref[...]).astype(bf16)
-    squares = rows * rows
-    square_high = squares.astype(bf16)
-    square_low = (squares - square_high.astype(f32)).astype(bf16)
-    ones = jnp.ones((8, features), bf16)
-    flat = ((1,), (1,))
-    means = product(ones, low, flat)[0:1] / features
-    totals = (product(ones, square_high, flat) + product(ones, square_low, flat))[0:1]
+    total = jnp.sum(rows * rows, axis=1, keepdims=True)
+    lane = lax.broadcasted_iota(jnp.int32, (rows.shape[0], LANES), 1)
+    lines = jnp.where(lane == 0, center, jnp.where(lane == 1, total, 0.0)).T
+    means, totals = lines[0:1], lines[1:2]
     stats = jnp.concatenate(thirds(means) + thirds(totals), axis=0)
     gains = product(jnp.broadcast_to(gain, (8, features)).astype(bf16), weight_ref[...])[0:1]
     gains = jnp.concatenate(thirds(gains), axis=0)
@@ -392,7 +389,8 @@
             projector.T,
         )
         first = exchange(first, "wide", groups)
-        first, student = lax.optimization_barrier((first, student))
+        core = (lax.axis_index("wide") % CORES).reshape(1, 1)
+        first, student, core = lax.optimization_barrier((first, student, core))
         norm, keys, values, probs, side, early, picked_norm, picked_in, mixed = student
         raw = first[:, :rows].reshape(half, features)
         raw_other = swap(raw)
@@ -458,7 +456,7 @@
             functools.partial(partial_kernel, piece, features, local_width),
             [totals_shape, totals_shape],
             4 * LANES * half * shared_width,
-            (lax.axis_index("wide") % CORES).reshape(1, 1),
+            core,
             got,
         )
         grad_projector, grad_attn_out, grad_qkv = call_kernel(

time: 162 us -> 160 us (0.988)
  blocking collectives: 30 us -> 56 us
  waiting for transfers between devices: 54.6 us -> 35 us
  starting transfers between devices: 52.4 us -> 45.8 us
    all_to_all x2 -> x3, blocking collectives: 30 us -> 56 us  [exchange(): return lax.all_to_all(block, axis, 0, 0, axis_index_groups=groups)]
    all_to_all x4 -> x3, waiting for transfers between devices: 51.1 us -> 31.5 us  [exchange(): return lax.all_to_all(block, axis, 0, 0, axis_index_groups=groups)]
    all_to_all x4 -> x3, starting transfers between devices: 31.7 us -> 25.1 us  [exchange(): return lax.all_to_all(block, axis, 0, 0, axis_index_groups=groups)]
  transfers between devices with their start and end apart: 8 -> 7, of which waited for: 7 -> 6; matrix products, arithmetic and copies ran while one was open for 2% -> 2% of each run, Pallas kernels for 3% -> 3%
where the time goes in v6:
time: 160 us; the launch traced here: 158 us
  blocking collectives  56 us (35%)
  starting transfers between devices  45.8 us (29%)
  waiting for transfers between devices  35 us (22%)
  Pallas kernels  10.3 us (6%)
  local copies, waits for them, and re-layouts  8.49 us (5%)
  other arithmetic  1.64 us (1%)
    all_to_all x3, blocking collectives, exchange(): return lax.all_to_all(block, axis, 0, 0, axis_index_groups=groups)  56 us
    all_to_all x3, waiting for transfers between devices, exchange(): return lax.all_to_all(block, axis, 0, 0, axis_index_groups=groups)  31.5 us
    all_to_all x3, starting transfers between devices, exchange(): return lax.all_to_all(block, axis, 0, 0, axis_index_groups=groups)  25.1 us
    ppermute x3, starting transfers between devices, swap(): return lax.ppermute(block, 'wide', pairs)  18.1 us
    pallas_call x10, Pallas kernels, call_kernel(): pl.pallas_call(kernel, out_shape=out_shape, in_specs=[whole] * len(operan...  10.3 us
    unnamed x52, local copies, waits for them, and re-layouts  5.93 us
    ppermute x3, waiting for transfers between devices, swap(): return lax.ppermute(block, 'wide', pairs)  3.53 us
  transfers between devices with their start and end apart: 7, of which 6 were waited for; matrix products, arithmetic and copies ran while one was open for 2% of the time, Pallas kernels for 3%

profile of v6, /device:TPU:1, one launch (start us, length us, event | category | flops | bytes accessed | tf_op | source)
XLA Modules:
  0.0 158.2 jit_solution(10083116869996898884)
XLA Ops:
  0.6 0.0 copy-start.12
  0.6 0.7 copy-done.12
  1.3 0.7 copy-done.20
  2.1 0.0 copy-start.21
  2.1 1.1 shard_map.139
  3.2 16.8 %all-to-all-start = ((bf16[32,24,768]{2,1,0:T(8,128)(2,1)}), bf16[32,24,768]{2,1,0:T(8,128)(2,1)}, u32[]{:S(2)}, u32[]{:S(2)}) async-start(bf16[32,24,768]{2,1,0:T(8,128)(2,1)} %shard_map.139), calls=%async_computation | async-start | bytes 2359296 | tf_op jit(solution)/shard_map/all_to_all | solution.py:29
  20.0 0.1 copy.17
  20.1 0.1 reshape.46.wanted_ref
  20.2 1.1 copy-done.6
  21.3 3.1 %shard_map.140 = (bf16[1024,1024]{1,0:T(8,128)(2,1)S(1)}, bf16[1024,128]{1,0:T(8,128)(2,1)S(1)}, bf16[1024,128]{1,0:T(8,128)(2,1)S(1)}, f32[16,1024]{1,0:T(8,128...) custom-call(s32[8,1]{1,0:T(8,128)S(1)} %reshape.46.wanted_ref, ...), custom_call_target="tpu_custom_call" | custom-call | flops 603979776 | bytes 3145824 | tf_op jit(solution)/shard_map/pallas_call | solution.py:308
  24.4 1.4 copy-done.2
  25.8 0.7 copy-done.10
  26.5 0.6 copy-done.14
  27.1 0.6 copy-done.16
  27.7 21.2 %all-to-all-done = bf16[32,24,768]{2,1,0:T(8,128)(2,1)} async-done(((bf16[32,24,768]{2,1,0:T(8,128)(2,1)}), bf16[32,24,768]{2,1,0:T(8,128)(2,1)}, u32[]{:S(2)}, u32[]{:S(2)}) %all-to-all-start) | async-done | bytes 1179680 | tf_op jit(solution)/shard_map/all_to_all | solution.py:29
  48.9 1.0 slice_bitcast_fusion.own_ref
  49.9 6.4 %collective-permute-start = (bf16[256,768]{1,0:T(8,128)(2,1)S(1)}, bf16[256,768]{1,0:T(8,128)(2,1)S(1)}, u32[]{:S(2)}, u32[]{:S(2)}) collective-permute-start(bf16[256,768]{1,0:T(8,128)(2,1)S(1)} %slice_bitcast_fusion.own_ref), channel_id=1, source_target_pairs={{0,8},{8,0},{16,24},{24,16},{32,40},{40,32},{48,56},{56,48},{64,72... | collective-permute-start | bytes 1179656 | tf_op jit(solution)/shard_map/ppermute | solution.py:334
  56.3 1.3 collective-permute-done.other_ref
  57.6 1.6 %shard_map.141 = bf16[8,80,384]{2,1,0:T(8,128)(2,1)} custom-call(bf16[256,768]{1,0:T(8,128)(2,1)S(1)} %slice_bitcast_fusion.own_ref, bf16[256,768]{1,0:T(8,128)(2,1)S(1)} %collective-permute-done.other_ref, bf16[1,768]{1,0:T(2,128)(2,1)S(1)} %reshape.40.gain_ref, bf16[768,384]{1,0:T(8,128)(2,1)S(1)} %copy-done.7), custom_call_target="tpu_custom_call" | custom-call | flops 301989888 | bytes 1377792 | tf_op jit(solution)/shard_map/pallas_call | solution.py:308
  59.2 4.9 %all-to-all-start.1 = ((bf16[8,80,384]{2,1,0:T(8,128)(2,1)}), bf16[8,80,384]{2,1,0:T(8,128)(2,1)S(1)}, u32[]{:S(2)}, u32[]{:S(2)}) async-start(bf16[8,80,384]{2,1,0:T(8,128)(2,1)} %shard_map.141), calls=%async_computation.1 | async-start | bytes 983040 | tf_op jit(solution)/shard_map/all_to_all | solution.py:29
  64.2 1.2 slice.7
  65.4 2.6 %collective-permute-start.1 = (bf16[32,16,768]{2,1,0:T(8,128)(2,1)S(1)}, bf16[32,16,768]{2,1,0:T(8,128)(2,1)}, u32[]{:S(2)}, u32[]{:S(2)}) collective-permute-start(bf16[32,16,768]{2,1,0:T(8,128)(2,1)S(1)} %slice.7), channel_id=1, source_target_pairs={{0,8},{8,0},{16,24},{24,16},{32,40},{40,32},{48,56},{56,48},{64,72... | collective-permute-start | bytes 2359304 | tf_op jit(solution)/shard_map/ppermute | solution.py:337
  67.9 5.3 %all-to-all-done.1.parts_ref = bf16[8,80,384]{2,1,0:T(8,128)(2,1)S(1)} async-done(((bf16[8,80,384]{2,1,0:T(8,128)(2,1)}), bf16[8,80,384]{2,1,0:T(8,128)(2,1)S(1)}, u32[]{:S(2)}, u32[]{:S(2)}) %all-to-all-start.1) | async-done | bytes 491552 | tf_op jit(solution)/shard_map/all_to_all | solution.py:29
  73.2 1.1 shard_map.142
  74.3 3.5 %all-to-all-start.2 = ((bf16[8,64,384]{2,1,0:T(8,128)(2,1)}), bf16[8,64,384]{2,1,0:T(8,128)(2,1)S(1)}, u32[]{:S(2)}, u32[]{:S(2)}) async-start(bf16[8,64,384]{2,1,0:T(8,128)(2,1)} %shard_map.142), calls=%async_computation.2 | async-start | bytes 786432 | tf_op jit(solution)/shard_map/all_to_all | solution.py:29
  77.8 0.1 broadcast_in_dim.34
  77.9 0.1 broadcast_in_dim.35
  78.0 0.0 collective-permute-done.1
  78.0 1.6 %bitcast_select_fusion.columns_ref = bf16[1024,768]{1,0:T(8,128)(2,1)S(1)} fusion(pred[1024]{0:T(1024)(128)(4,1)S(1)} %broadcast_in_dim.35, bf16[32,16,768]{2,1,0:T(8,128)(2,1)} %collective-permute-done.1, bf16[32,16,768]{2,1,0:T(8,128)(2,1)} %copy-done.22), kind=kLoop, calls=%fused_computation | loop fusion | flops 786432 | bytes 3146752 | tf_op jit(solution)/shard_map/jit(_where)/select_n | solution.py:340
  79.6 5.0 %all-to-all-done.2.hidden_ref = bf16[8,64,384]{2,1,0:T(8,128)(2,1)S(1)} async-done(((bf16[8,64,384]{2,1,0:T(8,128)(2,1)}), bf16[8,64,384]{2,1,0:T(8,128)(2,1)S(1)}, u32[]{:S(2)}, u32[]{:S(2)}) %all-to-all-start.2) | async-done | bytes 393248 | tf_op jit(solution)/shard_map/all_to_all | solution.py:29
  84.6 0.0 copy-done
  84.6 0.4 shard_map.143
  85.0 0.0 copy-start.13
  85.0 0.0 copy-start.19
  85.0 4.7 %collective-permute-start.2 = (bf16[256,768]{1,0:T(8,128)(2,1)S(1)}, bf16[256,768]{1,0:T(8,128)(2,1)S(1)}, u32[]{:S(2)}, u32[]{:S(2)}) collective-permute-start(bf16[256,768]{1,0:T(8,128)(2,1)S(1)} %shard_map.143), channel_id=1, source_target_pairs={{0,8},{8,0},{16,24},{24,16},{32,40},{40,32},{48,56},{56,48},{64,72... | collective-permute-start | bytes 1179656 | tf_op jit(solution)/shard_map/ppermute | solution.py:334
  89.7 1.3 collective-permute-done.2.add_ref
  91.0 0.4 shard_map.144
  91.4 21.9 %all_to_all.30.branch_ref = bf16[32,8,768]{2,1,0:T(8,128)(2,1)S(1)} all-to-all(bf16[32,8,768]{2,1,0:T(8,128)(2,1)S(1)} %bitcast.17), channel_id=1, replica_groups={{0,16,32,48,64,80,96,112,128,144,160,176,192,208,224,240,256,272,288,30..., dimensions={0} | all-to-all | bytes 786432 | tf_op jit(solution)/shard_map/all_to_all | solution.py:29
  113.3 0.0 copy-done.13
  113.3 0.5 shard_map.145
  113.8 8.1 %all_to_all.31.terms_ref = bf16[8,8,1024]{2,1,0:T(8,128)(2,1)S(1)} all-to-all(bf16[8,8,1024]{2,1,0:T(8,128)(2,1)S(1)} %get-tuple-element.46), channel_id=1, replica_groups=mesh['wide'=64,'narrow'=8] {'narrow'}, dimensions={0} | all-to-all | bytes 262144 | tf_op jit(solution)/shard_map/all_to_all | solution.py:29
  121.9 0.0 copy-done.3
  122.0 1.2 shard_map.146
  123.2 26.0 %all_to_all.32 = bf16[32,8,1536]{2,1,0:T(8,128)(2,1)S(1)} all-to-all(bf16[32,8,1536]{2,1,0:T(8,128)(2,1)S(1)} %bitcast.14), channel_id=1, replica_groups={{0,16,32,48,64,80,96,112,128,144,160,176,192,208,224,240,256,272,288,30..., dimensions={0} | all-to-all | bytes 1572864 | tf_op jit(solution)/shard_map/all_to_all | solution.py:29
  149.2 0.4 shard_map.147
  149.5 7.1 %collective-permute-start.3 = (f32[16,1280]{1,0:T(8,128)S(1)}, f32[16,1280]{1,0:T(8,128)S(1)}, u32[]{:S(2)}, u32[]{:S(2)}) collective-permute-start(f32[16,1280]{1,0:T(8,128)S(1)} %get-tuple-element.57), channel_id=1, source_target_pairs={{0,8},{8,0},{16,24},{24,16},{32,40},{40,32},{48,56},{56,48},{64,72... | collective-permute-start | bytes 245768 | tf_op jit(solution)/shard_map/ppermute | solution.py:334
  156.7 0.9 collective-permute-done.3.other_ref
  157.6 0.6 shard_map.148
  (41 shorter events, 0.1 us)
Async XLA Ops:
  0.6 0.7 copy-start.12
  1.3 0.7 copy-start.20
  2.1 17.9 %copy-start.24 = (s32[4,2]{0,1:T(2,128)S(1)}, s32[4,2]{0,1:T(2,128)}, u32[]{:S(2)}) copy-start(s32[4,2]{0,1:T(2,128)} %param.18) | copy-start | bytes 100
  2.1 17.9 %copy-start.25 = (s32[4,2]{0,1:T(2,128)S(1)}, s32[4,2]{0,1:T(2,128)}, u32[]{:S(2)}) copy-start(s32[4,2]{0,1:T(2,128)} %constant.34) | copy-start | bytes 100
  2.1 18.1 %copy-start.1 = (bf16[4,256,1024]{2,1,0:T(8,128)(2,1)S(1)}, bf16[4,256,1024]{2,1,0:T(8,128)(2,1)}, u32[]{:S(2)}) copy-start(bf16[4,256,1024]{2,1,0:T(8,128)(2,1)} %param.17) | copy-start | bytes 6291460
  2.1 18.1 %copy-start.5 = (bf16[128,1024]{1,0:T(8,128)(2,1)S(1)}, bf16[128,1024]{1,0:T(8,128)(2,1)}, u32[]{:S(2)}) copy-start(bf16[128,1024]{1,0:T(8,128)(2,1)} %w_out_ref.3) | copy-start | bytes 786436
  2.1 18.1 %copy-start.21 = (s32[16,1]{1,0:T(8,128)S(1)}, s32[16,1]{1,0:T(8,128)}, u32[]{:S(2)}) copy-start(s32[16,1]{1,0:T(8,128)} %constant.28.clone.first_ref) | copy-start | bytes 196
  3.2 45.7 %all-to-all-start = ((bf16[32,24,768]{2,1,0:T(8,128)(2,1)}), bf16[32,24,768]{2,1,0:T(8,128)(2,1)}, u32[]{:S(2)}, u32[]{:S(2)}) async-start(bf16[32,24,768]{2,1,0:T(8,128)(2,1)} %shard_map.139), calls=%async_computation | async-start | bytes 2359296 | tf_op jit(solution)/shard_map/all_to_all | solution.py:29
  20.2 1.1 copy-start.6
  21.3 35.0 %copy-start.23 = (bf16[768]{0:T(1024)(128)(2,1)S(1)}, bf16[768]{0:T(1024)(128)(2,1)}, u32[]{:S(2)}) copy-start(bf16[768]{0:T(1024)(128)(2,1)} %param.13) | copy-start | bytes 4612
  21.3 36.3 %copy-start.7 = (bf16[768,384]{1,0:T(8,128)(2,1)S(1)}, bf16[768,384]{1,0:T(8,128)(2,1)}, u32[]{:S(2)}) copy-start(bf16[768,384]{1,0:T(8,128)(2,1)} %weight_ref.3) | copy-start | bytes 1769476
  24.4 1.4 copy-start.2
  25.8 0.7 copy-start.10
  26.5 0.6 copy-start.14
  27.1 0.6 copy-start.16
  27.7 31.5 %copy-start.8 = (bf16[1024,128]{1,0:T(8,128)(2,1)}, bf16[1024,128]{1,0:T(8,128)(2,1)S(1)}, u32[]{:S(2)}) copy-start(bf16[1024,128]{1,0:T(8,128)(2,1)S(1)} %get-tuple-element.49.keys_ref) | copy-start | bytes 786436
  27.7 31.5 %copy-start.18 = (f32[8,1024]{1,0:T(8,128)}, f32[8,1024]{1,0:T(8,128)S(1)}, u32[]{:S(2)}) copy-start(f32[8,1024]{1,0:T(8,128)S(1)} %get-tuple-element.45.mixed_ref) | copy-start | bytes 98308
  49.9 7.7 %collective-permute-start = (bf16[256,768]{1,0:T(8,128)(2,1)S(1)}, bf16[256,768]{1,0:T(8,128)(2,1)S(1)}, u32[]{:S(2)}, u32[]{:S(2)}) collective-permute-start(bf16[256,768]{1,0:T(8,128)(2,1)S(1)} %slice_bitcast_fusion.own_ref), channel_id=1, source_target_pairs={{0,8},{8,0},{16,24},{24,16},{32,40},{40,32},{48,56},{56,48},{64,72... | collective-permute-start | bytes 1179656 | tf_op jit(solution)/shard_map/ppermute | solution.py:334
  59.2 14.0 %all-to-all-start.1 = ((bf16[8,80,384]{2,1,0:T(8,128)(2,1)}), bf16[8,80,384]{2,1,0:T(8,128)(2,1)S(1)}, u32[]{:S(2)}, u32[]{:S(2)}) async-start(bf16[8,80,384]{2,1,0:T(8,128)(2,1)} %shard_map.141), calls=%async_computation.1 | async-start | bytes 983040 | tf_op jit(solution)/shard_map/all_to_all | solution.py:29
  65.4 12.6 %copy-start.22 = (bf16[32,16,768]{2,1,0:T(8,128)(2,1)}, bf16[32,16,768]{2,1,0:T(8,128)(2,1)S(1)}, u32[]{:S(2)}) copy-start(bf16[32,16,768]{2,1,0:T(8,128)(2,1)S(1)} %slice.7) | copy-start | bytes 2359300
  65.4 12.6 %collective-permute-start.1 = (bf16[32,16,768]{2,1,0:T(8,128)(2,1)S(1)}, bf16[32,16,768]{2,1,0:T(8,128)(2,1)}, u32[]{:S(2)}, u32[]{:S(2)}) collective-permute-start(bf16[32,16,768]{2,1,0:T(8,128)(2,1)S(1)} %slice.7), channel_id=1, source_target_pairs={{0,8},{8,0},{16,24},{24,16},{32,40},{40,32},{48,56},{56,48},{64,72... | collective-permute-start | bytes 2359304 | tf_op jit(solution)/shard_map/ppermute | solution.py:337
  74.3 10.3 %all-to-all-start.2 = ((bf16[8,64,384]{2,1,0:T(8,128)(2,1)}), bf16[8,64,384]{2,1,0:T(8,128)(2,1)S(1)}, u32[]{:S(2)}, u32[]{:S(2)}) async-start(bf16[8,64,384]{2,1,0:T(8,128)(2,1)} %shard_map.142), calls=%async_computation.2 | async-start | bytes 786432 | tf_op jit(solution)/shard_map/all_to_all | solution.py:29
  78.0 6.6 %copy-start = (bf16[384,768]{1,0:T(8,128)(2,1)S(1)}, bf16[384,768]{1,0:T(8,128)(2,1)}, u32[]{:S(2)}) copy-start(bf16[384,768]{1,0:T(8,128)(2,1)} %weight_ref.5) | copy-start | bytes 1769476
  85.0 28.4 %copy-start.13 = (bf16[8,768]{1,0:T(8,128)(2,1)S(1)}, bf16[8,768]{1,0:T(8,128)(2,1)}, u32[]{:S(2)}) copy-start(bf16[8,768]{1,0:T(8,128)(2,1)} %teacher_ref.1) | copy-start | bytes 36868
  85.0 28.3 %copy-start.19 = (f32[8,1024]{1,0:T(8,128)S(1)}, f32[8,1024]{1,0:T(8,128)}, u32[]{:S(2)}) copy-start(f32[8,1024]{1,0:T(8,128)} %copy-done.18) | copy-start | bytes 98308
  85.0 6.0 %collective-permute-start.2 = (bf16[256,768]{1,0:T(8,128)(2,1)S(1)}, bf16[256,768]{1,0:T(8,128)(2,1)S(1)}, u32[]{:S(2)}, u32[]{:S(2)}) collective-permute-start(bf16[256,768]{1,0:T(8,128)(2,1)S(1)} %shard_map.143), channel_id=1, source_target_pairs={{0,8},{8,0},{16,24},{24,16},{32,40},{40,32},{48,56},{56,48},{64,72... | collective-permute-start | bytes 1179656 | tf_op jit(solution)/shard_map/ppermute | solution.py:334
  91.0 30.9 %copy-start.4 = (bf16[768,1024]{1,0:T(8,128)(2,1)S(1)}, bf16[768,1024]{1,0:T(8,128)(2,1)}, u32[]{:S(2)}) copy-start(bf16[768,1024]{1,0:T(8,128)(2,1)} %constant.29.clone.move_ref) | copy-start | bytes 4718596
  91.4 30.6 %copy-start.3 = (bf16[1024,1024]{1,0:T(8,128)(2,1)S(1)}, bf16[1024,1024]{1,0:T(8,128)(2,1)}, u32[]{:S(2)}) copy-start(bf16[1024,1024]{1,0:T(8,128)(2,1)} %copy-done.2) | copy-start | bytes 6291460
  91.4 30.6 %copy-start.9 = (bf16[1024,128]{1,0:T(8,128)(2,1)S(1)}, bf16[1024,128]{1,0:T(8,128)(2,1)}, u32[]{:S(2)}) copy-start(bf16[1024,128]{1,0:T(8,128)(2,1)} %copy-done.8) | copy-start | bytes 786436
  91.4 30.6 %copy-start.11 = (bf16[1024,128]{1,0:T(8,128)(2,1)S(1)}, bf16[1024,128]{1,0:T(8,128)(2,1)}, u32[]{:S(2)}) copy-start(bf16[1024,128]{1,0:T(8,128)(2,1)} %copy-done.10) | copy-start | bytes 786436
  91.4 30.6 %copy-start.15 = (f32[8,1024]{1,0:T(8,128)S(1)}, f32[8,1024]{1,0:T(8,128)}, u32[]{:S(2)}) copy-start(f32[8,1024]{1,0:T(8,128)} %copy-done.14) | copy-start | bytes 98308
  91.4 30.6 %copy-start.17 = (f32[8,1024]{1,0:T(8,128)S(1)}, f32[8,1024]{1,0:T(8,128)}, u32[]{:S(2)}) copy-start(f32[8,1024]{1,0:T(8,128)} %copy-done.16) | copy-start | bytes 98308
  149.5 8.0 %collective-permute-start.3 = (f32[16,1280]{1,0:T(8,128)S(1)}, f32[16,1280]{1,0:T(8,128)S(1)}, u32[]{:S(2)}, u32[]{:S(2)}) collective-permute-start(f32[16,1280]{1,0:T(8,128)S(1)} %get-tuple-element.57), channel_id=1, source_target_pairs={{0,8},{8,0},{16,24},{24,16},{32,40},{40,32},{48,56},{56,48},{64,72... | collective-permute-start | bytes 245768 | tf_op jit(solution)/shard_map/ppermute | solution.py:334

commit v7 on v6

--- a/solution.py
+++ b/solution.py
@@ -174,36 +174,48 @@
         send_ref[n] = block
 
 
-def up_kernel(own_ref, other_ref, gain_ref, weight_ref, send_ref):
-    parts, _, hidden = send_ref.shape
-    size = own_ref.shape[0] // parts
-    features = own_ref.shape[1]
-    pieces = []
-    for n in range(parts):
-        pieces += [own_ref[pl.ds(n * size, size), :], other_ref[pl.ds(n * size, size), :]]
-    low = jnp.concatenate(pieces, axis=0)
-    rows = low.astype(f32)
-    gain = gain_ref[...].astype(f32)
+def up_half(rows_ref, gain, weight_ref):
+    rows = rows_ref[...].astype(f32)
     center = jnp.mean(rows, axis=1, keepdims=True)
     pre = product(((rows - center) * gain).astype(bf16), weight_ref[...]).astype(bf16)
     total = jnp.sum(rows * rows, axis=1, keepdims=True)
     lane = lax.broadcasted_iota(jnp.int32, (rows.shape[0], LANES), 1)
     lines = jnp.where(lane == 0, center, jnp.where(lane == 1, total, 0.0)).T
-    means, totals = lines[0:1], lines[1:2]
-    stats = jnp.concatenate(thirds(means) + thirds(totals), axis=0)
-    gains = product(jnp.broadcast_to(gain, (8, features)).astype(bf16), weight_ref[...])[0:1]
-    gains = jnp.concatenate(thirds(gains), axis=0)
-    span = 2 * size
+    return pre, lines[:8]
+
+
+def up_own_kernel(rows_ref, gain_ref, weight_ref, pre_ref, lines_ref, gains_ref):
+    gain = gain_ref[...].astype(f32)
+    pre, lines = up_half(rows_ref, gain, weight_ref)
+    pre_ref[...] = pre
+    lines_ref[...] = lines
+    gain = jnp.broadcast_to(gain, (8, gain.shape[1])).astype(bf16)
+    gains_ref[...] = product(gain, weight_ref[...])
+
+
+def up_kernel(rows_ref, gain_ref, weight_ref, own_ref, own_lines_ref, gains_ref, send_ref):
+    parts, _, hidden = send_ref.shape
+    size = own_ref.shape[0] // parts
+    pre, lines = up_half(rows_ref, gain_ref[...].astype(f32), weight_ref)
+    gains = jnp.concatenate(thirds(gains_ref[0:1, :]), axis=0)
+    stats = []
+    for held in (own_lines_ref[...], lines):
+        stats.append(jnp.concatenate(thirds(held[0:1]) + thirds(held[1:2]), axis=0))
     for n in range(parts):
-        send_ref[n, pl.ds(0, span), :] = pre[n * span : (n + 1) * span]
-        tile = n * span // LANES * LANES
-        mine = stats[:, tile : tile + LANES]
-        if n * span % LANES:
-            mine = pltpu.roll(mine, LANES - n * span % LANES, 1)
-        lines = [mine] + [jnp.zeros_like(mine)] * (hidden // LANES - 1)
-        extra = jnp.concatenate([gains, jnp.concatenate(lines, axis=1)], axis=0)
+        send_ref[n, pl.ds(0, size), :] = own_ref[pl.ds(n * size, size), :]
+        send_ref[n, pl.ds(size, size), :] = pre[n * size : (n + 1) * size]
+        tile, shift = n * size // LANES * LANES, n * size % LANES
+        own, other = [block[:, tile : tile + LANES] for block in stats]
+        if shift:
+            own = pltpu.roll(own, LANES - shift, 1)
+        if shift != size:
+            other = pltpu.roll(other, (LANES + size - shift) % LANES, 1)
+        lane = lax.broadcasted_iota(jnp.int32, own.shape, 1)
+        mine = jnp.where(lane < size, own, other)
+        line = [mine] + [jnp.zeros_like(mine)] * (hidden // LANES - 1)
+        extra = jnp.concatenate([gains, jnp.concatenate(line, axis=1)], axis=0)
         extra = jnp.concatenate([extra, jnp.zeros((16 - extra.shape[0], hidden), f32)], axis=0)
-        send_ref[n, pl.ds(span, 16), :] = extra.astype(bf16)
+        send_ref[n, pl.ds(2 * size, 16), :] = extra.astype(bf16)
 
 
 def gelu_kernel(d_t, parts_ref, send_ref):
@@ -398,14 +410,27 @@
         hidden_shape = jax.ShapeDtypeStruct((narrow, 2 * half // narrow, mlp_in.shape[1]), bf16)
         rows_shape = jax.ShapeDtypeStruct((half, features), bf16)
         up_flops = 4 * half * mlp_in.size
+        gain = teacher_gain.reshape(1, features)
+        up_own = call_kernel(
+            up_own_kernel,
+            [
+                jax.ShapeDtypeStruct((half, mlp_in.shape[1]), bf16),
+                jax.ShapeDtypeStruct((8, half), f32),
+                jax.ShapeDtypeStruct((8, mlp_in.shape[1]), f32),
+            ],
+            up_flops // 2,
+            raw,
+            gain,
+            mlp_in,
+        )
         pre = call_kernel(
             up_kernel,
             jax.ShapeDtypeStruct((narrow, 2 * half // narrow + 16, mlp_in.shape[1]), bf16),
-            up_flops,
-            raw,
+            up_flops // 2,
             raw_other,
-            teacher_gain.reshape(1, features),
+            gain,
             mlp_in,
+            *up_own,
         )
         columns = doubled(first[:, rows:], 1).reshape(-1, features)
         pre = exchange(pre, "narrow")

time: 160 us -> 160 us (level)
  waiting for transfers between devices: 35 us -> 33.2 us
    unnamed x52 -> x48, local copies, waits for them, and re-layouts: 5.93 us -> 7.17 us
    pallas_call x10 -> x11, Pallas kernels: 10.3 us -> 10.6 us  [call_kernel(): pl.pallas_call(kernel, out_shape=out_shape, in_specs=[whole] * len(operan...]
where the time goes in v7:
time: 160 us; the launch traced here: 158 us
  blocking collectives  55.8 us (35%)
  starting transfers between devices  45.8 us (29%)
  waiting for transfers between devices  33.2 us (21%)
  Pallas kernels  10.6 us (7%)
  local copies, waits for them, and re-layouts  9.74 us (6%)
  other arithmetic  1.64 us (1%)
    all_to_all x3, blocking collectives, exchange(): return lax.all_to_all(block, axis, 0, 0, axis_index_groups=groups)  55.8 us
    all_to_all x3, waiting for transfers between devices, exchange(): return lax.all_to_all(block, axis, 0, 0, axis_index_groups=groups)  30.2 us
    all_to_all x3, starting transfers between devices, exchange(): return lax.all_to_all(block, axis, 0, 0, axis_index_groups=groups)  25.1 us
    ppermute x3, starting transfers between devices, swap(): return lax.ppermute(block, 'wide', pairs)  18.1 us
    pallas_call x11, Pallas kernels, call_kernel(): pl.pallas_call(kernel, out_shape=out_shape, in_specs=[whole] * len(operan...  10.6 us
    unnamed x48, local copies, waits for them, and re-layouts  7.17 us
  transfers between devices with their start and end apart: 7, of which 6 were waited for; matrix products, arithmetic and copies ran while one was open for 2% of the time, Pallas kernels for 3%

profile of v7, /device:TPU:1, one launch (start us, length us, event | category | flops | bytes accessed | tf_op | source)
XLA Modules:
  0.0 157.7 jit_solution(507672582857000384)
XLA Ops:
  0.6 0.0 copy-start.10
  0.6 0.7 copy-done.10
  1.3 0.7 copy-done.18
  2.1 1.1 shard_map.139
  3.2 16.8 %all-to-all-start = ((bf16[32,24,768]{2,1,0:T(8,128)(2,1)}), bf16[32,24,768]{2,1,0:T(8,128)(2,1)}, u32[]{:S(2)}, u32[]{:S(2)}) async-start(bf16[32,24,768]{2,1,0:T(8,128)(2,1)} %shard_map.139), calls=%async_computation | async-start | bytes 2359296 | tf_op jit(solution)/shard_map/all_to_all | solution.py:29
  20.0 0.0 copy-done.22
  20.0 0.1 copy.17
  20.1 0.1 reshape.46.wanted_ref
  20.2 1.1 copy-done.7
  21.3 0.7 copy-done.19
  22.0 3.1 %shard_map.140 = (bf16[1024,1024]{1,0:T(8,128)(2,1)S(1)}, bf16[1024,128]{1,0:T(8,128)(2,1)S(1)}, bf16[1024,128]{1,0:T(8,128)(2,1)S(1)}, f32[16,1024]{1,0:T(8,128...) custom-call(s32[8,1]{1,0:T(8,128)S(1)} %reshape.46.wanted_ref, ...), custom_call_target="tpu_custom_call" | custom-call | flops 603979776 | bytes 3145824 | tf_op jit(solution)/shard_map/pallas_call | solution.py:320
  25.1 1.4 copy-done.3
  26.5 0.6 copy-done.8
  27.1 0.6 copy-done.12
  27.8 0.6 copy-done.14
  28.4 0.6 copy-done.16
  29.0 19.9 %all-to-all-done = bf16[32,24,768]{2,1,0:T(8,128)(2,1)} async-done(((bf16[32,24,768]{2,1,0:T(8,128)(2,1)}), bf16[32,24,768]{2,1,0:T(8,128)(2,1)}, u32[]{:S(2)}, u32[]{:S(2)}) %all-to-all-start) | async-done | bytes 1179680 | tf_op jit(solution)/shard_map/all_to_all | solution.py:29
  48.9 1.0 slice_bitcast_fusion.rows_ref
  49.9 6.4 %collective-permute-start = (bf16[256,768]{1,0:T(8,128)(2,1)S(1)}, bf16[256,768]{1,0:T(8,128)(2,1)S(1)}, u32[]{:S(2)}, u32[]{:S(2)}) collective-permute-start(bf16[256,768]{1,0:T(8,128)(2,1)S(1)} %slice_bitcast_fusion.rows_ref), channel_id=1, source_target_pairs={{0,8},{8,0},{16,24},{24,16},{32,40},{40,32},{48,56},{56,48},{64,72... | collective-permute-start | bytes 1179656 | tf_op jit(solution)/shard_map/ppermute | solution.py:346
  56.3 0.5 shard_map.141
  56.9 0.8 collective-permute-done.rows_ref
  57.6 1.3 shard_map.142
  58.9 4.9 %all-to-all-start.1 = ((bf16[8,80,384]{2,1,0:T(8,128)(2,1)}), bf16[8,80,384]{2,1,0:T(8,128)(2,1)S(1)}, u32[]{:S(2)}, u32[]{:S(2)}) async-start(bf16[8,80,384]{2,1,0:T(8,128)(2,1)} %shard_map.142), calls=%async_computation.1 | async-start | bytes 983040 | tf_op jit(solution)/shard_map/all_to_all | solution.py:29
  63.8 1.2 slice.7
  65.0 2.6 %collective-permute-start.1 = (bf16[32,16,768]{2,1,0:T(8,128)(2,1)S(1)}, bf16[32,16,768]{2,1,0:T(8,128)(2,1)}, u32[]{:S(2)}, u32[]{:S(2)}) collective-permute-start(bf16[32,16,768]{2,1,0:T(8,128)(2,1)S(1)} %slice.7), channel_id=1, source_target_pairs={{0,8},{8,0},{16,24},{24,16},{32,40},{40,32},{48,56},{56,48},{64,72... | collective-permute-start | bytes 2359304 | tf_op jit(solution)/shard_map/ppermute | solution.py:349
  67.6 5.3 %all-to-all-done.1.parts_ref = bf16[8,80,384]{2,1,0:T(8,128)(2,1)S(1)} async-done(((bf16[8,80,384]{2,1,0:T(8,128)(2,1)}), bf16[8,80,384]{2,1,0:T(8,128)(2,1)S(1)}, u32[]{:S(2)}, u32[]{:S(2)}) %all-to-all-start.1) | async-done | bytes 491552 | tf_op jit(solution)/shard_map/all_to_all | solution.py:29
  72.9 1.1 shard_map.143
  74.0 3.5 %all-to-all-start.2 = ((bf16[8,64,384]{2,1,0:T(8,128)(2,1)}), bf16[8,64,384]{2,1,0:T(8,128)(2,1)S(1)}, u32[]{:S(2)}, u32[]{:S(2)}) async-start(bf16[8,64,384]{2,1,0:T(8,128)(2,1)} %shard_map.143), calls=%async_computation.2 | async-start | bytes 786432 | tf_op jit(solution)/shard_map/all_to_all | solution.py:29
  77.4 0.1 broadcast_in_dim.34
  77.5 0.1 broadcast_in_dim.35
  77.6 0.0 collective-permute-done.1
  77.6 1.6 %bitcast_select_fusion.columns_ref = bf16[1024,768]{1,0:T(8,128)(2,1)S(1)} fusion(pred[1024]{0:T(1024)(128)(4,1)S(1)} %broadcast_in_dim.35, bf16[32,16,768]{2,1,0:T(8,128)(2,1)} %collective-permute-done.1, bf16[32,16,768]{2,1,0:T(8,128)(2,1)} %copy-done.20), kind=kLoop, calls=%fused_computation | loop fusion | flops 786432 | bytes 3146752 | tf_op jit(solution)/shard_map/jit(_where)/select_n | solution.py:352
  79.3 5.0 %all-to-all-done.2.hidden_ref = bf16[8,64,384]{2,1,0:T(8,128)(2,1)S(1)} async-done(((bf16[8,64,384]{2,1,0:T(8,128)(2,1)}), bf16[8,64,384]{2,1,0:T(8,128)(2,1)S(1)}, u32[]{:S(2)}, u32[]{:S(2)}) %all-to-all-start.2) | async-done | bytes 393248 | tf_op jit(solution)/shard_map/all_to_all | solution.py:29
  84.3 0.4 shard_map.144
  84.6 0.0 copy-start.11
  84.6 0.0 copy-start.17
  84.6 4.7 %collective-permute-start.2 = (bf16[256,768]{1,0:T(8,128)(2,1)S(1)}, bf16[256,768]{1,0:T(8,128)(2,1)S(1)}, u32[]{:S(2)}, u32[]{:S(2)}) collective-permute-start(bf16[256,768]{1,0:T(8,128)(2,1)S(1)} %shard_map.144), channel_id=1, source_target_pairs={{0,8},{8,0},{16,24},{24,16},{32,40},{40,32},{48,56},{56,48},{64,72... | collective-permute-start | bytes 1179656 | tf_op jit(solution)/shard_map/ppermute | solution.py:346
  89.3 1.3 collective-permute-done.2.add_ref
  90.6 0.4 shard_map.145
  91.0 21.8 %all_to_all.30.branch_ref = bf16[32,8,768]{2,1,0:T(8,128)(2,1)S(1)} all-to-all(bf16[32,8,768]{2,1,0:T(8,128)(2,1)S(1)} %bitcast.17), channel_id=1, replica_groups={{0,16,32,48,64,80,96,112,128,144,160,176,192,208,224,240,256,272,288,30..., dimensions={0} | all-to-all | bytes 786432 | tf_op jit(solution)/shard_map/all_to_all | solution.py:29
  112.8 0.5 shard_map.146
  113.3 8.1 %all_to_all.31.terms_ref = bf16[8,8,1024]{2,1,0:T(8,128)(2,1)S(1)} all-to-all(bf16[8,8,1024]{2,1,0:T(8,128)(2,1)S(1)} %get-tuple-element.52), channel_id=1, replica_groups=mesh['wide'=64,'narrow'=8] {'narrow'}, dimensions={0} | all-to-all | bytes 262144 | tf_op jit(solution)/shard_map/all_to_all | solution.py:29
  121.5 1.2 shard_map.147
  122.7 26.0 %all_to_all.32 = bf16[32,8,1536]{2,1,0:T(8,128)(2,1)S(1)} all-to-all(bf16[32,8,1536]{2,1,0:T(8,128)(2,1)S(1)} %bitcast.14), channel_id=1, replica_groups={{0,16,32,48,64,80,96,112,128,144,160,176,192,208,224,240,256,272,288,30..., dimensions={0} | all-to-all | bytes 1572864 | tf_op jit(solution)/shard_map/all_to_all | solution.py:29
  148.7 0.4 shard_map.148
  149.0 7.1 %collective-permute-start.3 = (f32[16,1280]{1,0:T(8,128)S(1)}, f32[16,1280]{1,0:T(8,128)S(1)}, u32[]{:S(2)}, u32[]{:S(2)}) collective-permute-start(f32[16,1280]{1,0:T(8,128)S(1)} %get-tuple-element.63), channel_id=1, source_target_pairs={{0,8},{8,0},{16,24},{24,16},{32,40},{40,32},{48,56},{56,48},{64,72... | collective-permute-start | bytes 245768 | tf_op jit(solution)/shard_map/ppermute | solution.py:346
  156.2 0.9 collective-permute-done.3.other_ref
  157.1 0.6 shard_map.149
  (38 shorter events, 0.1 us)
Async XLA Ops:
  0.6 0.7 copy-start.10
  1.3 0.7 copy-start.18
  2.1 17.9 %copy-start.22 = (s32[4,2]{0,1:T(2,128)S(1)}, s32[4,2]{0,1:T(2,128)}, u32[]{:S(2)}) copy-start(s32[4,2]{0,1:T(2,128)} %param.18) | copy-start | bytes 100
  2.1 17.9 %copy-start.23 = (s32[4,2]{0,1:T(2,128)S(1)}, s32[4,2]{0,1:T(2,128)}, u32[]{:S(2)}) copy-start(s32[4,2]{0,1:T(2,128)} %constant.34) | copy-start | bytes 100
  2.1 18.1 %copy-start.2 = (bf16[4,256,1024]{2,1,0:T(8,128)(2,1)S(1)}, bf16[4,256,1024]{2,1,0:T(8,128)(2,1)}, u32[]{:S(2)}) copy-start(bf16[4,256,1024]{2,1,0:T(8,128)(2,1)} %param.17) | copy-start | bytes 6291460
  2.1 18.1 %copy-start.6 = (bf16[128,1024]{1,0:T(8,128)(2,1)S(1)}, bf16[128,1024]{1,0:T(8,128)(2,1)}, u32[]{:S(2)}) copy-start(bf16[128,1024]{1,0:T(8,128)(2,1)} %w_out_ref.3) | copy-start | bytes 786436
  3.2 45.7 %all-to-all-start = ((bf16[32,24,768]{2,1,0:T(8,128)(2,1)}), bf16[32,24,768]{2,1,0:T(8,128)(2,1)}, u32[]{:S(2)}, u32[]{:S(2)}) async-start(bf16[32,24,768]{2,1,0:T(8,128)(2,1)} %shard_map.139), calls=%async_computation | async-start | bytes 2359296 | tf_op jit(solution)/shard_map/all_to_all | solution.py:29
  20.2 1.1 copy-start.7
  21.3 0.7 copy-start.19
  22.0 34.3 %copy-start.21 = (bf16[768]{0:T(1024)(128)(2,1)S(1)}, bf16[768]{0:T(1024)(128)(2,1)}, u32[]{:S(2)}) copy-start(bf16[768]{0:T(1024)(128)(2,1)} %param.13) | copy-start | bytes 4612
  22.0 34.3 %copy-start = (bf16[768,384]{1,0:T(8,128)(2,1)S(1)}, bf16[768,384]{1,0:T(8,128)(2,1)}, u32[]{:S(2)}) copy-start(bf16[768,384]{1,0:T(8,128)(2,1)} %weight_ref.5) | copy-start | bytes 1769476
  25.1 1.4 copy-start.3
  26.5 0.6 copy-start.8
  27.1 0.6 copy-start.12
  27.8 0.6 copy-start.14
  28.4 0.6 copy-start.16
  49.9 7.7 %collective-permute-start = (bf16[256,768]{1,0:T(8,128)(2,1)S(1)}, bf16[256,768]{1,0:T(8,128)(2,1)S(1)}, u32[]{:S(2)}, u32[]{:S(2)}) collective-permute-start(bf16[256,768]{1,0:T(8,128)(2,1)S(1)} %slice_bitcast_fusion.rows_ref), channel_id=1, source_target_pairs={{0,8},{8,0},{16,24},{24,16},{32,40},{40,32},{48,56},{56,48},{64,72... | collective-permute-start | bytes 1179656 | tf_op jit(solution)/shard_map/ppermute | solution.py:346
  58.9 14.0 %all-to-all-start.1 = ((bf16[8,80,384]{2,1,0:T(8,128)(2,1)}), bf16[8,80,384]{2,1,0:T(8,128)(2,1)S(1)}, u32[]{:S(2)}, u32[]{:S(2)}) async-start(bf16[8,80,384]{2,1,0:T(8,128)(2,1)} %shard_map.142), calls=%async_computation.1 | async-start | bytes 983040 | tf_op jit(solution)/shard_map/all_to_all | solution.py:29
  65.0 12.6 %copy-start.20 = (bf16[32,16,768]{2,1,0:T(8,128)(2,1)}, bf16[32,16,768]{2,1,0:T(8,128)(2,1)S(1)}, u32[]{:S(2)}) copy-start(bf16[32,16,768]{2,1,0:T(8,128)(2,1)S(1)} %slice.7) | copy-start | bytes 2359300
  65.0 12.6 %collective-permute-start.1 = (bf16[32,16,768]{2,1,0:T(8,128)(2,1)S(1)}, bf16[32,16,768]{2,1,0:T(8,128)(2,1)}, u32[]{:S(2)}, u32[]{:S(2)}) collective-permute-start(bf16[32,16,768]{2,1,0:T(8,128)(2,1)S(1)} %slice.7), channel_id=1, source_target_pairs={{0,8},{8,0},{16,24},{24,16},{32,40},{40,32},{48,56},{56,48},{64,72... | collective-permute-start | bytes 2359304 | tf_op jit(solution)/shard_map/ppermute | solution.py:349
  74.0 10.3 %all-to-all-start.2 = ((bf16[8,64,384]{2,1,0:T(8,128)(2,1)}), bf16[8,64,384]{2,1,0:T(8,128)(2,1)S(1)}, u32[]{:S(2)}, u32[]{:S(2)}) async-start(bf16[8,64,384]{2,1,0:T(8,128)(2,1)} %shard_map.143), calls=%async_computation.2 | async-start | bytes 786432 | tf_op jit(solution)/shard_map/all_to_all | solution.py:29
  77.6 6.6 %copy-start.1 = (bf16[384,768]{1,0:T(8,128)(2,1)S(1)}, bf16[384,768]{1,0:T(8,128)(2,1)}, u32[]{:S(2)}) copy-start(bf16[384,768]{1,0:T(8,128)(2,1)} %weight_ref.7) | copy-start | bytes 1769476
  84.6 28.2 %copy-start.11 = (bf16[8,768]{1,0:T(8,128)(2,1)S(1)}, bf16[8,768]{1,0:T(8,128)(2,1)}, u32[]{:S(2)}) copy-start(bf16[8,768]{1,0:T(8,128)(2,1)} %teacher_ref.1) | copy-start | bytes 36868
  84.6 28.2 %copy-start.17 = (f32[8,1024]{1,0:T(8,128)S(1)}, f32[8,1024]{1,0:T(8,128)}, u32[]{:S(2)}) copy-start(f32[8,1024]{1,0:T(8,128)} %copy-done.16) | copy-start | bytes 98308
  84.6 6.0 %collective-permute-start.2 = (bf16[256,768]{1,0:T(8,128)(2,1)S(1)}, bf16[256,768]{1,0:T(8,128)(2,1)S(1)}, u32[]{:S(2)}, u32[]{:S(2)}) collective-permute-start(bf16[256,768]{1,0:T(8,128)(2,1)S(1)} %shard_map.144), channel_id=1, source_target_pairs={{0,8},{8,0},{16,24},{24,16},{32,40},{40,32},{48,56},{56,48},{64,72... | collective-permute-start | bytes 1179656 | tf_op jit(solution)/shard_map/ppermute | solution.py:346
  90.6 30.8 %copy-start.5 = (bf16[768,1024]{1,0:T(8,128)(2,1)S(1)}, bf16[768,1024]{1,0:T(8,128)(2,1)}, u32[]{:S(2)}) copy-start(bf16[768,1024]{1,0:T(8,128)(2,1)} %constant.29.clone.move_ref) | copy-start | bytes 4718596
  91.0 30.4 %copy-start.4 = (bf16[1024,1024]{1,0:T(8,128)(2,1)S(1)}, bf16[1024,1024]{1,0:T(8,128)(2,1)}, u32[]{:S(2)}) copy-start(bf16[1024,1024]{1,0:T(8,128)(2,1)} %copy-done.3) | copy-start | bytes 6291460
  91.0 30.4 %copy-start.9 = (f32[16,1024]{1,0:T(8,128)S(1)}, f32[16,1024]{1,0:T(8,128)}, u32[]{:S(2)}) copy-start(f32[16,1024]{1,0:T(8,128)} %copy-done.8) | copy-start | bytes 196612
  91.0 30.4 %copy-start.13 = (f32[8,1024]{1,0:T(8,128)S(1)}, f32[8,1024]{1,0:T(8,128)}, u32[]{:S(2)}) copy-start(f32[8,1024]{1,0:T(8,128)} %copy-done.12) | copy-start | bytes 98308
  91.0 30.4 %copy-start.15 = (f32[8,1024]{1,0:T(8,128)S(1)}, f32[8,1024]{1,0:T(8,128)}, u32[]{:S(2)}) copy-start(f32[8,1024]{1,0:T(8,128)} %copy-done.14) | copy-start | bytes 98308
  149.0 8.0 %collective-permute-start.3 = (f32[16,1280]{1,0:T(8,128)S(1)}, f32[16,1280]{1,0:T(8,128)S(1)}, u32[]{:S(2)}, u32[]{:S(2)}) collective-permute-start(f32[16,1280]{1,0:T(8,128)S(1)} %get-tuple-element.63), channel_id=1, source_target_pairs={{0,8},{8,0},{16,24},{24,16},{32,40},{40,32},{48,56},{56,48},{64,72... | collective-permute-start | bytes 245768 | tf_op jit(solution)/shard_map/ppermute | solution.py:346
